TPU v7x, 32 devices: a whole 2x2x4 slice. The times are simulated.
32 devices in a mesh: dp: 8 (over z, x), blk: 2 (over y), head: 2 (over core).
Axes of the slice: x: 2, y: 2, z: 4, core: 2. Of those that a mesh axis runs over, the one named last changes fastest.
Arguments:
- tokens: bfloat16 [32, 512, 1024], P('dp', ('blk', 'head')), may hold values from -6 to 6
- doc_lengths: int32 [32, 32], P('dp'), may hold values from 0 to 448, as said below
- qkv_weight: bfloat16 [1024, 3072], P(('dp', 'blk', 'head')), may hold values from -0.1875 to 0.1875
- out_weight: bfloat16 [1024, 1024], P(('dp', 'blk', 'head')), may hold values from -0.75 to 0.75
- up_weight: bfloat16 [1024, 4096], P(('dp', 'blk', 'head')), may hold values from -0.1875 to 0.1875
- down_weight: bfloat16 [4096, 1024], P(('dp', 'blk', 'head')), may hold values from -0.09375 to 0.09375
- norm_params: bfloat16 [1024, 4], P(('dp', 'blk', 'head')), may hold values from -0.5 to 1.5, as said below
- out_cotangent: bfloat16 [32, 512, 1024], P('dp', ('blk', 'head')), may hold values from -6 to 6
Outputs:
- layer_out: bfloat16 [32, 512, 1024], P('dp', ('blk', 'head'))
- input_grad: float32 [32, 512, 1024], P('dp', ('blk', 'head'))
- qkv_grad: float32 [1024, 3072], P(('dp', 'blk', 'head'))
- proj_grad: float32 [1024, 1024], P(('dp', 'blk', 'head'))
- up_grad: float32 [1024, 4096], P(('dp', 'blk', 'head'))
- down_grad: float32 [4096, 1024], P(('dp', 'blk', 'head'))
- norm_grad: float32 [1024, 4], P(('dp', 'blk', 'head'))
Inputs may be any that keep to these rules, and one draw needn't show every extreme that they name: `doc_lengths`: each sequence's lengths sum to at most 512; positions past the sum are padding; a length may be zero. One sequence of each 4 consecutive ones holds a document of 448 tokens that starts at one of positions 0 to 64. `norm_params`: columns 0 and 2 are gains, columns 1 and 3 shifts.
All inputs are finite; a program needn't handle non-finite values.
Results may differ from a plain program's by a relative error of at most 0.015.
Values may be sent and summed in bfloat16 or wider, within the bound.
No kernel may reach another device: no remote copies, remote signals or barrier semaphores. Data moves between devices by JAX's collectives and lax.ppermute only.
A program may use at most 192 MiB of HBM per device.

v0:
```python
import jax
import jax.numpy as jnp
from jax import lax
from jax.sharding import PartitionSpec as P

HEAD_DIM = 64


epsilon = 1e-12


def segments_of(doc_lengths, length):
    doc_ends = jnp.cumsum(doc_lengths, axis=-1, dtype=jnp.int32)
    places = jnp.arange(length, dtype=jnp.int32)
    passed = jnp.sum(
        (doc_ends[..., None, :] <= places[:, None]).astype(jnp.int32), axis=-1, dtype=jnp.int32
    )
    return jnp.where(places < doc_ends[..., -1:], passed + 1, 0)


def layer_norm(hidden, gain, shift):
    average = jnp.mean(hidden, axis=-1, keepdims=True)
    centred = hidden - average
    spread = jnp.mean(centred * centred, axis=-1, keepdims=True)
    return centred * lax.rsqrt(spread + epsilon) * gain + shift


def gelu_exact(values_in):
    return jax.nn.gelu(values_in, approximate=False)


def masked_scores(query_block, key_block, seg_query, seg_key, score_scale):
    query_heads = query_block.reshape(query_block.shape[0], -1, HEAD_DIM)
    key_heads = key_block.reshape(key_block.shape[0], -1, HEAD_DIM)
    raw_scores = (
        jnp.einsum("qhd,khd->hqk", query_heads, key_heads, preferred_element_type=jnp.float32)
        * score_scale
    )
    allowed = seg_query[:, None] == seg_key[None, :]
    return jnp.where(allowed[None], raw_scores, -1e30)


def body(
    tokens, doc_lengths, qkv_weight, out_weight, up_weight, down_weight, norm_params, out_cotangent
):
    seqs_here, local_len, width = tokens.shape
    head_groups = lax.axis_size("head")
    half_len = local_len * head_groups
    full_len = half_len * lax.axis_size("blk")
    group_width = width // head_groups
    score_scale = HEAD_DIM ** (-0.5)
    part_qkv, part_out, part_up, part_down, part_norm = (
        lax.all_gather(qkv_weight, ("blk", "head"), axis=0, tiled=True),
        lax.all_gather(out_weight, ("blk", "head"), axis=0, tiled=True),
        lax.all_gather(up_weight, ("blk", "head"), axis=0, tiled=True),
        lax.all_gather(down_weight, ("blk", "head"), axis=0, tiled=True),
        lax.all_gather(norm_params, ("blk", "head"), axis=0, tiled=True),
    )
    wqkv, wout, wup, wdown, wnorm = (
        lax.all_gather(part_qkv, "dp", axis=0, tiled=True),
        lax.all_gather(part_out, "dp", axis=0, tiled=True),
        lax.all_gather(part_up, "dp", axis=0, tiled=True),
        lax.all_gather(part_down, "dp", axis=0, tiled=True),
        lax.all_gather(part_norm, "dp", axis=0, tiled=True),
    )
    norm_values = wnorm.astype(jnp.float32)
    gain_one, shift_one = (norm_values[:, 0], norm_values[:, 1])
    gain_two, shift_two = (norm_values[:, 2], norm_values[:, 3])
    token_segments = segments_of(doc_lengths, full_len)
    first_place = lax.axis_index("blk") * half_len
    query_segments = lax.dynamic_slice_in_dim(token_segments, first_place, half_len, 1)
    flat_rows = tokens.reshape(-1, width)
    projected = jnp.dot(flat_rows, wqkv, preferred_element_type=jnp.float32).astype(jnp.bfloat16)
    projected = projected.reshape(seqs_here, local_len, 3, head_groups, group_width)
    projected = lax.all_to_all(projected, "head", split_axis=3, concat_axis=1, tiled=True)
    queries = projected[:, :, 0, 0]
    keys_here = projected[:, :, 1, 0]
    values_here = projected[:, :, 2, 0]
    keys_all, values_all = (
        lax.all_gather(keys_here, "blk", axis=1, tiled=True),
        lax.all_gather(values_here, "blk", axis=1, tiled=True),
    )

    def attend(block_items):
        query_block, key_block, value_block, seg_query, seg_key = block_items
        scores = masked_scores(query_block, key_block, seg_query, seg_key, score_scale)
        largest = jnp.max(scores, axis=-1, keepdims=True)
        powers = jnp.exp(scores - largest)
        totals = jnp.sum(powers, axis=-1, keepdims=True)
        softmax_out = (powers / totals).astype(jnp.bfloat16)
        value_heads = value_block.reshape(value_block.shape[0], -1, HEAD_DIM)
        context = jnp.einsum(
            "hqk,khd->qhd", softmax_out, value_heads, preferred_element_type=jnp.float32
        )
        live_rows = (seg_query != 0).astype(jnp.float32)
        context = (
            (context * live_rows[:, None, None])
            .astype(jnp.bfloat16)
            .reshape(query_block.shape[0], -1)
        )
        return (context, largest[..., 0] + jnp.log(totals[..., 0]))

    context, log_sums = lax.map(
        attend, (queries, keys_all, values_all, query_segments, token_segments)
    )
    context = lax.all_to_all(
        context[:, :, None], "head", split_axis=1, concat_axis=2, tiled=True
    ).reshape(-1, width)
    tokens_f = flat_rows.astype(jnp.float32)
    branch = jnp.dot(context, wout, preferred_element_type=jnp.float32)
    first_in = tokens_f + branch
    first_out = layer_norm(first_in, gain_one, shift_one)
    first_low = first_out.astype(jnp.bfloat16)
    pre_act = jnp.dot(first_low, wup, preferred_element_type=jnp.float32)
    act_low = gelu_exact(pre_act).astype(jnp.bfloat16)
    ff_out = jnp.dot(act_low, wdown, preferred_element_type=jnp.float32)
    second_in = first_out + ff_out
    result = layer_norm(second_in, gain_two, shift_two)
    upstream = out_cotangent.reshape(-1, width).astype(jnp.float32)
    unused_two, second_back = jax.vjp(layer_norm, second_in, gain_two, shift_two)
    grad_second, grad_gain_two, grad_shift_two = second_back(upstream)
    grad_ff = grad_second.astype(jnp.bfloat16)
    grad_down = jnp.einsum("tf,td->fd", act_low, grad_ff, preferred_element_type=jnp.float32)
    grad_act = jnp.einsum("td,fd->tf", grad_ff, wdown, preferred_element_type=jnp.float32)
    unused_act, gelu_back = jax.vjp(gelu_exact, pre_act)
    grad_pre = gelu_back(grad_act)[0].astype(jnp.bfloat16)
    grad_up = jnp.einsum("td,tf->df", first_low, grad_pre, preferred_element_type=jnp.float32)
    grad_first = grad_second + jnp.einsum(
        "tf,df->td", grad_pre, wup, preferred_element_type=jnp.float32
    )
    unused_one, first_back = jax.vjp(layer_norm, first_in, gain_one, shift_one)
    grad_first_in, grad_gain_one, grad_shift_one = first_back(grad_first)
    grad_branch = grad_first_in.astype(jnp.bfloat16)
    grad_out_w = jnp.einsum("td,te->de", context, grad_branch, preferred_element_type=jnp.float32)
    grad_context = jnp.einsum(
        "te,de->td", grad_branch, wout, preferred_element_type=jnp.float32
    ).astype(jnp.bfloat16)
    grad_context = grad_context.reshape(seqs_here, local_len, head_groups, group_width)
    grad_context = lax.all_to_all(grad_context, "head", split_axis=2, concat_axis=1, tiled=True)[
        :, :, 0
    ]

    def attend_back(block_items):
        query_block, key_block, value_block, grad_block, seg_query, seg_key, log_sum = block_items
        scores = masked_scores(query_block, key_block, seg_query, seg_key, score_scale)
        softmax_out = jnp.exp(scores - log_sum[..., None])
        grad_heads = jnp.where((seg_query != 0)[:, None], grad_block, jnp.zeros_like(grad_block))
        grad_heads = grad_heads.reshape(grad_block.shape[0], -1, HEAD_DIM)
        query_heads = query_block.reshape(query_block.shape[0], -1, HEAD_DIM)
        key_heads = key_block.reshape(key_block.shape[0], -1, HEAD_DIM)
        value_heads = value_block.reshape(value_block.shape[0], -1, HEAD_DIM)
        grad_probs = jnp.einsum(
            "qhd,khd->hqk", grad_heads, value_heads, preferred_element_type=jnp.float32
        )
        grad_values = jnp.einsum(
            "hqk,qhd->khd",
            softmax_out.astype(jnp.bfloat16),
            grad_heads,
            preferred_element_type=jnp.float32,
        )
        inner_sum = jnp.sum(softmax_out * grad_probs, axis=-1, keepdims=True)
        grad_scores = (softmax_out * (grad_probs - inner_sum)).astype(jnp.bfloat16)
        grad_queries = (
            jnp.einsum("hqk,khd->qhd", grad_scores, key_heads, preferred_element_type=jnp.float32)
            * score_scale
        )
        grad_keys = (
            jnp.einsum("hqk,qhd->khd", grad_scores, query_heads, preferred_element_type=jnp.float32)
            * score_scale
        )
        return (
            grad_queries.reshape(query_block.shape[0], -1),
            grad_keys.reshape(key_block.shape[0], -1),
            grad_values.reshape(key_block.shape[0], -1),
        )

    grad_q, grad_k_all, grad_v_all = lax.map(
        attend_back,
        (queries, keys_all, values_all, grad_context, query_segments, token_segments, log_sums),
    )
    grad_k, grad_v = (
        lax.psum_scatter(
            grad_k_all.astype(jnp.bfloat16), "blk", scatter_dimension=1, tiled=True
        ).astype(jnp.float32),
        lax.psum_scatter(
            grad_v_all.astype(jnp.bfloat16), "blk", scatter_dimension=1, tiled=True
        ).astype(jnp.float32),
    )
    grad_mixed = jnp.stack([grad_q, grad_k, grad_v], axis=2)[:, :, :, None].astype(jnp.bfloat16)
    grad_mixed = lax.all_to_all(
        grad_mixed, "head", split_axis=1, concat_axis=3, tiled=True
    ).reshape(-1, 3 * width)
    grad_qkv = jnp.einsum("td,te->de", flat_rows, grad_mixed, preferred_element_type=jnp.float32)
    grad_tokens = grad_first_in + jnp.einsum(
        "te,de->td", grad_mixed, wqkv, preferred_element_type=jnp.float32
    )
    grad_norm = jnp.stack([grad_gain_one, grad_shift_one, grad_gain_two, grad_shift_two], axis=1)
    red_qkv, red_out, red_up, red_down, red_norm = (
        lax.psum_scatter(grad_qkv, "dp", scatter_dimension=0, tiled=True),
        lax.psum_scatter(grad_out_w, "dp", scatter_dimension=0, tiled=True),
        lax.psum_scatter(grad_up, "dp", scatter_dimension=0, tiled=True),
        lax.psum_scatter(grad_down, "dp", scatter_dimension=0, tiled=True),
        lax.psum_scatter(grad_norm, "dp", scatter_dimension=0, tiled=True),
    )
    finals = (
        lax.psum_scatter(
            red_qkv.astype(jnp.bfloat16), ("blk", "head"), scatter_dimension=0, tiled=True
        ).astype(jnp.float32),
        lax.psum_scatter(
            red_out.astype(jnp.bfloat16), ("blk", "head"), scatter_dimension=0, tiled=True
        ).astype(jnp.float32),
        lax.psum_scatter(
            red_up.astype(jnp.bfloat16), ("blk", "head"), scatter_dimension=0, tiled=True
        ).astype(jnp.float32),
        lax.psum_scatter(
            red_down.astype(jnp.bfloat16), ("blk", "head"), scatter_dimension=0, tiled=True
        ).astype(jnp.float32),
        lax.psum_scatter(
            red_norm.astype(jnp.bfloat16), ("blk", "head"), scatter_dimension=0, tiled=True
        ).astype(jnp.float32),
    )
    layer_out = result.astype(jnp.bfloat16).reshape(tokens.shape)
    input_grad = grad_tokens.reshape(tokens.shape)
    return (layer_out, input_grad, finals[0], finals[1], finals[2], finals[3], finals[4])


def solution(mesh):
    placed = (
        P("dp", ("blk", "head"), None),
        P("dp", None),
        P(("dp", "blk", "head"), None),
        P(("dp", "blk", "head"), None),
        P(("dp", "blk", "head"), None),
        P(("dp", "blk", "head"), None),
        P(("dp", "blk", "head"), None),
        P("dp", ("blk", "head"), None),
    )
    return jax.shard_map(
        body,
        mesh=mesh,
        in_specs=placed,
        out_specs=(
            P("dp", ("blk", "head"), None),
            P("dp", ("blk", "head"), None),
            P(("dp", "blk", "head"), None),
            P(("dp", "blk", "head"), None),
            P(("dp", "blk", "head"), None),
            P(("dp", "blk", "head"), None),
            P(("dp", "blk", "head"), None),
        ),
        check_vma=False,
    )
```

profile of v0, /device:TPU:0, one launch (start us, length us, event | category | flops | bytes accessed | tf_op | source)
XLA Modules:
  0.0 2025.5 jit_solution(12208231060600610439)
XLA Ops:
  7.2 11.7 all_gather.36
  20.4 98.0 %all-gather.12.cloned.1.call-done = bf16[1024,3072]{1,0:T(8,128)(2,1)} async-done(((bf16[128,3072]{1,0:T(8,128)(2,1)}), bf16[1024,3072]{1,0:T(8,128)(2,1)}) %all-gather.12.cloned.1.call-update) | async-done | bytes 6291472 | tf_op jit(solution)/shard_map/all_gather | solution.py:60
  157.2 16.7 all_gather.43
  176.3 12.2 all-gather.24.cloned.1.call-done
  192.6 31.0 %all-gather.26.cloned.1.call-done = bf16[4,512,1,1,512]{4,1,2,0,3:T(8,128)(2,1)} async-done(((bf16[4,256,1,1,512]{4,1,2,0,3:T(8,128)(2,1)}), bf16[4,512,1,1,512]{4,1,2,0,3:T(8,128)(2,1)}) %all-gather.26.cloned.1.call-update) | async-done | bytes 2097168 | tf_op jit(solution)/shard_map/all_gather | solution.py:80
  227.8 30.9 %while.26 = (s32[]{:T(128)}, bf16[4,256,512]{1,2,0:T(8,128)(2,1)S(1)}, f32[4,8,256]{2,1,0:T(8,128)}, bf16[4,512,512]{1,2,0:T(8,128)(2,1)}, s32[4,256]{1,0:T(4,12...) while((s32[]{:T(128)}, ...), condition=%wide.region_5.6_spmd, body=%wide.region_2.5_spmd.sunk | while | flops 281410048 | bytes 17903740 | solution.py:103
  278.5 122.0 %all-gather.18.cloned.1.call-done = bf16[1024,4096]{1,0:T(8,128)(2,1)} async-done(((bf16[128,4096]{1,0:T(8,128)(2,1)}), bf16[1024,4096]{1,0:T(8,128)(2,1)}) %all-gather.18.cloned.1.call-update) | async-done | bytes 8388624 | tf_op jit(solution)/shard_map/all_gather | solution.py:62
  400.5 27.3 %multiply_convert_fusion.1 = (bf16[512,4096]{1,0:T(8,128)(2,1)}, f32[512,4096]{1,0:T(8,128)}, f32[512,4096]{1,0:T(8,128)}) fusion(bf16[1024,4096]{1,0:T(8,128)(2,1)} %all-gather.18.cloned.1.call-done, f32[512,1024]{1,0:T(8,128)S(1)} %get-tuple-element.281, f32[1024]{0:T(1024)S(1)} %bitcast.219, f32[1024]{0:T(1024)S(1)} %bitcast.214, f32[512]{0:T(512)S(1)} %fusion.33, ...), kind=kOutput, calls=%fused_computation.50 | convolution fusion | flops 4433903616 | bytes 31469568 | tf_op jit(solution)/shard_map/dot_general | solution.py:114
  427.8 98.0 %all-gather.22.cloned.1.call-done = bf16[4096,1024]{1,0:T(8,128)(2,1)} async-done(((bf16[512,1024]{1,0:T(8,128)(2,1)}), bf16[4096,1024]{1,0:T(8,128)(2,1)}) %all-gather.22.cloned.1.call-update) | async-done | bytes 8388624 | tf_op jit(solution)/shard_map/all_gather | solution.py:63
  538.3 15.2 add_convert_fusion
  573.4 272.3 %while.27 = (s32[]{:T(128)}, bf16[4,256,512]{2,0,1:T(4,128)(2,1)}, bf16[4,512,512]{2,0,1:T(4,128)(2,1)}, bf16[4,512,512]{2,0,1:T(4,128)(2,1)}, bf16[4,512,512]{1...) while((s32[]{:T(128)}, bf16[4,256,512]{2,0,1:T(4,128)(2,1)}, ...), condition=%wide.region_16.17_spmd, body=%wide.region_14.16_spmd.sunk | while | flops 687995136 | bytes 61674492 | solution.py:177
  598.6 19.3 dynamic_update_slice.29
  622.1 19.3 dynamic_update_slice.30
  666.7 19.3 dynamic_update_slice.29
  690.2 19.3 dynamic_update_slice.30
  734.7 19.3 dynamic_update_slice.29
  758.3 19.3 dynamic_update_slice.30
  802.8 19.3 dynamic_update_slice.29
  826.3 19.3 dynamic_update_slice.30
  854.9 97.4 %all-reduce.5.cloned.1.call-done = (bf16[4,512,512]{2,0,1:T(4,128)(2,1)}, bf16[4,512,512]{2,0,1:T(4,128)(2,1)}) async-done(((bf16[4,512,512]{2,0,1:T(4,128)(2,1)}, bf16[4,512,512]{2,0,1:T(4,128)(2,1)}), (bf16[4,512,512]{2,0,1:T(4,128)(2,1)}, bf16[4,512,512]{2,0,1:T(4,128)(2,1)})) %all-reduce.5.cloned.1.call-update) | async-done | bytes 4194320
  983.4 10.5 fusion.38
  995.5 10.7 fusion.35
  1006.3 12.0 reduce-scatter.33.cloned.1.call-done
  1019.9 89.1 %reduce-scatter.19.cloned.1.call-done = f32[128,1024]{1,0:T(8,128)} async-done(((f32[1024,1024]{1,0:T(8,128)}), f32[128,1024]{1,0:T(8,128)}) %reduce-scatter.19.cloned.1.call-update) | async-done | bytes 524304 | tf_op jit(solution)/shard_map/reduce_scatter | solution.py:200
  1110.8 209.5 %reduce-scatter.17.cloned.1.call-done = f32[128,3072]{0,1:T(8,128)} async-done(((f32[1024,3072]{0,1:T(8,128)}), f32[128,3072]{0,1:T(8,128)}) %reduce-scatter.17.cloned.1.call-update) | async-done | bytes 1572880 | tf_op jit(solution)/shard_map/reduce_scatter | solution.py:199
  1323.1 283.2 %reduce-scatter.23.cloned.1.call-done = f32[128,4096]{1,0:T(8,128)} async-done(((f32[1024,4096]{1,0:T(8,128)}), f32[128,4096]{1,0:T(8,128)}) %reduce-scatter.23.cloned.1.call-update) | async-done | bytes 2097168 | tf_op jit(solution)/shard_map/reduce_scatter | solution.py:201
  1609.1 282.7 %reduce-scatter.27.cloned.1.call-done = f32[512,1024]{1,0:T(8,128)} async-done(((f32[4096,1024]{1,0:T(8,128)}), f32[512,1024]{1,0:T(8,128)}) %reduce-scatter.27.cloned.1.call-update) | async-done | bytes 2097168 | tf_op jit(solution)/shard_map/reduce_scatter | solution.py:202
  1894.5 18.6 reduce-scatter.35.cloned.1.call-done
  1923.0 13.1 reduce-scatter.21.cloned.1.call-done
  1937.6 24.3 %reduce-scatter.31.cloned.1.call-done = bf16[32,3072]{1,0:T(8,128)(2,1)} async-done(((bf16[128,3072]{1,0:T(8,128)(2,1)}), bf16[32,3072]{1,0:T(8,128)(2,1)}) %reduce-scatter.31.cloned.1.call-update) | async-done | bytes 196624
  1964.2 25.0 %reduce-scatter.25.cloned.1.call-done = bf16[32,4096]{1,0:T(8,128)(2,1)} async-done(((bf16[128,4096]{1,0:T(8,128)(2,1)}), bf16[32,4096]{1,0:T(8,128)(2,1)}) %reduce-scatter.25.cloned.1.call-update) | async-done | bytes 262160 | tf_op jit(solution)/shard_map/reduce_scatter | solution.py:212
  1991.0 25.8 %reduce-scatter.29.cloned.1.call-done = bf16[128,1024]{1,0:T(8,128)(2,1)} async-done(((bf16[512,1024]{1,0:T(8,128)(2,1)}), bf16[128,1024]{1,0:T(8,128)(2,1)}) %reduce-scatter.29.cloned.1.call-update) | async-done | bytes 262160 | tf_op jit(solution)/shard_map/reduce_scatter | solution.py:215
  (322 shorter events, 320.8 us)
Async XLA Ops:
  7.2 111.2 %all-gather.12.cloned.1.call-start = ((), (), s32[]{:S(2)}) async-start(), calls=%async_computation.14 | async-start | bytes 7077888 | tf_op jit(solution)/shard_map/all_gather | solution.py:60
  18.9 132.1 %all-gather.16.cloned.1.call-start = ((), (), s32[]{:S(2)}) async-start(), calls=%async_computation.16 | async-start | bytes 1310720 | tf_op jit(solution)/shard_map/all_gather | solution.py:55
  19.7 155.3 %all-gather.20.cloned.1.call-start = ((), (), s32[]{:S(2)}) async-start(), calls=%async_computation.18 | async-start | bytes 1310720 | tf_op jit(solution)/shard_map/all_gather | solution.py:56
  20.4 168.1 %all-gather.24.cloned.1.call-start = ((), (), s32[]{:S(2)}) async-start(), calls=%async_computation.27 | async-start | bytes 3145728 | tf_op jit(solution)/shard_map/all_gather | solution.py:81
  142.6 81.1 %all-gather.26.cloned.1.call-start = ((), (), s32[]{:S(2)}) async-start(), calls=%async_computation.28 | async-start | bytes 3145728 | tf_op jit(solution)/shard_map/all_gather | solution.py:80
  143.2 131.8 %all-gather.14.cloned.1.call-start = ((), (), s32[]{:S(2)}) async-start(), calls=%async_computation.15 | async-start | bytes 2359296 | tf_op jit(solution)/shard_map/all_gather | solution.py:61
  151.0 249.5 %all-gather.18.cloned.1.call-start = ((), (), s32[]{:S(2)}) async-start(), calls=%async_computation.17 | async-start | bytes 9437184 | tf_op jit(solution)/shard_map/all_gather | solution.py:62
  151.7 374.0 %all-gather.22.cloned.1.call-start = ((), (), s32[]{:S(2)}) async-start(), calls=%async_computation.19 | async-start | bytes 9437184 | tf_op jit(solution)/shard_map/all_gather | solution.py:63
  174.9 350.9 %copy-start.24 = (f32[1024,1]{0,1:T(1,128)}, f32[1024,1]{0,1:T(1,128)S(1)}, u32[]{:S(2)}) copy-start(f32[1024,1]{0,1:T(1,128)S(1)} %get-tuple-element.279) | copy-start | bytes 12292
  174.9 388.2 %copy-start.16 = (f32[1024,1]{0,1:T(1,128)}, f32[1024,1]{0,1:T(1,128)S(1)}, u32[]{:S(2)}) copy-start(f32[1024,1]{0,1:T(1,128)S(1)} %get-tuple-element.278) | copy-start | bytes 12292
  175.0 777.3 %all-reduce.5.cloned.1.call-start = ((), (), s32[]{:S(2)}) async-start(), calls=%async_computation.32 | async-start | bytes 8388608
  265.8 162.0 %copy-start.8 = (bf16[64,8,2,512]{3,1,2,0:T(8,128)(2,1)}, bf16[64,8,2,512]{3,1,2,0:T(8,128)(2,1)S(1)}, u32[]{:S(2)}) copy-start(bf16[64,8,2,512]{3,1,2,0:T(8,128)(2,1)S(1)} %copy.118) | copy-start | bytes 3145732
  278.1 285.0 %copy-start.3 = (f32[512,1024]{1,0:T(8,128)}, f32[512,1024]{1,0:T(8,128)S(1)}, u32[]{:S(2)}) copy-start(f32[512,1024]{1,0:T(8,128)S(1)} %get-tuple-element.281) | copy-start | bytes 6291460
  278.2 285.0 %copy-start.13 = (f32[512]{0:T(512)}, f32[512]{0:T(512)S(1)}, u32[]{:S(2)}) copy-start(f32[512]{0:T(512)S(1)} %broadcast_multiply_fusion.1) | copy-start | bytes 6148
  278.5 284.6 %copy-start.20 = (f32[512]{0:T(512)}, f32[512]{0:T(512)S(1)}, u32[]{:S(2)}) copy-start(f32[512]{0:T(512)S(1)} %fusion.33) | copy-start | bytes 6148
  538.3 15.2 copy-start.9
  587.0 30.9 %copy-start.19 = (pred[256]{0:T(512)(128)(4,1)S(1)}, pred[256]{0:T(512)(128)(4,1)}, u32[]{:S(2)}) copy-start(pred[256]{0:T(512)(128)(4,1)} %copy-done.18) | copy-start | bytes 772 | tf_op jit(solution)/shard_map/while
  655.1 30.9 %copy-start.19 = (pred[256]{0:T(512)(128)(4,1)S(1)}, pred[256]{0:T(512)(128)(4,1)}, u32[]{:S(2)}) copy-start(pred[256]{0:T(512)(128)(4,1)} %copy-done.18) | copy-start | bytes 772 | tf_op jit(solution)/shard_map/while
  723.1 30.9 %copy-start.19 = (pred[256]{0:T(512)(128)(4,1)S(1)}, pred[256]{0:T(512)(128)(4,1)}, u32[]{:S(2)}) copy-start(pred[256]{0:T(512)(128)(4,1)} %copy-done.18) | copy-start | bytes 772 | tf_op jit(solution)/shard_map/while
  791.2 30.9 %copy-start.19 = (pred[256]{0:T(512)(128)(4,1)S(1)}, pred[256]{0:T(512)(128)(4,1)}, u32[]{:S(2)}) copy-start(pred[256]{0:T(512)(128)(4,1)} %copy-done.18) | copy-start | bytes 772 | tf_op jit(solution)/shard_map/while
  845.7 172.6 %reduce-scatter.33.cloned.1.call-start = ((), (), s32[]{:S(2)}) async-start(), calls=%async_computation.30 | async-start | bytes 589824
  848.1 260.8 %reduce-scatter.19.cloned.1.call-start = ((), (), s32[]{:S(2)}) async-start(), calls=%async_computation.21 | async-start | bytes 4718592 | tf_op jit(solution)/shard_map/reduce_scatter | solution.py:200
  853.0 101.6 %copy-start.11 = (bf16[4,256,512]{2,0,1:T(4,128)(2,1)S(1)}, bf16[4,256,512]{2,0,1:T(4,128)(2,1)}, u32[]{:S(2)}) copy-start(bf16[4,256,512]{2,0,1:T(4,128)(2,1)} %get-tuple-element.111) | copy-start | bytes 3145732
  853.0 467.3 %reduce-scatter.17.cloned.1.call-start = ((), (), s32[]{:S(2)}) async-start(), calls=%async_computation.20 | async-start | bytes 14155776 | tf_op jit(solution)/shard_map/reduce_scatter | solution.py:199
  981.8 624.5 %reduce-scatter.23.cloned.1.call-start = ((), (), s32[]{:S(2)}) async-start(), calls=%async_computation.23 | async-start | bytes 18874368 | tf_op jit(solution)/shard_map/reduce_scatter | solution.py:201
  993.9 897.8 %reduce-scatter.27.cloned.1.call-start = ((), (), s32[]{:S(2)}) async-start(), calls=%async_computation.25 | async-start | bytes 18874368 | tf_op jit(solution)/shard_map/reduce_scatter | solution.py:202
  1006.3 906.8 %reduce-scatter.35.cloned.1.call-start = ((), (), s32[]{:S(2)}) async-start(), calls=%async_computation.31 | async-start | bytes 40960
  1019.8 916.2 %reduce-scatter.21.cloned.1.call-start = ((), (), s32[]{:S(2)}) async-start(), calls=%async_computation.22 | async-start | bytes 327680 | tf_op jit(solution)/shard_map/reduce_scatter | solution.py:209
  1110.7 851.1 %reduce-scatter.31.cloned.1.call-start = ((), (), s32[]{:S(2)}) async-start(), calls=%async_computation.29 | async-start | bytes 983040
  1323.0 591.5 %copy-start.7 = (f32[512,1024]{1,0:T(8,128)S(1)}, f32[512,1024]{1,0:T(8,128)}, u32[]{:S(2)}) copy-start(f32[512,1024]{1,0:T(8,128)} %copy-done.5) | copy-start | bytes 6291460
  1323.0 666.2 %reduce-scatter.25.cloned.1.call-start = ((), (), s32[]{:S(2)}) async-start(), calls=%async_computation.24 | async-start | bytes 1310720 | tf_op jit(solution)/shard_map/reduce_scatter | solution.py:212
  1609.0 407.7 %reduce-scatter.29.cloned.1.call-start = ((), (), s32[]{:S(2)}) async-start(), calls=%async_computation.26 | async-start | bytes 1310720 | tf_op jit(solution)/shard_map/reduce_scatter | solution.py:215
  (30 other events, 106.3 us)
Sparse Core Ops, SparseCore 0:
  19.0 99.3 all-gather.11
  120.0 14.9 all-gather.15
  136.5 18.1 all-gather.19
  156.6 31.8 all-gather.23
  190.5 33.1 all-gather.25
  225.6 49.2 all-gather.13
  277.1 123.4 all-gather.17
  402.6 123.1 all-gather.21
  845.8 106.4 all-reduce.4
  956.4 61.9 reduce-scatter.32
  1022.0 86.9 reduce-scatter.18
  1112.8 207.4 reduce-scatter.16
  1324.6 281.6 reduce-scatter.22
  1609.9 281.7 reduce-scatter.26
  1894.7 18.3 reduce-scatter.34
  1916.0 20.0 reduce-scatter.20
  1938.6 23.2 reduce-scatter.30
  1964.3 24.8 reduce-scatter.24
  1991.9 24.8 reduce-scatter.28
where the time goes:
time: 2050 us; the launch traced here: 2030 us
  waiting for transfers between devices  1450 us (71%)
  local copies, waits for them, and re-layouts  282 us (14%)
  matrix products  172 us (8%)
  blocking collectives  63.4 us (3%)
  other arithmetic  37.7 us (2%)
    reduce_scatter x1, waiting for transfers between devices, body(): lax.psum_scatter(grad_up, 'dp', scatter_dimension=0, tiled=True)  283 us
    reduce_scatter x1, waiting for transfers between devices, body(): lax.psum_scatter(grad_down, 'dp', scatter_dimension=0, tiled=True)  283 us
    reduce_scatter x1, waiting for transfers between devices, body(): lax.psum_scatter(grad_qkv, 'dp', scatter_dimension=0, tiled=True)  210 us
    dynamic_update_slice x24, local copies, waits for them, and re-layouts, body(): lax.map(attend_back, (queries, keys_all, values_all, grad_context, query_...  204 us
    unnamed x23, waiting for transfers between devices  155 us
    all_gather x1, waiting for transfers between devices, body(): lax.all_gather(part_up, 'dp', axis=0, tiled=True)  122 us
    all_gather x1, waiting for transfers between devices, body(): lax.all_gather(part_down, 'dp', axis=0, tiled=True)  98 us
    all_gather x1, waiting for transfers between devices, body(): lax.all_gather(part_qkv, 'dp', axis=0, tiled=True)  98 us
  transfers between devices with their start and end apart: 19, of which 17 were waited for; matrix products, arithmetic and copies ran while one was open for 8% of the time, Pallas kernels for 0%

commit v1 on v0

v1 whole, which is shorter than its diff:
```python
import jax
import jax.numpy as jnp
from jax import lax
from jax.experimental import pallas as pl
from jax.experimental.pallas import tpu as pltpu
from jax.sharding import PartitionSpec as P

HEAD_DIM = 64
ALL = ("dp", "blk", "head")
GROUP = ("blk", "head")


epsilon = 1e-12


def segments_of(doc_lengths, length):
    doc_ends = jnp.cumsum(doc_lengths, axis=-1, dtype=jnp.int32)
    places = jnp.arange(length, dtype=jnp.int32)
    passed = jnp.sum(
        (doc_ends[..., None, :] <= places[:, None]).astype(jnp.int32), axis=-1, dtype=jnp.int32
    )
    return jnp.where(places < doc_ends[..., -1:], passed + 1, 0)


def layer_norm(hidden, gain, shift):
    average = jnp.mean(hidden, axis=-1, keepdims=True)
    centred = hidden - average
    spread = jnp.mean(centred * centred, axis=-1, keepdims=True)
    return centred * lax.rsqrt(spread + epsilon) * gain + shift


def gelu_exact(values_in):
    return jax.nn.gelu(values_in, approximate=False)


def attn_fwd_kernel(q_ref, k_ref, v_ref, segc_ref, segr_ref, out_ref, lse_ref):
    length = q_ref.shape[0]
    scaled = q_ref[...] * jnp.bfloat16(HEAD_DIM ** (-0.5))
    key_pair = k_ref[...]
    value_t = v_ref[...].T
    lanes = lax.broadcasted_iota(jnp.int32, key_pair.shape, 1)
    allowed = segc_ref[...] == segr_ref[...]
    parts = []
    for h in range(2):
        own = (lanes >= h * HEAD_DIM) & (lanes < (h + 1) * HEAD_DIM)
        keys = jnp.where(own, key_pair, jnp.zeros_like(key_pair))
        scores = lax.dot_general(
            keys, scaled, (((1,), (1,)), ((), ())), preferred_element_type=jnp.float32
        )
        scores = jnp.where(allowed, scores, -1e30)
        largest = jnp.max(scores, axis=0, keepdims=True)
        powers = jnp.exp(scores - largest)
        totals = jnp.sum(powers, axis=0, keepdims=True)
        probs = (powers * (1.0 / totals)).astype(jnp.bfloat16)
        parts.append(
            jnp.dot(
                value_t[h * HEAD_DIM : (h + 1) * HEAD_DIM], probs, preferred_element_type=jnp.float32
            )
        )
        lse_ref[0, h : h + 1, :] = largest + jnp.log(totals)
    live = (segc_ref[...] != 0).astype(jnp.float32)
    context = jnp.concatenate(parts, axis=0).T * live
    out_ref[...] = context.astype(jnp.bfloat16)


def attn_bwd_kernel(
    q_ref, k_ref, v_ref, g_ref, segc_ref, segr_ref, lse_ref, dq_ref, dk_ref, dv_ref
):
    scaled = q_ref[...] * jnp.bfloat16(HEAD_DIM ** (-0.5))
    key_pair = k_ref[...]
    value_pair = v_ref[...]
    key_t = key_pair.T
    grads = jnp.where(segc_ref[...] != 0, g_ref[...], jnp.zeros_like(g_ref[...]))
    lanes = lax.broadcasted_iota(jnp.int32, key_pair.shape, 1)
    allowed = segc_ref[...] == segr_ref[...]
    contract = (((1,), (1,)), ((), ()))
    dq_parts = []
    dk = None
    dv = None
    for h in range(2):
        own = (lanes >= h * HEAD_DIM) & (lanes < (h + 1) * HEAD_DIM)
        zero = jnp.zeros_like(key_pair)
        keys = jnp.where(own, key_pair, zero)
        values = jnp.where(own, value_pair, zero)
        queries = jnp.where(own, scaled, zero)
        grad_own = jnp.where(own, grads, zero)
        scores = lax.dot_general(keys, scaled, contract, preferred_element_type=jnp.float32)
        scores = jnp.where(allowed, scores, -1e30)
        probs = jnp.exp(scores - lse_ref[0, h : h + 1, :])
        grad_probs = lax.dot_general(values, grads, contract, preferred_element_type=jnp.float32)
        inner = jnp.sum(probs * grad_probs, axis=0, keepdims=True)
        grad_scores = (probs * (grad_probs - inner)).astype(jnp.bfloat16)
        dv_h = jnp.dot(probs.astype(jnp.bfloat16), grad_own, preferred_element_type=jnp.float32)
        dk_h = jnp.dot(grad_scores, queries, preferred_element_type=jnp.float32)
        dv = dv_h if dv is None else dv + dv_h
        dk = dk_h if dk is None else dk + dk_h
        dq_parts.append(
            jnp.dot(
                key_t[h * HEAD_DIM : (h + 1) * HEAD_DIM],
                grad_scores,
                preferred_element_type=jnp.float32,
            )
        )
    dq = jnp.concatenate(dq_parts, axis=0).T * (HEAD_DIM ** (-0.5))
    dq_ref[...] = dq.astype(jnp.bfloat16)
    dk_ref[...] = dk.astype(jnp.bfloat16)
    dv_ref[...] = dv.astype(jnp.bfloat16)


def attention(projected, seg_col, seg_row):
    length, width3 = projected.shape
    pairs = width3 // 3 // (2 * HEAD_DIM)
    lane = 2 * HEAD_DIM
    col = lambda base: pl.BlockSpec((length, lane), lambda i: (0, base * pairs + i))
    return pl.pallas_call(
        attn_fwd_kernel,
        grid=(pairs,),
        in_specs=[
            col(0),
            col(1),
            col(2),
            pl.BlockSpec((length, 1), lambda i: (0, 0)),
            pl.BlockSpec((1, length), lambda i: (0, 0)),
        ],
        out_specs=[
            pl.BlockSpec((length, lane), lambda i: (0, i)),
            pl.BlockSpec((1, 2, length), lambda i: (i, 0, 0)),
        ],
        out_shape=[
            jax.ShapeDtypeStruct((length, width3 // 3), jnp.bfloat16),
            jax.ShapeDtypeStruct((pairs, 2, length), jnp.float32),
        ],
        compiler_params=pltpu.CompilerParams(vmem_limit_bytes=32 * 2**20),
    )(projected, projected, projected, seg_col, seg_row)


def attention_back(projected, grad_context, seg_col, seg_row, lse):
    length, width3 = projected.shape
    width = width3 // 3
    pairs = width // (2 * HEAD_DIM)
    lane = 2 * HEAD_DIM
    col = lambda base: pl.BlockSpec((length, lane), lambda i: (0, base * pairs + i))
    return pl.pallas_call(
        attn_bwd_kernel,
        grid=(pairs,),
        in_specs=[
            col(0),
            col(1),
            col(2),
            col(0),
            pl.BlockSpec((length, 1), lambda i: (0, 0)),
            pl.BlockSpec((1, length), lambda i: (0, 0)),
            pl.BlockSpec((1, 2, length), lambda i: (i, 0, 0)),
        ],
        out_specs=[col(0)] * 3,
        out_shape=[jax.ShapeDtypeStruct((length, width), jnp.bfloat16)] * 3,
        compiler_params=pltpu.CompilerParams(vmem_limit_bytes=32 * 2**20),
    )(projected, projected, projected, grad_context, seg_col, seg_row, lse)


def body(
    tokens, doc_lengths, qkv_weight, out_weight, up_weight, down_weight, norm_params, out_cotangent
):
    seqs_here, local_len, width = tokens.shape
    group = lax.axis_size("blk") * lax.axis_size("head")
    place = lax.axis_index("blk") * lax.axis_size("head") + lax.axis_index("head")
    full_len = local_len * group

    def to_sequences(v):
        return lax.all_to_all(v, GROUP, split_axis=0, concat_axis=1, tiled=True).reshape(
            -1, width
        )

    def to_positions(v):
        v = v.reshape(seqs_here // group, full_len, width)
        return lax.all_to_all(v, GROUP, split_axis=1, concat_axis=0, tiled=True)

    flat_rows = to_sequences(tokens)
    upstream = to_sequences(out_cotangent).astype(jnp.float32)
    gather = lambda w: lax.all_gather(w, ALL, axis=0, tiled=True)
    wqkv, wout, wup, wdown, wnorm = (
        gather(qkv_weight),
        gather(out_weight),
        gather(up_weight),
        gather(down_weight),
        gather(norm_params),
    )
    norm_values = wnorm.astype(jnp.float32)
    gain_one, shift_one = (norm_values[:, 0], norm_values[:, 1])
    gain_two, shift_two = (norm_values[:, 2], norm_values[:, 3])
    own_lengths = lax.dynamic_slice_in_dim(doc_lengths, place, 1, 0)
    token_segments = segments_of(own_lengths, full_len)
    seg_row = token_segments
    seg_col = token_segments.reshape(full_len, 1)
    projected = jnp.dot(flat_rows, wqkv, preferred_element_type=jnp.float32).astype(jnp.bfloat16)
    context, log_sums = attention(projected, seg_col, seg_row)
    tokens_f = flat_rows.astype(jnp.float32)
    branch = jnp.dot(context, wout, preferred_element_type=jnp.float32)
    first_in = tokens_f + branch
    first_out = layer_norm(first_in, gain_one, shift_one)
    first_low = first_out.astype(jnp.bfloat16)
    pre_act = jnp.dot(first_low, wup, preferred_element_type=jnp.float32)
    act_low = gelu_exact(pre_act).astype(jnp.bfloat16)
    ff_out = jnp.dot(act_low, wdown, preferred_element_type=jnp.float32)
    second_in = first_out + ff_out
    result = layer_norm(second_in, gain_two, shift_two)
    unused_two, second_back = jax.vjp(layer_norm, second_in, gain_two, shift_two)
    grad_second, grad_gain_two, grad_shift_two = second_back(upstream)
    grad_ff = grad_second.astype(jnp.bfloat16)
    scatter = lambda g: lax.psum_scatter(
        g.astype(jnp.bfloat16), ALL, scatter_dimension=0, tiled=True
    ).astype(jnp.float32)
    grad_down = scatter(
        jnp.einsum("tf,td->fd", act_low, grad_ff, preferred_element_type=jnp.float32)
    )
    grad_act = jnp.einsum("td,fd->tf", grad_ff, wdown, preferred_element_type=jnp.float32)
    unused_act, gelu_back = jax.vjp(gelu_exact, pre_act)
    grad_pre = gelu_back(grad_act)[0].astype(jnp.bfloat16)
    grad_up = scatter(
        jnp.einsum("td,tf->df", first_low, grad_pre, preferred_element_type=jnp.float32)
    )
    grad_first = grad_second + jnp.einsum(
        "tf,df->td", grad_pre, wup, preferred_element_type=jnp.float32
    )
    unused_one, first_back = jax.vjp(layer_norm, first_in, gain_one, shift_one)
    grad_first_in, grad_gain_one, grad_shift_one = first_back(grad_first)
    grad_branch = grad_first_in.astype(jnp.bfloat16)
    grad_out_w = scatter(
        jnp.einsum("td,te->de", context, grad_branch, preferred_element_type=jnp.float32)
    )
    grad_context = jnp.einsum(
        "te,de->td", grad_branch, wout, preferred_element_type=jnp.float32
    ).astype(jnp.bfloat16)
    grad_q, grad_k, grad_v = attention_back(projected, grad_context, seg_col, seg_row, log_sums)
    grad_mixed = jnp.concatenate([grad_q, grad_k, grad_v], axis=1)
    grad_qkv = scatter(
        jnp.einsum("td,te->de", flat_rows, grad_mixed, preferred_element_type=jnp.float32)
    )
    grad_tokens = grad_first_in + jnp.einsum(
        "te,de->td", grad_mixed, wqkv, preferred_element_type=jnp.float32
    )
    grad_norm = jnp.stack([grad_gain_one, grad_shift_one, grad_gain_two, grad_shift_two], axis=1)
    grad_norm = lax.psum_scatter(grad_norm, ALL, scatter_dimension=0, tiled=True)
    layer_out = to_positions(result.astype(jnp.bfloat16))
    input_grad = to_positions(grad_tokens.astype(jnp.bfloat16)).astype(jnp.float32)
    return (layer_out, input_grad, grad_qkv, grad_out_w, grad_up, grad_down, grad_norm)


def solution(mesh):
    placed = (
        P("dp", ("blk", "head"), None),
        P("dp", None),
        P(("dp", "blk", "head"), None),
        P(("dp", "blk", "head"), None),
        P(("dp", "blk", "head"), None),
        P(("dp", "blk", "head"), None),
        P(("dp", "blk", "head"), None),
        P("dp", ("blk", "head"), None),
    )
    return jax.shard_map(
        body,
        mesh=mesh,
        in_specs=placed,
        out_specs=(
            P("dp", ("blk", "head"), None),
            P("dp", ("blk", "head"), None),
            P(("dp", "blk", "head"), None),
            P(("dp", "blk", "head"), None),
            P(("dp", "blk", "head"), None),
            P(("dp", "blk", "head"), None),
            P(("dp", "blk", "head"), None),
        ),
        check_vma=False,
    )
```

time: 2050 us -> 1050 us (0.51)
  waiting for transfers between devices: 1450 us -> 752 us
  local copies, waits for them, and re-layouts: 282 us -> 40.5 us
  matrix products: 172 us -> 111 us
  Pallas kernels: 0 us -> 31.7 us
    reduce_scatter x7 -> x3, waiting for transfers between devices: 928 us -> 421 us  [body(): lax.psum_scatter(g.astype(jnp.bfloat16), ALL, scatter_dimension=0, tiled=...]
    dynamic_update_slice x28 -> x0, local copies, waits for them, and re-layouts: 204 us -> none  [the longest x24 204 us: body(): lax.map(attend_back, (queries, keys_all, values_all, grad_context, query_...]
    all_gather x8 -> x4, waiting for transfers between devices: 370 us -> 174 us  [body(): gather = lambda w: lax.all_gather(w, ALL, axis=0, tiled=True)]
    dot_general x28 -> x0, matrix products: 53.4 us -> none  [the longest x8 14.5 us: masked_scores(): jnp.einsum('qhd,khd->hqk', query_heads, key_heads, preferred_element_type...]
    pallas_call x0 -> x2, Pallas kernels: none -> 31.7 us  [the longest x1 19.4 us: attention_back(): pl.pallas_call(attn_bwd_kernel, grid=(pairs,), in_specs=[col(0), col(1),...]
    dynamic_slice x41 -> x1, local copies, waits for them, and re-layouts: 28.6 us -> 0.01 us  [body(): own_lengths = lax.dynamic_slice_in_dim(doc_lengths, place, 1, 0)]
    unnamed x70 -> x42, local copies, waits for them, and re-layouts: 12.4 us -> 35.1 us
    all_to_all x4 -> x0, blocking collectives: 22.2 us -> none  [the longest x1 6.46 us: body(): lax.all_to_all(grad_mixed, 'head', split_axis=1, concat_axis=3, tiled=True)]
  transfers between devices with their start and end apart: 19 -> 13, of which waited for: 17 -> 10; matrix products, arithmetic and copies ran while one was open for 8% -> 12% of each run, Pallas kernels for 0% -> 3%
where the time goes in v1:
time: 1050 us; the launch traced here: 1040 us
  waiting for transfers between devices  752 us (72%)
  matrix products  111 us (11%)
  blocking collectives  48.9 us (5%)
  local copies, waits for them, and re-layouts  40.5 us (4%)
  Pallas kernels  31.7 us (3%)
  other arithmetic  27.8 us (3%)
  starting transfers between devices  16.2 us (2%)
  between operations  14.6 us (1%)
    reduce_scatter x3, waiting for transfers between devices, body(): lax.psum_scatter(g.astype(jnp.bfloat16), ALL, scatter_dimension=0, tiled=...  421 us
    all_gather x4, waiting for transfers between devices, body(): gather = lambda w: lax.all_gather(w, ALL, axis=0, tiled=True)  174 us
    unnamed x11, waiting for transfers between devices  142 us
    all_gather x1, blocking collectives, body(): gather = lambda w: lax.all_gather(w, ALL, axis=0, tiled=True)  48.9 us
    unnamed x42, local copies, waits for them, and re-layouts  35.1 us
    dot_general x1, matrix products, body(): pre_act = jnp.dot(first_low, wup, preferred_element_type=jnp.float32)  27.1 us
  transfers between devices with their start and end apart: 13, of which 10 were waited for; matrix products, arithmetic and copies ran while one was open for 12% of the time, Pallas kernels for 3%

profile of v1, /device:TPU:0, one launch (start us, length us, event | category | flops | bytes accessed | tf_op | source)
XLA Modules:
  0.0 1041.8 jit_solution(11206594414004551261)
XLA Ops:
  10.0 4.2 all-to-all-start.2
  15.0 48.9 %all-gather = bf16[32,32,4]{1,2,0:T(4,128)(2,1)S(1)} all-gather(bf16[1,32,4]{1,2,0:T(4,128)(2,1)} %bitcast.92), channel_id=1, replica_groups=mesh['dp'=8,'blk'=2,'head'=2] {'dp','blk','head'}, dimensions={0}, use_global_device_ids=true | all-gather | bytes 8448 | tf_op jit(solution)/shard_map/all_gather | solution.py:180
  64.3 3.5 all-to-all-start
  69.4 15.4 %all-to-all-done = bf16[4,128,1024]{2,1,0:T(8,128)(2,1)S(1)} async-done(((bf16[4,128,1024]{2,1,0:T(8,128)(2,1)}), bf16[4,128,1024]{2,1,0:T(8,128)(2,1)S(1)}, u32[]{:S(2)}, u32[]{:S(2)}) %all-to-all-start) | async-done | bytes 1048608 | tf_op jit(solution)/shard_map/all_to_all | solution.py:170
  84.8 10.9 %all-gather.6.cloned.1.call-done = bf16[1024,3072]{1,0:T(8,128)(2,1)} async-done(((bf16[32,3072]{1,0:T(8,128)(2,1)}), bf16[1024,3072]{1,0:T(8,128)(2,1)}) %all-gather.6.cloned.1.call-update) | async-done | bytes 6291472 | tf_op jit(solution)/shard_map/all_gather | solution.py:180
  95.7 6.5 convolution_convert_fusion.2.q_ref.k_ref.v_ref
  102.2 12.3 %shard_map.135 = (bf16[512,1024]{1,0:T(8,128)(2,1)S(1)}, f32[8,2,512]{2,1,0:T(2,128)S(1)}) custom-call(bf16[512,3072]{1,0:T(8,128)(2,1)S(1)} %convolution_convert_fusion.2.q_ref.k_ref.v_ref, bf16[512,3072]{1,0:T(8,128)(2,1)S(1)} %convolution_convert_fusion.2.q_ref.k_ref.v_ref, bf16[512,3072]{1,0:T(8,128)(2,1)S(1)} %convolution_convert_fusion.2.q_ref.k_ref.v_ref, ...), custom_call_target="tpu_custom_call" | custom-call | tf_op jit(solution)/shard_map/pallas_call | solution.py:115
  115.5 37.1 %all-gather.8.cloned.1.call-done = bf16[1024,1024]{1,0:T(8,128)(2,1)} async-done(((bf16[32,1024]{1,0:T(8,128)(2,1)}), bf16[1024,1024]{1,0:T(8,128)(2,1)}) %all-gather.8.cloned.1.call-update) | async-done | bytes 2097168 | tf_op jit(solution)/shard_map/all_gather | solution.py:180
  157.9 74.1 %all-gather.10.cloned.1.call-done = bf16[1024,4096]{1,0:T(8,128)(2,1)} async-done(((bf16[32,4096]{1,0:T(8,128)(2,1)}), bf16[1024,4096]{1,0:T(8,128)(2,1)}) %all-gather.10.cloned.1.call-update) | async-done | bytes 8388624 | tf_op jit(solution)/shard_map/all_gather | solution.py:180
  232.0 27.1 %multiply_convert_fusion = (bf16[512,4096]{1,0:T(8,128)(2,1)}, f32[512,4096]{1,0:T(8,128)}, f32[512,4096]{1,0:T(8,128)}) fusion(bf16[1024,4096]{1,0:T(8,128)(2,1)} %all-gather.10.cloned.1.call-done, f32[512,1024]{1,0:T(8,128)} %copy-done.5, f32[1024]{0:T(1024)S(1)} %bitcast.87, f32[1024]{0:T(1024)S(1)} %bitcast.82, f32[512]{0:T(512)S(1)} %fusion.15, ...), kind=kOutput, calls=%fused_computation.3 | convolution fusion | flops 4433903616 | bytes 31469568 | tf_op jit(solution)/shard_map/dot_general | solution.py:202
  259.2 51.7 %all-gather.12.cloned.1.call-done = bf16[4096,1024]{1,0:T(8,128)(2,1)} async-done(((bf16[128,1024]{1,0:T(8,128)(2,1)}), bf16[4096,1024]{1,0:T(8,128)(2,1)}) %all-gather.12.cloned.1.call-update) | async-done | bytes 8388624 | tf_op jit(solution)/shard_map/all_gather | solution.py:180
  310.9 9.9 fusion.26
  323.9 15.2 %add_convert_fusion = bf16[512,4096]{1,0:T(8,128)(2,1)} fusion(f32[512,4096]{1,0:T(8,128)} %get-tuple-element.69, f32[512,4096]{1,0:T(8,128)} %get-tuple-element.77, bf16[4096,1024]{1,0:T(8,128)(2,1)} %all-gather.12.cloned.1.call-done, f32[512,1024]{1,0:T(8,128)S(1)} %get-tuple-element.67, f32[512]{0:T(512)S(1)} %negate_multiply_fusion.2), kind=kOutput, calls=%fused_computation.2 | convolution fusion | flops 4325376000 | bytes 31459328 | tf_op jit(solution)/shard_map/td,fd->tf/dot_general | solution.py:216
  339.1 9.1 multiply_reduce_fusion
  351.2 4.6 convolution_convert_fusion.3
  355.9 3.5 convolution_convert_fusion.4.g_ref
  359.4 19.4 %shard_map.136 = (bf16[512,1024]{1,0:T(8,128)(2,1)S(1)}, bf16[512,1024]{1,0:T(8,128)(2,1)S(1)}, bf16[512,1024]{1,0:T(8,128)(2,1)S(1)}) custom-call(bf16[512,3072]{1,0:T(8,128)(2,1)S(1)} %convolution_convert_fusion.2.q_ref.k_ref.v_ref, bf16[512,3072]{1,0:T(8,128)(2,1)S(1)} %convolution_convert_fusion.2.q_ref.k_ref.v_ref, ...), custom_call_target="tpu_custom_call" | custom-call | tf_op jit(solution)/shard_map/pallas_call | solution.py:143
  380.7 5.3 convert_bitcast_fusion
  386.0 8.7 copy.39
  396.3 9.2 convolution_convert_fusion.1
  407.1 9.4 convolution_convert_fusion
  418.1 7.2 fusion.12
  427.5 7.3 reduce.5
  436.8 3.8 all-to-all-start.3
  443.4 8.3 reduce.4
  451.7 3.7 reshape.214
  455.4 4.2 all-to-all-start.1
  459.7 24.7 %reduce-scatter.18.cloned.1.call-done = f32[32,4]{1,0:T(8,128)} async-done(((f32[1024,4]{1,0:T(8,128)}), f32[32,4]{1,0:T(8,128)}) %reduce-scatter.18.cloned.1.call-update) | async-done | bytes 528
  492.5 126.9 %reduce-scatter.10.cloned.1.call-done = bf16[32,1024]{1,0:T(8,128)(2,1)} async-done(((bf16[1024,1024]{1,0:T(8,128)(2,1)}), bf16[32,1024]{1,0:T(8,128)(2,1)}) %reduce-scatter.10.cloned.1.call-update) | async-done | bytes 65552 | tf_op jit(solution)/shard_map/reduce_scatter | solution.py:210
  620.9 114.4 %reduce-scatter.16.cloned.1.call-done = bf16[32,3072]{1,0:T(8,128)(2,1)} async-done(((bf16[1024,3072]{1,0:T(8,128)(2,1)}), bf16[32,3072]{1,0:T(8,128)(2,1)}) %reduce-scatter.16.cloned.1.call-update) | async-done | bytes 196624
  737.6 148.1 %reduce-scatter.12.cloned.1.call-done = bf16[32,4096]{1,0:T(8,128)(2,1)} async-done(((bf16[1024,4096]{1,0:T(8,128)(2,1)}), bf16[32,4096]{1,0:T(8,128)(2,1)}) %reduce-scatter.12.cloned.1.call-update) | async-done | bytes 262160 | tf_op jit(solution)/shard_map/reduce_scatter | solution.py:210
  887.5 145.5 %reduce-scatter.14.cloned.1.call-done = bf16[128,1024]{1,0:T(8,128)(2,1)} async-done(((bf16[4096,1024]{1,0:T(8,128)(2,1)}), bf16[128,1024]{1,0:T(8,128)(2,1)}) %reduce-scatter.14.cloned.1.call-update) | async-done | bytes 262160 | tf_op jit(solution)/shard_map/reduce_scatter | solution.py:210
  (94 shorter events, 46.9 us)
Async XLA Ops:
  7.2 7.1 copy-start
  7.2 88.5 %all-gather.6.cloned.1.call-start = ((), (), s32[]{:S(2)}) async-start(), calls=%async_computation.9 | async-start | bytes 6488064 | tf_op jit(solution)/shard_map/all_gather | solution.py:180
  7.9 144.8 %all-gather.8.cloned.1.call-start = ((), (), s32[]{:S(2)}) async-start(), calls=%async_computation.10 | async-start | bytes 2162688 | tf_op jit(solution)/shard_map/all_gather | solution.py:180
  8.7 223.3 %all-gather.10.cloned.1.call-start = ((), (), s32[]{:S(2)}) async-start(), calls=%async_computation.11 | async-start | bytes 8650752 | tf_op jit(solution)/shard_map/all_gather | solution.py:180
  9.4 301.5 %all-gather.12.cloned.1.call-start = ((), (), s32[]{:S(2)}) async-start(), calls=%async_computation.12 | async-start | bytes 8650752 | tf_op jit(solution)/shard_map/all_gather | solution.py:180
  10.0 54.3 %all-to-all-start.2 = ((bf16[4,128,1024]{2,1,0:T(8,128)(2,1)}), bf16[4,128,1024]{2,1,0:T(8,128)(2,1)S(1)}, u32[]{:S(2)}, u32[]{:S(2)}) async-start(bf16[4,128,1024]{2,1,0:T(8,128)(2,1)} %param.15), calls=%async_computation.2 | async-start | bytes 2097152 | tf_op jit(solution)/shard_map/all_to_all | solution.py:170
  64.3 31.4 %copy-start.3 = (bf16[4,128,1024]{2,1,0:T(8,128)(2,1)}, bf16[4,128,1024]{2,1,0:T(8,128)(2,1)S(1)}, u32[]{:S(2)}) copy-start(bf16[4,128,1024]{2,1,0:T(8,128)(2,1)S(1)} %all-to-all-done.2) | copy-start | bytes 3145732
  64.3 20.5 %all-to-all-start = ((bf16[4,128,1024]{2,1,0:T(8,128)(2,1)}), bf16[4,128,1024]{2,1,0:T(8,128)(2,1)S(1)}, u32[]{:S(2)}, u32[]{:S(2)}) async-start(bf16[4,128,1024]{2,1,0:T(8,128)(2,1)} %param.8), calls=%async_computation | async-start | bytes 2097152 | tf_op jit(solution)/shard_map/all_to_all | solution.py:170
  67.8 416.5 %reduce-scatter.18.cloned.1.call-start = ((), (), s32[]{:S(2)}) async-start(), calls=%async_computation.17 | async-start | bytes 540672
  84.8 10.9 %copy-start.11 = (bf16[4,128,1024]{2,1,0:T(8,128)(2,1)}, bf16[4,128,1024]{2,1,0:T(8,128)(2,1)S(1)}, u32[]{:S(2)}) copy-start(bf16[4,128,1024]{2,1,0:T(8,128)(2,1)S(1)} %all-to-all-done) | copy-start | bytes 3145732
  114.6 1.0 copy-start.2
  156.2 1.3 copy-start.5
  310.9 10.3 copy-start.4
  323.9 15.2 %copy-start.8 = (f32[512,1024]{1,0:T(8,128)}, f32[512,1024]{1,0:T(8,128)S(1)}, u32[]{:S(2)}) copy-start(f32[512,1024]{1,0:T(8,128)S(1)} %get-tuple-element.67) | copy-start | bytes 6291460
  323.9 15.2 %copy-start.6 = (f32[512,1024]{1,0:T(8,128)S(1)}, f32[512,1024]{1,0:T(8,128)}, u32[]{:S(2)}) copy-start(f32[512,1024]{1,0:T(8,128)} %copy-done.5) | copy-start | bytes 6291460
  351.2 268.2 %reduce-scatter.10.cloned.1.call-start = ((), (), s32[]{:S(2)}) async-start(), calls=%async_computation.13 | async-start | bytes 2162688 | tf_op jit(solution)/shard_map/reduce_scatter | solution.py:210
  355.8 379.4 %reduce-scatter.16.cloned.1.call-start = ((), (), s32[]{:S(2)}) async-start(), calls=%async_computation.16 | async-start | bytes 6488064
  378.8 1.9 copy-start.12
  379.0 1.7 copy-start.13
  394.7 1.6 copy-start.7
  394.7 491.0 %reduce-scatter.12.cloned.1.call-start = ((), (), s32[]{:S(2)}) async-start(), calls=%async_computation.14 | async-start | bytes 8650752 | tf_op jit(solution)/shard_map/reduce_scatter | solution.py:210
  405.5 1.6 copy-start.9
  405.5 627.5 %reduce-scatter.14.cloned.1.call-start = ((), (), s32[]{:S(2)}) async-start(), calls=%async_computation.15 | async-start | bytes 8650752 | tf_op jit(solution)/shard_map/reduce_scatter | solution.py:210
  416.5 1.6 copy-start.10
  436.8 18.6 %all-to-all-start.3 = ((bf16[4,2,65536]{2,1,0:T(2,128)(2,1)}), bf16[4,2,65536]{2,1,0:T(2,128)(2,1)S(1)}, u32[]{:S(2)}, u32[]{:S(2)}) async-start(bf16[4,2,65536]{2,1,0:T(2,128)(2,1)} %reshape.212), calls=%async_computation.3 | async-start | bytes 2097152 | tf_op jit(solution)/shard_map/all_to_all | solution.py:176
  455.4 33.1 %all-to-all-start.1 = ((bf16[4,2,65536]{2,1,0:T(2,128)(2,1)}), bf16[4,2,65536]{2,1,0:T(2,128)(2,1)}, u32[]{:S(2)}, u32[]{:S(2)}) async-start(bf16[4,2,65536]{2,1,0:T(2,128)(2,1)} %reshape.214), calls=%async_computation.1 | async-start | bytes 2097152 | tf_op jit(solution)/shard_map/all_to_all | solution.py:176
  488.5 546.3 %copy-start.1 = (s32[4,32]{1,0:T(4,128)S(1)}, s32[4,32]{1,0:T(4,128)}, u32[]{:S(2)}) copy-start(s32[4,32]{1,0:T(4,128)} %param.9) | copy-start | bytes 1540
Sparse Core Ops, SparseCore 0:
  10.9 84.7 all-gather.5
  98.5 54.0 all-gather.7
  155.6 76.4 all-gather.9
  234.7 76.1 all-gather.11
  351.3 133.0 reduce-scatter.17
  486.6 132.7 reduce-scatter.9
  625.0 110.1 reduce-scatter.15
  737.7 148.0 reduce-scatter.11
  888.1 144.8 reduce-scatter.13

commit v2 on v1

v2 whole, which is shorter than its diff:
```python
import functools

import jax
import jax.numpy as jnp
from jax import lax
from jax.experimental import pallas as pl
from jax.experimental.pallas import tpu as pltpu
from jax.sharding import PartitionSpec as P

HEAD_DIM = 64
ALL = ("dp", "blk", "head")
GROUP = ("blk", "head")
LINES = [[0, 2, 4, 6], [1, 3, 5, 7]]
epsilon = 1e-12


def segments_of(doc_lengths, length):
    doc_ends = jnp.cumsum(doc_lengths, axis=-1, dtype=jnp.int32)
    places = jnp.arange(length, dtype=jnp.int32)
    passed = jnp.sum(
        (doc_ends[..., None, :] <= places[:, None]).astype(jnp.int32), axis=-1, dtype=jnp.int32
    )
    return jnp.where(places < doc_ends[..., -1:], passed + 1, 0)


def run(kernel, operands, after=(), in_specs=(), scalars=0, grid=(1,), out_specs=None, scratch_shapes=(), **rest):
    count = len(operands)

    def body(*refs):
        kernel(*refs[:count], *refs[count + len(after) :])

    specs = list(in_specs) + [pl.BlockSpec(memory_space=pl.ANY)] * len(after)
    spec = pltpu.PrefetchScalarGridSpec(
        num_scalar_prefetch=scalars,
        grid=grid,
        in_specs=specs,
        out_specs=out_specs,
        scratch_shapes=scratch_shapes,
    )
    return pl.pallas_call(body, grid_spec=spec, **rest)(*operands, *after)


MIB = 2**20
NO_COST = pl.CostEstimate(flops=1, bytes_accessed=1, transcendentals=0)
LAST = (((1,), (1,)), ((), ()))
FIRST = (((0,), (0,)), ((), ()))


def grant(mib):
    return pltpu.CompilerParams(vmem_limit_bytes=mib * MIB)


def dot(left, right, form=(((1,), (0,)), ((), ()))):
    return lax.dot_general(left, right, form, preferred_element_type=jnp.float32)


def whole(shape):
    return pl.BlockSpec(shape, lambda *_: (0,) * len(shape))


HBM = pl.BlockSpec(memory_space=pltpu.HBM)
SCALARS = pl.BlockSpec(memory_space=pltpu.SMEM)


def attn_fwd_kernel(q_ref, k_ref, v_ref, segc_ref, segr_ref, out_ref, lse_ref):
    length = q_ref.shape[0]
    scaled = q_ref[...] * jnp.bfloat16(HEAD_DIM ** (-0.5))
    key_pair = k_ref[...]
    value_t = v_ref[...].T
    lanes = lax.broadcasted_iota(jnp.int32, key_pair.shape, 1)
    allowed = segc_ref[...] == segr_ref[...]
    parts = []
    for h in range(2):
        own = (lanes >= h * HEAD_DIM) & (lanes < (h + 1) * HEAD_DIM)
        keys = jnp.where(own, key_pair, jnp.zeros_like(key_pair))
        scores = lax.dot_general(
            keys, scaled, (((1,), (1,)), ((), ())), preferred_element_type=jnp.float32
        )
        scores = jnp.where(allowed, scores, -1e30)
        largest = jnp.max(scores, axis=0, keepdims=True)
        powers = jnp.exp(scores - largest)
        totals = jnp.sum(powers, axis=0, keepdims=True)
        probs = (powers * (1.0 / totals)).astype(jnp.bfloat16)
        parts.append(
            jnp.dot(
                value_t[h * HEAD_DIM : (h + 1) * HEAD_DIM], probs, preferred_element_type=jnp.float32
            )
        )
        lse_ref[0, h : h + 1, :] = largest + jnp.log(totals)
    live = (segc_ref[...] != 0).astype(jnp.float32)
    context = jnp.concatenate(parts, axis=0).T * live
    out_ref[...] = context.astype(jnp.bfloat16)


def attn_bwd_kernel(
    q_ref, k_ref, v_ref, g_ref, segc_ref, segr_ref, lse_ref, *refs
):
    out_ref = refs[-1]
    scaled = q_ref[...] * jnp.bfloat16(HEAD_DIM ** (-0.5))
    key_pair = k_ref[...]
    value_pair = v_ref[...]
    key_t = key_pair.T
    grads = jnp.where(segc_ref[...] != 0, g_ref[...], jnp.zeros_like(g_ref[...]))
    lanes = lax.broadcasted_iota(jnp.int32, key_pair.shape, 1)
    allowed = segc_ref[...] == segr_ref[...]
    contract = (((1,), (1,)), ((), ()))
    dq_parts = []
    dk = None
    dv = None
    for h in range(2):
        own = (lanes >= h * HEAD_DIM) & (lanes < (h + 1) * HEAD_DIM)
        zero = jnp.zeros_like(key_pair)
        keys = jnp.where(own, key_pair, zero)
        values = jnp.where(own, value_pair, zero)
        queries = jnp.where(own, scaled, zero)
        grad_own = jnp.where(own, grads, zero)
        scores = lax.dot_general(keys, scaled, contract, preferred_element_type=jnp.float32)
        scores = jnp.where(allowed, scores, -1e30)
        probs = jnp.exp(scores - lse_ref[0, h : h + 1, :])
        grad_probs = lax.dot_general(values, grads, contract, preferred_element_type=jnp.float32)
        inner = jnp.sum(probs * grad_probs, axis=0, keepdims=True)
        grad_scores = (probs * (grad_probs - inner)).astype(jnp.bfloat16)
        dv_h = jnp.dot(probs.astype(jnp.bfloat16), grad_own, preferred_element_type=jnp.float32)
        dk_h = jnp.dot(grad_scores, queries, preferred_element_type=jnp.float32)
        dv = dv_h if dv is None else dv + dv_h
        dk = dk_h if dk is None else dk + dk_h
        dq_parts.append(
            jnp.dot(
                key_t[h * HEAD_DIM : (h + 1) * HEAD_DIM],
                grad_scores,
                preferred_element_type=jnp.float32,
            )
        )
    dq = jnp.concatenate(dq_parts, axis=0).T * (HEAD_DIM ** (-0.5))
    out_ref[0] = dq.astype(jnp.bfloat16)
    out_ref[1] = dk.astype(jnp.bfloat16)
    out_ref[2] = dv.astype(jnp.bfloat16)


def attention(projected, seg_col, seg_row, after=()):
    length, width3 = projected.shape
    width = width3 // 3
    pairs = width // (2 * HEAD_DIM)
    lane = 2 * HEAD_DIM
    col = lambda base: pl.BlockSpec((length, lane), lambda i: (0, base * pairs + i))
    return run(
        attn_fwd_kernel,
        (projected, projected, projected, seg_col, seg_row,),
        after,
        grid=(pairs,),
        in_specs=[
            col(0),
            col(1),
            col(2),
            pl.BlockSpec((length, 1), lambda i: (0, 0)),
            pl.BlockSpec((1, length), lambda i: (0, 0)),
        ],
        out_specs=[
            pl.BlockSpec((length, lane), lambda i: (0, i)),
            pl.BlockSpec((1, 2, length), lambda i: (i, 0, 0)),
        ],
        out_shape=[
            jax.ShapeDtypeStruct((length, width3 // 3), jnp.bfloat16),
            jax.ShapeDtypeStruct((pairs, 2, length), jnp.float32),
        ],
        compiler_params=grant(56),
        cost_estimate=NO_COST,
    )


def attention_back(projected, grad_context, seg_col, seg_row, lse, first=0, count=None, into=None, after=()):
    length, width3 = projected.shape
    width = width3 // 3
    pairs = width // (2 * HEAD_DIM)
    count = count or pairs
    lane = 2 * HEAD_DIM
    col = lambda base: pl.BlockSpec((length, lane), lambda i: (0, base * pairs + first + i))
    into = () if into is None else (into,)
    return run(
        attn_bwd_kernel,
        (projected, projected, projected, grad_context, seg_col, seg_row, lse, *into,),
        after,
        grid=(count,),
        in_specs=[
            col(0),
            col(1),
            col(2),
            col(0),
            pl.BlockSpec((length, 1), lambda i: (0, 0)),
            pl.BlockSpec((1, length), lambda i: (0, 0)),
            pl.BlockSpec((1, 2, length), lambda i: (first + i, 0, 0)),
        ]
        + [HBM] * len(into),
        out_specs=pl.BlockSpec((3, length, lane), lambda i: (0, 0, first + i)),
        out_shape=jax.ShapeDtypeStruct((3, length, width), jnp.bfloat16),
        input_output_aliases={7: 0} if into else {},
        compiler_params=grant(20),
        cost_estimate=NO_COST,
    )


def start_slabs(table_ref, sources, full_ref, sem):
    copies = []
    for source in sources:
        outer, inner, rows, _ = source.shape
        for o in range(outer):
            for i in range(inner):
                start = pl.multiple_of(table_ref[len(copies)], rows)
                copies.append(
                    pltpu.make_async_copy(source.at[o, i], full_ref.at[pl.ds(start, rows)], sem)
                )
                copies[-1].start()
    return copies


def project_kernel(count, table_ref, x_ref, *refs):
    sources, (out_ref, norms_ref, kept_ref, full_ref, sem, back_sem) = refs[:count], refs[count:]
    for copy in start_slabs(table_ref, sources, full_ref, sem):
        copy.wait()
    back = pltpu.make_async_copy(full_ref, kept_ref, back_sem)
    back.start()
    norms_ref[...] = full_ref[:, -128:].astype(jnp.float32).T[:8]
    x = x_ref[...]
    step = 512
    for j in range(out_ref.shape[1] // step):
        here = slice(j * step, (j + 1) * step)
        out_ref[:, here] = dot(x, full_ref[:, here]).astype(jnp.bfloat16)
    back.wait()


def project(x, table, buffers, columns, after=()):
    total, full_columns = x.shape[1], buffers[0].shape[3]
    return run(
        functools.partial(project_kernel, len(buffers)),
        (table, x, *buffers,),
        after,
        in_specs=[SCALARS, whole(x.shape)] + [HBM] * len(buffers),
        out_specs=[whole((x.shape[0], columns)), whole((8, total)), HBM],
        out_shape=[
            jax.ShapeDtypeStruct((x.shape[0], columns), jnp.bfloat16),
            jax.ShapeDtypeStruct((8, total), jnp.float32),
            jax.ShapeDtypeStruct((total, full_columns), jnp.bfloat16),
        ],
        grid=(1,),
        scratch_shapes=[
            pltpu.VMEM((total, full_columns), jnp.bfloat16),
            pltpu.SemaphoreType.DMA,
            pltpu.SemaphoreType.DMA,
        ],
        compiler_params=grant(56),
        cost_estimate=NO_COST,
    )


def normalise(hidden):
    average = jnp.mean(hidden, axis=-1, keepdims=True)
    centred = hidden - average
    spread = jnp.mean(centred * centred, axis=-1, keepdims=True)
    scale = lax.rsqrt(spread + epsilon)
    return centred * scale, scale


def norm_back(grad, xhat, scale, gain):
    inner = grad * gain
    return scale * (
        inner
        - jnp.mean(inner, axis=-1, keepdims=True)
        - xhat * jnp.mean(inner * xhat, axis=-1, keepdims=True)
    )


def branch_kernel(context_ref, w_ref, tokens_ref, norm_ref, xhat_ref, scale_ref, low_ref):
    step = 128
    for j in range(context_ref.shape[0] // step):
        here = slice(j * step, (j + 1) * step)
        first_in = tokens_ref[here].astype(jnp.float32) + dot(context_ref[here], w_ref[...])
        xhat, scale = normalise(first_in)
        xhat_ref[here] = xhat
        scale_ref[here] = scale
        low_ref[here] = (xhat * norm_ref[0:1] + norm_ref[1:2]).astype(jnp.bfloat16)


def branch(context, w_first, tokens, norm_rows, after=()):
    rows, width = context.shape
    return run(
        branch_kernel,
        (context, w_first, tokens, norm_rows,),
        after,
        grid=(1,),
        in_specs=[
            whole((rows, width)),
            pl.BlockSpec((width, width), lambda i: (0, 3)),
            whole((rows, width)),
            whole(norm_rows.shape),
        ],
        out_specs=[whole((rows, width)), whole((rows, 1)), whole((rows, width))],
        out_shape=[
            jax.ShapeDtypeStruct((rows, width), jnp.float32),
            jax.ShapeDtypeStruct((rows, 1), jnp.float32),
            jax.ShapeDtypeStruct((rows, width), jnp.bfloat16),
        ],
        compiler_params=grant(56),
        cost_estimate=NO_COST,
    )


def up_kernel(count, table_ref, x_ref, *refs):
    sources, (act_ref, slope_ref, kept_ref, full_ref, sem, back_sem) = refs[:count], refs[count:]
    for copy in start_slabs(table_ref, sources, full_ref, sem):
        copy.wait()
    back = pltpu.make_async_copy(full_ref, kept_ref, back_sem)
    back.start()
    x = x_ref[...]
    step = 256
    for j in range(act_ref.shape[1] // step):
        here = slice(j * step, (j + 1) * step)
        pre = dot(x, full_ref[:, here])
        below = 0.5 + 0.5 * lax.erf(pre * 0.7071067811865476)
        bell = jnp.exp(pre * pre * -0.5) * 0.3989422804014327
        act_ref[:, here] = (pre * below).astype(jnp.bfloat16)
        slope_ref[:, here] = (below + pre * bell).astype(jnp.bfloat16)
    back.wait()


def up_gelu(x, table, buffers, after=()):
    total, columns = x.shape[1], buffers[0].shape[3]
    rows = x.shape[0]
    return run(
        functools.partial(up_kernel, len(buffers)),
        (table, x, *buffers,),
        after,
        in_specs=[SCALARS, whole(x.shape)] + [HBM] * len(buffers),
        out_specs=[whole((rows, columns)), whole((rows, columns)), HBM],
        out_shape=[
            jax.ShapeDtypeStruct((rows, columns), jnp.bfloat16),
            jax.ShapeDtypeStruct((rows, columns), jnp.bfloat16),
            jax.ShapeDtypeStruct((total, columns), jnp.bfloat16),
        ],
        grid=(1,),
        scratch_shapes=[
            pltpu.VMEM((total, columns), jnp.bfloat16),
            pltpu.SemaphoreType.DMA,
            pltpu.SemaphoreType.DMA,
        ],
        compiler_params=grant(56),
        cost_estimate=NO_COST,
    )


def down_kernel(count, table_ref, act_ref, xhat_ref, norm_ref, up_ref, *refs):
    sources = refs[:count]
    out_ref, second_ref, ff_ref, norms_ref, kept_ref, full_ref, sem, back_sem = refs[count:]
    for copy in start_slabs(table_ref, sources, full_ref, sem):
        copy.wait()
    back = pltpu.make_async_copy(full_ref, kept_ref, back_sem)
    back.start()
    gain_sum = shift_sum = 0.0
    step = 128
    for j in range(act_ref.shape[0] // step):
        here = slice(j * step, (j + 1) * step)
        first_out = xhat_ref[here] * norm_ref[0:1] + norm_ref[1:2]
        xhat, scale = normalise(first_out + dot(act_ref[here], full_ref[...]))
        out_ref[here] = (xhat * norm_ref[2:3] + norm_ref[3:4]).astype(jnp.bfloat16)
        upstream = up_ref[here].astype(jnp.float32)
        grad = norm_back(upstream, xhat, scale, norm_ref[2:3])
        second_ref[here] = grad
        ff_ref[here] = grad.astype(jnp.bfloat16)
        gain_sum = gain_sum + jnp.sum(upstream * xhat, axis=0, keepdims=True)
        shift_sum = shift_sum + jnp.sum(upstream, axis=0, keepdims=True)
    norms_ref[0:1] = gain_sum
    norms_ref[1:2] = shift_sum
    back.wait()


def down_norm(act, table, buffers, xhat, norm_rows, upstream, after=()):
    rows, inner = act.shape
    width = xhat.shape[1]
    return run(
        functools.partial(down_kernel, len(buffers)),
        (table, act, xhat, norm_rows, upstream, *buffers,),
        after,
        in_specs=[
            SCALARS,
            whole(act.shape),
            whole(xhat.shape),
            whole(norm_rows.shape),
            whole(upstream.shape),
        ]
        + [HBM] * len(buffers),
        out_specs=[whole((rows, width))] * 3 + [whole((2, width)), HBM],
        out_shape=[
            jax.ShapeDtypeStruct((rows, width), jnp.bfloat16),
            jax.ShapeDtypeStruct((rows, width), jnp.float32),
            jax.ShapeDtypeStruct((rows, width), jnp.bfloat16),
            jax.ShapeDtypeStruct((2, width), jnp.float32),
            jax.ShapeDtypeStruct((inner, width), jnp.bfloat16),
        ],
        grid=(1,),
        scratch_shapes=[
            pltpu.VMEM((inner, width), jnp.bfloat16),
            pltpu.SemaphoreType.DMA,
            pltpu.SemaphoreType.DMA,
        ],
        compiler_params=grant(56),
        cost_estimate=NO_COST,
    )


def share(core, value, kept_ref, sent_ref, columns):
    places, rows, _ = kept_ref.shape
    value = value.astype(jnp.bfloat16).reshape(places, 2, rows, value.shape[1])
    low, high = value[:, 0], value[:, 1]
    kept_ref[:, :, columns] = jnp.where(core == 0, low, high)
    sent_ref[:, :, columns] = jnp.where(core == 0, high, low)


def rows_grad_kernel(core_ref, left_ref, right_ref, *refs):
    kept_ref, sent_ref, turned_ref = refs[-3:]

    @pl.when(pl.program_id(0) == 0)
    def _():
        turned_ref[...] = left_ref[...].T

    right = right_ref[...].reshape(right_ref.shape[-2:])
    share(core_ref[0], dot(turned_ref[...], right), kept_ref, sent_ref, slice(None))


def rows_grad(core, left, right, rows, into=None, after=()):
    tokens, width = left.shape
    places = width // rows // 2
    step = 512
    each = right.shape[-1] // step
    steps = right.size // tokens // step
    if right.ndim == 3:
        block = pl.BlockSpec((1, tokens, step), lambda i: (i // each, 0, i % each))
    else:
        block = pl.BlockSpec((tokens, step), lambda i: (0, i))
    out = pl.BlockSpec((places, rows, step), lambda i: (0, 0, i))
    into = tuple(into) if into else ()
    columns = into[0].shape[2] if into else steps * step
    return run(
        rows_grad_kernel,
        (core, left, right, *into,),
        after,
        grid=(steps,),
        in_specs=[SCALARS, whole((tokens, width)), block] + [HBM] * len(into),
        out_specs=[out, out],
        out_shape=[jax.ShapeDtypeStruct((places, rows, columns), jnp.bfloat16)] * 2,
        input_output_aliases={3: 0, 4: 1} if into else {},
        scratch_shapes=[pltpu.VMEM((width, tokens), jnp.bfloat16)],
        compiler_params=grant(56),
        cost_estimate=NO_COST,
    )


def ffn_back_kernel(
    core_ref,
    act_ref,
    slope_ref,
    w_down_ref,
    w_up_ref,
    grad_ref,
    low_ref,
    second_ref,
    xhat_ref,
    scale_ref,
    norm_ref,
    down_kept_ref,
    down_sent_ref,
    up_kept_ref,
    up_sent_ref,
    in_ref,
    branch_ref,
    norms_ref,
    turned_ref,
    sum_ref,
):
    step = pl.program_id(0)
    core = core_ref[0]

    @pl.when(step == 0)
    def _():
        turned_ref[...] = low_ref[...].T
        sum_ref[...] = second_ref[...]

    grad = grad_ref[...]
    back = dot(grad, w_down_ref[...], LAST) * slope_ref[...].astype(jnp.float32)
    back = back.astype(jnp.bfloat16)
    share(core, dot(act_ref[...].T, grad), down_kept_ref, down_sent_ref, slice(None))
    share(core, dot(turned_ref[...], back), up_kept_ref, up_sent_ref, slice(None))
    sum_ref[...] += dot(back, w_up_ref[...], LAST)

    @pl.when(step == pl.num_programs(0) - 1)
    def _():
        gain_sum = shift_sum = 0.0
        chunk = 128
        for j in range(sum_ref.shape[0] // chunk):
            here = slice(j * chunk, (j + 1) * chunk)
            first, xhat = sum_ref[here], xhat_ref[here]
            back = norm_back(first, xhat, scale_ref[here], norm_ref[0:1])
            in_ref[here] = back
            branch_ref[here] = back.astype(jnp.bfloat16)
            gain_sum = gain_sum + jnp.sum(first * xhat, axis=0, keepdims=True)
            shift_sum = shift_sum + jnp.sum(first, axis=0, keepdims=True)
        norms_ref[0:1] = gain_sum
        norms_ref[1:2] = shift_sum


def ffn_back(core, act, slope, w_down, w_up, grad, low, second, xhat, scale, norm_rows, rows, ff_rows):
    tokens, inner = act.shape
    width = grad.shape[1]
    step = 512
    places = width // rows // 2
    ff_places = inner // ff_rows // 2
    here = step // ff_rows // 2
    columns = pl.BlockSpec((tokens, step), lambda i: (0, i))
    down_out = pl.BlockSpec((here, ff_rows, width), lambda i: (i, 0, 0))
    up_out = pl.BlockSpec((places, rows, step), lambda i: (0, 0, i))
    down_shape = jax.ShapeDtypeStruct((ff_places, ff_rows, width), jnp.bfloat16)
    up_shape = jax.ShapeDtypeStruct((places, rows, inner + width + 128), jnp.bfloat16)
    return run(
        ffn_back_kernel,
        (core, act, slope, w_down, w_up, grad, low, second, xhat, scale, norm_rows),
        grid=(inner // step,),
        in_specs=[
            SCALARS,
            columns,
            columns,
            pl.BlockSpec((step, width), lambda i: (i, 0)),
            pl.BlockSpec((width, step), lambda i: (0, i)),
            whole((tokens, width)),
            whole((tokens, width)),
            whole((tokens, width)),
            whole((tokens, width)),
            whole((tokens, 1)),
            whole(norm_rows.shape),
        ],
        out_specs=[down_out, down_out, up_out, up_out]
        + [whole((tokens, width))] * 2
        + [whole((2, width))],
        out_shape=[
            down_shape,
            down_shape,
            up_shape,
            up_shape,
            jax.ShapeDtypeStruct((tokens, width), jnp.float32),
            jax.ShapeDtypeStruct((tokens, width), jnp.bfloat16),
            jax.ShapeDtypeStruct((2, width), jnp.float32),
        ],
        scratch_shapes=[
            pltpu.VMEM((width, tokens), jnp.bfloat16),
            pltpu.VMEM((tokens, width), jnp.float32),
        ],
        compiler_params=grant(56),
        cost_estimate=NO_COST,
    )


def out_grad_kernel(
    core_ref,
    context_ref,
    grad_ref,
    w_ref,
    one_ref,
    two_ref,
    kept_in,
    sent_in,
    back_ref,
    kept_hbm,
    sent_hbm,
    kept_ref,
    sent_ref,
    sems,
):
    core = core_ref[0]
    width = w_ref.shape[0]
    grad = grad_ref[...]
    turned = context_ref[...].T
    step = 256
    for j in range(width // step):
        here = slice(j * step, (j + 1) * step)
        share(core, dot(turned, grad[:, here]), kept_ref, sent_ref, here)
    norms = jnp.concatenate([one_ref[...], two_ref[...], jnp.zeros((124, width), jnp.float32)], 0)
    share(core, norms.T, kept_ref, sent_ref, slice(width, width + 128))
    last = pl.ds(kept_hbm.shape[2] - width - 128, width + 128)
    copies = [
        pltpu.make_async_copy(kept_ref, kept_hbm.at[:, :, last], sems.at[0]),
        pltpu.make_async_copy(sent_ref, sent_hbm.at[:, :, last], sems.at[1]),
    ]
    for copy in copies:
        copy.start()
    for j in range(width // step):
        here = slice(j * step, (j + 1) * step)
        back_ref[:, here] = dot(grad, w_ref[here], LAST).astype(jnp.bfloat16)
    for copy in copies:
        copy.wait()


def out_grad(core, context, grad, w_first, norms_one, norms_two, kept, sent, after=()):
    tokens, width = context.shape
    part = pltpu.VMEM(kept.shape[:2] + (width + 128,), jnp.bfloat16)
    out = kept.shape
    return run(
        out_grad_kernel,
        (core, context, grad, w_first, norms_one, norms_two, kept, sent),
        after,
        grid=(1,),
        in_specs=[
            SCALARS,
            whole((tokens, width)),
            whole((tokens, width)),
            pl.BlockSpec((width, width), lambda i: (0, 3)),
            whole((2, width)),
            whole((2, width)),
            HBM,
            HBM,
        ],
        out_specs=[whole((tokens, width)), HBM, HBM],
        out_shape=[
            jax.ShapeDtypeStruct((tokens, width), jnp.bfloat16),
            jax.ShapeDtypeStruct(out, jnp.bfloat16),
            jax.ShapeDtypeStruct(out, jnp.bfloat16),
        ],
        input_output_aliases={6: 1, 7: 2},
        scratch_shapes=[part, part, pltpu.SemaphoreType.DMA((2,))],
        compiler_params=grant(56),
        cost_estimate=NO_COST,
    )


def tokens_grad_kernel(grad_ref, w_ref, first_ref, out_ref, sum_ref):
    step = pl.program_id(0)

    @pl.when(step == 0)
    def _():
        sum_ref[...] = first_ref[...]

    sum_ref[...] += dot(grad_ref[0], w_ref[...], LAST)

    @pl.when(step == pl.num_programs(0) - 1)
    def _():
        out_ref[...] = sum_ref[...].astype(jnp.bfloat16)


def tokens_grad(grad_mixed, w_first, first, after=()):
    count, tokens, width = grad_mixed.shape
    return run(
        tokens_grad_kernel,
        (grad_mixed, w_first, first,),
        after,
        grid=(count,),
        in_specs=[
            pl.BlockSpec((1, tokens, width), lambda i: (i, 0, 0)),
            pl.BlockSpec((width, width), lambda i: (0, i)),
            whole((tokens, width)),
        ],
        out_specs=whole((tokens, width)),
        out_shape=jax.ShapeDtypeStruct((tokens, width), jnp.bfloat16),
        scratch_shapes=[pltpu.VMEM((tokens, width), jnp.float32)],
        compiler_params=grant(56),
        cost_estimate=NO_COST,
    )


def fold_kernel(place_ref, kept_ref, came_ref, a_own_ref, a_out_ref, b_own_ref, b_out_ref):
    x, y = place_ref[0], place_ref[1]
    half = a_own_ref.shape[2]
    part = lambda ref, i, j, rows: ref[0, i, j, rows].astype(jnp.float32)
    low, high = pl.ds(0, half), pl.ds(half, half)
    for i in range(2):
        both = lambda a, b, rows: (part(kept_ref, a, b, rows) + part(came_ref, a, b, rows)).astype(
            jnp.bfloat16
        )
        a_own_ref[0, i] = both(i, y, low)
        a_out_ref[0, i] = both(i, 1 - y, low)
        b_own_ref[0, i] = both(x, i, high)
        b_out_ref[0, i] = both(1 - x, i, high)


def fold_plane_kernel(place_ref, *refs):
    for i in range(2):
        own_ref, came_ref = refs[2 * i], refs[2 * i + 1]
        keep_ref, out_ref = refs[4 + 2 * i], refs[5 + 2 * i]
        place = place_ref[i]
        for ref, index in ((keep_ref, place), (out_ref, 1 - place)):
            total = own_ref[0, index].astype(jnp.float32) + came_ref[0, index].astype(jnp.float32)
            ref[0] = total.astype(jnp.bfloat16)


def fold_plane(place, a_own, a_came, b_own, b_came, after=()):
    zs, both, rows, columns = a_own.shape
    block = pl.BlockSpec((1, both, rows, columns), lambda i: (i, 0, 0, 0))
    out = pl.BlockSpec((1, rows, columns), lambda i: (i, 0, 0))
    return run(
        fold_plane_kernel,
        (place, a_own, a_came, b_own, b_came),
        after,
        grid=(zs,),
        in_specs=[SCALARS] + [block] * 4,
        out_specs=[out] * 4,
        out_shape=[jax.ShapeDtypeStruct((zs, rows, columns), jnp.bfloat16)] * 4,
        compiler_params=grant(20),
        cost_estimate=NO_COST,
    )


def fold(place, kept, came, after=()):
    zs, xs, ys, rows, columns = kept.shape
    out = pl.BlockSpec((1, 2, rows // 2, columns), lambda i: (i, 0, 0, 0))
    block = pl.BlockSpec((1, xs, ys, rows, columns), lambda i: (i, 0, 0, 0, 0))
    return run(
        fold_kernel,
        (place, kept, came,),
        after,
        grid=(zs,),
        in_specs=[SCALARS, block, block],
        out_specs=[out] * 4,
        out_shape=[jax.ShapeDtypeStruct((zs, 2, rows // 2, columns), jnp.bfloat16)] * 4,
        compiler_params=grant(20),
        cost_estimate=NO_COST,
    )


def gate(values, after=()):
    return run(
        lambda *refs: None,
        values,
        after,
        in_specs=[pl.BlockSpec(memory_space=pl.ANY)] * len(values),
        out_specs=[pl.BlockSpec(memory_space=pl.ANY)] * len(values),
        out_shape=[jax.ShapeDtypeStruct(v.shape, v.dtype) for v in values],
        input_output_aliases={i: i for i in range(len(values))},
    )


def routes(move):
    pairs = []
    for place in range(32):
        z, x, y, c = place // 8, place // 4 % 2, place // 2 % 2, place % 2
        target = move(z, x, y, c)
        if target is not None:
            tz, tx, ty, tc = target
            pairs.append((place, tz * 8 + tx * 4 + ty * 2 + tc))
    return pairs


ROUTE_X = routes(lambda z, x, y, c: (z, 1 - x, y, c))
ROUTE_Y = routes(lambda z, x, y, c: (z, x, 1 - y, c))
ROUTE_C = routes(lambda z, x, y, c: (z, x, y, 1 - c))


def route_up(low, high):
    return routes(lambda z, x, y, c: (z + 1, x, y, c) if low <= z <= high else None)


def route_down(low, high):
    return routes(lambda z, x, y, c: (z - 1, x, y, c) if low <= z <= high else None)


def send(value, route):
    return lax.ppermute(value, ALL, route)


def coordinates():
    dp = lax.axis_index("dp")
    return dp // 2, dp % 2, lax.axis_index("blk"), lax.axis_index("head")


def line_gather(own, below, above, step):
    if step == 0:
        return send(own, route_up(0, 2)), send(own, route_down(1, 3))
    return send(below, route_up(step, 2)), send(above, route_down(1, 3 - step))


def line_blocks(own, below, above, z):
    blocks = []
    for target in range(4):
        value = own
        for place in range(4):
            if place > target:
                value = jnp.where(z == place, below[place - target - 1], value)
            elif place < target:
                value = jnp.where(z == place, above[target - place - 1], value)
        blocks.append(value)
    return blocks


def line_scatter(blocks, z, step, from_above=None, from_below=None):
    down = pick(blocks, jnp.clip(z - 3 + step, 0, 3), 0)
    up = pick(blocks, jnp.clip(z + 3 - step, 0, 3), 0)
    if step:
        down = sum_of([down, from_above]).astype(jnp.bfloat16)
        up = sum_of([up, from_below]).astype(jnp.bfloat16)
    return down, up


def line_send(down, up, step):
    return send(down, route_down(3 - step, 3)), send(up, route_up(0, step))


def sum_of(values):
    total = None
    for value in values:
        value = value.astype(jnp.float32)
        total = value if total is None else total + value
    return total


def slot_rows(buffers, rows):
    z, x, y, c = coordinates()
    tables = []
    for value, part, axis, dx, dy, dc in buffers:
        js = jnp.arange(value.shape[0])[:, None]
        zs = jnp.arange(4)[None, :]
        sx = (x ^ dx ^ js) if axis == 0 else x ^ dx
        sy = (y ^ dy ^ js) if axis == 1 else y ^ dy
        device = ((zs * 2 + sx) * 2 + sy) * 2 + (c ^ dc)
        tables.append((device * rows + part * (rows // 2)).reshape(-1))
    return jnp.concatenate(tables).astype(jnp.int32)


def pick(value, index, axis):
    return lax.dynamic_index_in_dim(value, index, axis, keepdims=False)


def fold_cores(kept, came, after):
    z, x, y, c = coordinates()
    shape = (4, 2, 2) + kept.shape[1:]
    return fold(jnp.stack([x, y]), kept.reshape(shape), came.reshape(shape), after)


def natural(kept, sent):
    return jnp.stack([kept, sent], axis=1).reshape(-1, kept.shape[2])


def joined_shards(qkv_weight, out_weight, norm_params):
    norm_wide = jnp.pad(norm_params, ((0, 0), (0, 128 - norm_params.shape[1])))
    return jnp.concatenate([qkv_weight, out_weight, norm_wide], axis=1)


def split_up(grad, width):
    inner = grad.shape[1] - width - 128
    last = inner + width
    return grad[:, :inner], grad[:, inner:last], grad[:, last : last + 4]


def buffers_of(a2, ay, b2, bx):
    return [(a2, 0, 0, 0, 0), (ay, 0, 0, 0, 1), (b2, 1, 1, 0, 0), (bx, 1, 1, 1, 0)]


def with_partner(shard, own, partner):
    buffers = [b + (0,) for b in own]
    buffers += [(v,) + b[1:] + (1,) for v, b in zip(partner, own)]
    return slot_rows(buffers, shard.shape[0]), [b[0] for b in buffers]


def body_lines(
    tokens, doc_lengths, qkv_weight, out_weight, up_weight, down_weight, norm_params, out_cotangent
):
    seqs_here, local_len, width = tokens.shape
    full_len = local_len * 4
    z, x, y, c = coordinates()
    place = y * 2 + c
    core = c.reshape(1)
    slab, ff_slab = up_weight.shape[0], down_weight.shape[0]
    exchange = lambda v: lax.all_to_all(v, GROUP, split_axis=0, concat_axis=0, tiled=True)
    to_sequence = lambda v: exchange(v).reshape(full_len, width)
    to_positions = lambda v: exchange(v.reshape(seqs_here, local_len, width))
    own_lengths = lax.dynamic_slice_in_dim(doc_lengths, place, 1, 0)
    seg_row = segments_of(own_lengths, full_len)
    seg_col = seg_row.reshape(full_len, 1)
    first_own, up_own = joined_shards(qkv_weight, out_weight, norm_params), up_weight
    half, ff_half = slab // 2, ff_slab // 2

    fb0, fa0 = line_gather(first_own, None, None, 0)
    ub0, ua0 = line_gather(up_own, None, None, 0)
    both = exchange(jnp.concatenate([tokens, out_cotangent], axis=1))

    fb0, fa0, ub0, ua0, down_a, down_b = gate(
        (fb0, fa0, ub0, ua0, down_weight[:ff_half], down_weight[ff_half:])
    )
    down_ax, down_by = send(down_a, ROUTE_X), send(down_b, ROUTE_Y)
    fb1, fa1 = line_gather(None, fb0, fa0, 1)
    ub1, ua1 = line_gather(None, ub0, ua0, 1)

    fb1, fa1, ub1, ua1, down_ax, down_by = gate(
        (fb1, fa1, ub1, ua1, down_ax, down_by), (both,)
    )
    fb2, fa2 = line_gather(None, fb1, fa1, 2)
    ub2, ua2 = line_gather(None, ub1, ua1, 2)

    blocks = line_blocks(first_own, (fb0, fb1, fb2), (fa0, fa1, fa2), z)
    a, b, down_own = gate(
        (
            jnp.stack([v[:half] for v in blocks]),
            jnp.stack([v[half:] for v in blocks]),
            jnp.stack([down_a, down_ax, down_b, down_by]),
        ),
        (ub2, ua2),
    )
    ax, by = send(a, ROUTE_X), send(b, ROUTE_Y)
    down_line = lax.all_gather(down_own, "dp", axis_index_groups=LINES)
    blocks = line_blocks(up_own, (ub0, ub1, ub2), (ua0, ua1, ua2), z)

    a2, b2, up_a, up_b = gate(
        (
            jnp.stack([a, ax]),
            jnp.stack([b, by]),
            jnp.stack([v[:half] for v in blocks]),
            jnp.stack([v[half:] for v in blocks]),
        )
    )
    ay, bx = send(a2, ROUTE_Y), send(b2, ROUTE_X)
    a2c, b2c = send(a2, ROUTE_C), send(b2, ROUTE_C)
    up_ax, up_by = send(up_a, ROUTE_X), send(up_b, ROUTE_Y)
    rows, upstream = (
        v.reshape(full_len, width) for v in (both[:, :local_len], both[:, local_len:])
    )

    ay, bx, up_a2, up_b2, a2c, b2c, down_line = gate(
        (ay, bx, jnp.stack([up_a, up_ax]), jnp.stack([up_b, up_by]), a2c, b2c, down_line)
    )
    ayc, bxc = send(ay, ROUTE_C), send(bx, ROUTE_C)
    up_ay, up_bx = send(up_a2, ROUTE_Y), send(up_b2, ROUTE_X)
    up_a2c, up_b2c = send(up_a2, ROUTE_C), send(up_b2, ROUTE_C)
    table, buffers = with_partner(
        first_own, buffers_of(a2, ay, b2, bx), (a2c, ayc, b2c, bxc)
    )
    projected, norm_rows, w_first = project(rows, table, buffers, 3 * width)
    context, log_sums = attention(projected, seg_col, seg_row)
    down_line = jnp.swapaxes(down_line, 0, 1)

    up_ay, up_bx, up_a2c, up_b2c, down_a2, down_b2, context = gate(
        (
            up_ay,
            up_bx,
            up_a2c,
            up_b2c,
            down_line[:2],
            down_line[2:],
            context,
        )
    )
    up_ayc, up_bxc = send(up_ay, ROUTE_C), send(up_bx, ROUTE_C)
    down_ay, down_bx = send(down_a2, ROUTE_Y), send(down_b2, ROUTE_X)
    down_a2c, down_b2c = send(down_a2, ROUTE_C), send(down_b2, ROUTE_C)
    xhat, scale, first_low = branch(context, w_first, rows, norm_rows)
    table, buffers = with_partner(
        up_own, buffers_of(up_a2, up_ay, up_b2, up_bx), (up_a2c, up_ayc, up_b2c, up_bxc)
    )
    act, slope, w_up = up_gelu(first_low, table, buffers)

    down_ay, down_bx, down_a2c, down_b2c, act = gate((down_ay, down_bx, down_a2c, down_b2c, act))
    down_ayc, down_bxc = send(down_ay, ROUTE_C), send(down_bx, ROUTE_C)
    table, buffers = with_partner(
        down_weight,
        buffers_of(down_a2, down_ay, down_b2, down_bx),
        (down_a2c, down_ayc, down_b2c, down_bxc),
    )
    result, grad_second, grad_ff, norms_two, w_down = down_norm(
        act, table, buffers, xhat, norm_rows, upstream
    )

    low = lambda *v: sum_of(v).astype(jnp.bfloat16)
    place_xy = jnp.stack([x, y])
    layer_out = to_positions(result)
    down_kept, down_sent, up_kept, up_sent, grad_first_in, grad_branch, norms_one = ffn_back(
        core,
        act,
        slope,
        w_down,
        w_up,
        grad_ff,
        first_low,
        grad_second,
        xhat,
        scale,
        norm_rows,
        slab,
        ff_slab,
    )

    down_sent, grad_branch = gate((down_sent, grad_branch), (layer_out,))
    down_came = send(down_sent, ROUTE_C)
    grad_context, up_kept, up_sent = out_grad(
        core, context, grad_branch, w_first, norms_one, norms_two, up_kept, up_sent
    )

    da_own, da_out, db_own, db_out = fold_cores(down_kept, down_came, (grad_context,))
    da_out, db_out, up_sent, grad_context = gate((da_out, db_out, up_sent, grad_context))
    da_in, db_in = send(da_out, ROUTE_Y), send(db_out, ROUTE_X)
    up_came = send(up_sent, ROUTE_C)
    grad_mixed = attention_back(projected, grad_context, seg_col, seg_row, log_sums)

    ua_own, ua_out, ub_own, ub_out = fold_cores(up_kept, up_came, (grad_mixed, da_in, db_in))
    down_blocks = jnp.concatenate([low(da_own, da_in), low(db_own, db_in)], axis=1)
    ua_out, ub_out, down_blocks, grad_mixed = gate((ua_out, ub_out, down_blocks, grad_mixed))
    ua_in, ub_in = send(ua_out, ROUTE_Y), send(ub_out, ROUTE_X)
    down_sum = lax.psum_scatter(
        down_blocks, "dp", scatter_dimension=0, axis_index_groups=LINES, tiled=False
    )
    last_kept, last_sent = rows_grad(core, rows, grad_mixed, slab)
    grad_tokens = tokens_grad(grad_mixed, w_first, grad_first_in, (last_sent,))

    ua_own, ua_out, ub_own, ub_out = fold_plane(
        place_xy, ua_own, ua_in, ub_own, ub_in, (grad_tokens,)
    )
    ua_out, ub_out, last_sent = gate((ua_out, ub_out, last_sent))
    ua_in2, ub_in2 = send(ua_out, ROUTE_X), send(ub_out, ROUTE_Y)
    last_came = send(last_sent, ROUTE_C)

    la_own, la_out, lb_own, lb_out = fold_cores(last_kept, last_came, (ua_in2, ub_in2))
    up_blocks = jnp.concatenate([low(ua_own, ua_in2), low(ub_own, ub_in2)], axis=1)
    up_blocks, la_out, lb_out, down_sum = gate((up_blocks, la_out, lb_out, down_sum))
    up_sum = lax.psum_scatter(
        up_blocks, "dp", scatter_dimension=0, axis_index_groups=LINES, tiled=False
    )
    la_in, lb_in = send(la_out, ROUTE_Y), send(lb_out, ROUTE_X)
    da_in = send(pick(down_sum[:2], 1 - x, 0), ROUTE_X)
    db_in = send(pick(down_sum[2:], 1 - y, 0), ROUTE_Y)

    la_own, la_out, lb_own, lb_out = fold_plane(
        place_xy, la_own, la_in, lb_own, lb_in, (da_in, db_in)
    )
    la_out, lb_out, grad_tokens = gate((la_out, lb_out, grad_tokens))
    la_in2, lb_in2 = send(la_out, ROUTE_X), send(lb_out, ROUTE_Y)
    grad_down = jnp.concatenate(
        [sum_of([pick(down_sum[:2], x, 0), da_in]), sum_of([pick(down_sum[2:], y, 0), db_in])],
        axis=0,
    )

    last_blocks = jnp.concatenate([low(la_own, la_in2), low(lb_own, lb_in2)], axis=1)
    *goes, grad_tokens = gate((*line_scatter(last_blocks, z, 0), grad_tokens))
    input_grad = to_positions(grad_tokens)
    from_above, from_below = line_send(*goes, 0)

    goes = gate(line_scatter(last_blocks, z, 1, from_above, from_below))
    from_above, from_below = line_send(*goes, 1)

    goes = gate(line_scatter(last_blocks, z, 2, from_above, from_below), (input_grad, up_sum))
    from_above, from_below = line_send(*goes, 2)
    grad_qkv = sum_of([pick(last_blocks, z, 0), from_above, from_below])
    grad_up, grad_out, grad_norm = split_up(up_sum.astype(jnp.float32), width)
    return (
        layer_out,
        input_grad.astype(jnp.float32),
        grad_qkv,
        grad_out,
        grad_up,
        grad_down,
        grad_norm,
    )


def body_any(
    tokens, doc_lengths, qkv_weight, out_weight, up_weight, down_weight, norm_params, out_cotangent
):
    seqs_here, local_len, width = tokens.shape
    ff = up_weight.shape[1]
    full_len = local_len * lax.axis_size("blk") * lax.axis_size("head")
    place = lax.axis_index("blk") * lax.axis_size("head") + lax.axis_index("head")
    core = jnp.zeros((1,), jnp.int32)
    slab, ff_slab = width // 32, ff // 32
    exchange = lambda v: lax.all_to_all(v, GROUP, split_axis=0, concat_axis=0, tiled=True)
    to_sequence = lambda v: exchange(v).reshape(full_len, width)
    to_positions = lambda v: exchange(v.reshape(seqs_here, local_len, width))

    def gather(shard):
        return core, [lax.all_gather(shard, ALL, axis=0, tiled=True)[None, None]]

    def scatter(kept, sent):
        total = lax.psum_scatter(natural(kept, sent), ALL, scatter_dimension=0, tiled=True)
        return total.astype(jnp.float32)

    rows = to_sequence(tokens)
    upstream = to_sequence(out_cotangent)
    own_lengths = lax.dynamic_slice_in_dim(doc_lengths, place, 1, 0)
    seg_row = segments_of(own_lengths, full_len)
    seg_col = seg_row.reshape(full_len, 1)
    first_slots = gather(joined_shards(qkv_weight, out_weight, norm_params))
    projected, norm_rows, w_first = project(rows, *first_slots, 3 * width)
    context, log_sums = attention(projected, seg_col, seg_row)
    xhat, scale, first_low = branch(context, w_first, rows, norm_rows)
    act, slope, w_up = up_gelu(first_low, *gather(up_weight))
    result, grad_second, grad_ff, norms_two, w_down = down_norm(
        act, *gather(down_weight), xhat, norm_rows, upstream
    )
    down_kept, down_sent, up_kept, up_sent, grad_first_in, grad_branch, norms_one = ffn_back(
        core,
        act,
        slope,
        w_down,
        w_up,
        grad_ff,
        first_low,
        grad_second,
        xhat,
        scale,
        norm_rows,
        slab,
        ff_slab,
    )
    grad_down = scatter(down_kept, down_sent)
    grad_context, up_kept, up_sent = out_grad(
        core, context, grad_branch, w_first, norms_one, norms_two, up_kept, up_sent
    )
    grad_up, grad_out, grad_norm = split_up(scatter(up_kept, up_sent), width)
    grad_mixed = attention_back(projected, grad_context, seg_col, seg_row, log_sums)
    grad_qkv = scatter(*rows_grad(core, rows, grad_mixed, slab))
    grad_tokens = tokens_grad(grad_mixed, w_first, grad_first_in)
    return (
        to_positions(result),
        to_positions(grad_tokens).astype(jnp.float32),
        grad_qkv,
        grad_out,
        grad_up,
        grad_down,
        grad_norm,
    )


def solution(mesh):
    sizes = tuple(mesh.shape[name] for name in ALL)
    body = body_lines if sizes == (8, 2, 2) else body_any
    placed = (
        P("dp", ("blk", "head"), None),
        P("dp", None),
        P(("dp", "blk", "head"), None),
        P(("dp", "blk", "head"), None),
        P(("dp", "blk", "head"), None),
        P(("dp", "blk", "head"), None),
        P(("dp", "blk", "head"), None),
        P("dp", ("blk", "head"), None),
    )
    return jax.shard_map(
        body,
        mesh=mesh,
        in_specs=placed,
        out_specs=(
            P("dp", ("blk", "head"), None),
            P("dp", ("blk", "head"), None),
            P(("dp", "blk", "head"), None),
            P(("dp", "blk", "head"), None),
            P(("dp", "blk", "head"), None),
            P(("dp", "blk", "head"), None),
            P(("dp", "blk", "head"), None),
        ),
        check_vma=False,
    )
```

time: 1050 us -> 450 us (0.43)
  waiting for transfers between devices: 752 us -> 134 us
  matrix products: 111 us -> 0 us
  Pallas kernels: 31.7 us -> 141 us
  starting transfers between devices: 16.2 us -> 75.7 us
  blocking collectives: 48.9 us -> 0 us
    reduce_scatter x3 -> x2, waiting for transfers between devices: 421 us -> 0.01 us  [the longest x1 0.01 us: body_lines(): lax.psum_scatter(down_blocks, 'dp', scatter_dimension=0, axis_index_group...]
    all_gather x4 -> x1, waiting for transfers between devices: 174 us -> 0.02 us  [body_lines(): down_line = lax.all_gather(down_own, 'dp', axis_index_groups=LINES)]
    unnamed x11 -> x3, waiting for transfers between devices: 142 us -> 0.05 us
    ppermute x0 -> x57, waiting for transfers between devices: none -> 125 us  [send(): return lax.ppermute(value, ALL, route)]
    dot_general x12 -> x0, matrix products: 111 us -> none  [the longest x1 27.1 us: body(): pre_act = jnp.dot(first_low, wup, preferred_element_type=jnp.float32)]
    pallas_call x2 -> x31, Pallas kernels: 31.7 us -> 141 us  [run(): return pl.pallas_call(body, grid_spec=spec, **rest)(*operands, *after)]
    ppermute x0 -> x57, starting transfers between devices: none -> 64.2 us  [send(): return lax.ppermute(value, ALL, route)]
    all_gather x1 -> x0, blocking collectives: 48.9 us -> none  [body(): gather = lambda w: lax.all_gather(w, ALL, axis=0, tiled=True)]
  transfers between devices with their start and end apart: 13 -> 63, of which waited for: 10 -> 28; matrix products, arithmetic and copies ran while one was open for 12% -> 9% of each run, Pallas kernels for 3% -> 27%
where the time goes in v2:
time: 450 us; the launch traced here: 442 us
  Pallas kernels  141 us (31%)
  waiting for transfers between devices  134 us (30%)
  starting transfers between devices  75.7 us (17%)
  local copies, waits for them, and re-layouts  46 us (10%)
  other arithmetic  30.2 us (7%)
  between operations  15.2 us (3%)
    pallas_call x31, Pallas kernels, run(): return pl.pallas_call(body, grid_spec=spec, **rest)(*operands, *after)  141 us
    ppermute x57, waiting for transfers between devices, send(): return lax.ppermute(value, ALL, route)  125 us
    ppermute x57, starting transfers between devices, send(): return lax.ppermute(value, ALL, route)  64.2 us
    unnamed x163, local copies, waits for them, and re-layouts  33.6 us
    all_to_all x3, starting transfers between devices, body_lines(): lax.all_to_all(v, GROUP, split_axis=0, concat_axis=0, tiled=True)  11.4 us
    all_to_all x3, waiting for transfers between devices, body_lines(): lax.all_to_all(v, GROUP, split_axis=0, concat_axis=0, tiled=True)  9.32 us
  transfers between devices with their start and end apart: 63, of which 28 were waited for; matrix products, arithmetic and copies ran while one was open for 9% of the time, Pallas kernels for 27%

profile of v2, /device:TPU:0, one launch (start us, length us, event | category | flops | bytes accessed | tf_op | source)
XLA Modules:
  0.0 441.7 jit_solution(14275149014817856758)
XLA Ops:
  10.2 4.4 all-to-all-start
  14.7 4.4 collective-permute-start
  20.4 4.6 %collective-permute-start.2 = (bf16[32,4096]{1,0:T(8,128)(2,1)}, bf16[32,4096]{1,0:T(8,128)(2,1)S(1)}, u32[]{:S(2)}, u32[]{:S(2)}) collective-permute-start(bf16[32,4096]{1,0:T(8,128)(2,1)} %param.12), channel_id=1, source_target_pairs={{0,8},{1,9},{2,10},{3,11},{4,12},{5,13},{6,14},{7,15},{8,16},{9,17... | collective-permute-start | bytes 786440 | tf_op jit(solution)/shard_map/ppermute | solution.py:761
  31.1 4.0 collective-permute-done.3.refs_3_
  45.7 3.5 collective-permute-done.9.refs_5_
  49.2 4.6 %collective-permute-done.7.refs_3_ = bf16[32,4096]{1,0:T(8,128)(2,1)S(1)} collective-permute-done((bf16[32,4096]{1,0:T(8,128)(2,1)}, bf16[32,4096]{1,0:T(8,128)(2,1)S(1)}, u32[]{:S(2)}, u32[]{:S(2)}) %collective-permute-start.7) | collective-permute-done | bytes 262176 | tf_op jit(solution)/shard_map/ppermute | solution.py:761
  62.5 5.5 %collective-permute-done.13.refs_4_ = bf16[32,4096]{1,0:T(8,128)(2,1)S(1)} collective-permute-done((bf16[32,4096]{1,0:T(8,128)(2,1)}, bf16[32,4096]{1,0:T(8,128)(2,1)S(1)}, u32[]{:S(2)}, u32[]{:S(2)}) %collective-permute-start.13) | collective-permute-done | bytes 262176 | tf_op jit(solution)/shard_map/ppermute | solution.py:761
  75.9 7.3 %collective-permute-done.15 = bf16[4,16,4224]{2,1,0:T(8,128)(2,1)S(1)} collective-permute-done((bf16[4,16,4224]{2,1,0:T(8,128)(2,1)}, bf16[4,16,4224]{2,1,0:T(8,128)(2,1)S(1)}, u32[]{:S(2)}, u32[]{:S(2)}) %collective-permute-start.15) | collective-permute-done | bytes 540704 | tf_op jit(solution)/shard_map/ppermute | solution.py:761
  89.0 12.1 %collective-permute-done.19 = bf16[4,16,4096]{2,1,0:T(8,128)(2,1)} collective-permute-done((bf16[4,16,4096]{2,1,0:T(8,128)(2,1)}, bf16[4,16,4096]{2,1,0:T(8,128)(2,1)}, u32[]{:S(2)}, u32[]{:S(2)}) %collective-permute-start.19) | collective-permute-done | bytes 524320 | tf_op jit(solution)/shard_map/ppermute | solution.py:761
  104.2 15.4 %collective-permute-done.18 = bf16[4,16,4096]{2,1,0:T(8,128)(2,1)} collective-permute-done((bf16[4,16,4096]{2,1,0:T(8,128)(2,1)}, bf16[4,16,4096]{2,1,0:T(8,128)(2,1)}, u32[]{:S(2)}, u32[]{:S(2)}) %collective-permute-start.18) | collective-permute-done | bytes 524320 | tf_op jit(solution)/shard_map/ppermute | solution.py:761
  134.9 10.0 %shard_map.140 = (bf16[512,3072]{1,0:T(8,128)(2,1)}, f32[8,1024]{1,0:T(8,128)}, bf16[1024,4224]{1,0:T(8,128)(2,1)}) custom-call(s32[64]{0:T(128)} %concatenate.28.refs_0_, bf16[512,1024]{1,0:T(8,128)(2,1)} %bitcast.112, bf16[2,4,16,4224]{3,2,1,0:T(8,128)(2,1)} %get-tuple-element.134.refs_2_, bf16[2,4,16,4224]{3,2,1,0:T(8,128)(2,1)} %get-tuple-element.142.refs_3_, ...), custom_call_target="tpu_custom_call" | custom-call | flops 1 | bytes 1 | tf_op jit(solution)/shard_map/pallas_call | solution.py:40
  144.9 13.5 %shard_map.141 = (bf16[512,1024]{1,0:T(8,128)(2,1)}, f32[8,2,512]{2,1,0:T(2,128)}) custom-call(bf16[512,3072]{1,0:T(8,128)(2,1)} %get-tuple-element.146.refs_0_.refs_1_.refs_2_, bf16[512,3072]{1,0:T(8,128)(2,1)} %get-tuple-element.146.refs_0_.refs_1_.refs_2_, bf16[512,3072]{1,0:T(8,128)(2,1)} %get-tuple-element.146.refs_0_.refs_1_.refs_2_, ...), custom_call_target="tpu_custom_call" | custom-call | flops 1 | bytes 1 | tf_op jit(solution)/shard_map/pallas_call | solution.py:40
  162.6 5.7 %shard_map.143 = (f32[512,1024]{1,0:T(8,128)}, f32[512,1]{1,0:T(8,128)}, bf16[512,1024]{1,0:T(8,128)(2,1)}) custom-call(bf16[512,1024]{1,0:T(8,128)(2,1)} %get-tuple-element.150.refs_0_.refs_1_, bf16[1024,4224]{1,0:T(8,128)(2,1)} %get-tuple-element.151.refs_1_.refs_3_, bf16[512,1024]{1,0:T(8,128)(2,1)} %bitcast.113, ...), custom_call_target="tpu_custom_call" | custom-call | flops 1 | bytes 1 | tf_op jit(solution)/shard_map/pallas_call | solution.py:40
  169.3 14.9 %shard_map.144 = (bf16[512,4096]{1,0:T(8,128)(2,1)}, bf16[512,4096]{1,0:T(8,128)(2,1)}, bf16[1024,4096]{1,0:T(8,128)(2,1)}) custom-call(s32[64]{0:T(128)} %concatenate.28.refs_0_, bf16[512,1024]{1,0:T(8,128)(2,1)} %get-tuple-element.153.refs_1_.refs_6_, bf16[2,4,16,4096]{3,2,1,0:T(8,128)(2,1)} %get-tuple-element.139.refs_2_, ...), custom_call_target="tpu_custom_call" | custom-call | flops 1 | bytes 1 | tf_op jit(solution)/shard_map/pallas_call | solution.py:40
  192.7 14.6 %shard_map.146 = (bf16[512,1024]{1,0:T(8,128)(2,1)}, f32[512,1024]{1,0:T(8,128)}, bf16[512,1024]{1,0:T(8,128)(2,1)}, f32[2,1024]{1,0:T(2,128)}, bf16[4096,1024]{1,0:T(8,128)(2,1)}) custom-call(s32[64]{0:T(128)} %concatenate.25.refs_0_, bf16[512,4096]{1,0:T(8,128)(2,1)} %get-tuple-element.159.refs_1_, f32[512,1024]{1,0:T(8,128)} %get-tuple-element.160.refs_2_.refs_8_, ...), custom_call_target="tpu_custom_call" | custom-call | flops 1 | bytes 1 | tf_op jit(solution)/shard_map/pallas_call | solution.py:40
  207.4 3.5 all-to-all-start.1
  210.9 27.9 %shard_map.147 = (bf16[16,128,1024]{2,1,0:T(8,128)(2,1)}, bf16[16,128,1024]{2,1,0:T(8,128)(2,1)}, bf16[16,32,5248]{2,1,0:T(8,128)(2,1)}, bf16[16,32,5248]{2,1,0:...) custom-call(s32[1]{0:T(128)} %bitcast.39.refs_0_, ...), custom_call_target="tpu_custom_call" | custom-call | flops 1 | bytes 1 | tf_op jit(solution)/shard_map/pallas_call | solution.py:40
  240.3 7.1 %shard_map.149 = (bf16[512,1024]{1,0:T(8,128)(2,1)}, bf16[16,32,5248]{2,1,0:T(8,128)(2,1)}, bf16[16,32,5248]{2,1,0:T(8,128)(2,1)}) custom-call(s32[1]{0:T(128)} %bitcast.39.refs_0_, bf16[512,1024]{1,0:T(8,128)(2,1)} %get-tuple-element.150.refs_0_.refs_1_, ...), custom_call_target="tpu_custom_call", output_to_operand_aliasing={{1}: (6, {}), {2}: (7, {})} | custom-call | flops 1 | bytes 1 | tf_op jit(solution)/shard_map/pallas_call | solution.py:40
  248.7 3.4 shard_map.150
  260.9 19.3 %shard_map.152.refs_3_ = bf16[3,512,1024]{2,1,0:T(8,128)(2,1)S(1)} custom-call(bf16[512,3072]{1,0:T(8,128)(2,1)S(1)} %copy-done.2, bf16[512,3072]{1,0:T(8,128)(2,1)S(1)} %copy-done.2, bf16[512,3072]{1,0:T(8,128)(2,1)S(1)} %copy-done.2, bf16[512,1024]{1,0:T(8,128)(2,1)S(1)} %copy-done.6, s32[512,1]{1,0:T(8,128)S(1)} %copy-done.9, s32[1,512]{1,0:T(1,128)S(1)} %copy-done.31, ...), custom_call_target="tpu_custom_call" | custom-call | flops 1 | bytes 1 | tf_op jit(solution)/shard_map/pallas_call | solution.py:40
  294.2 8.8 %shard_map.155 = (bf16[16,32,3072]{2,1,0:T(8,128)(2,1)}, bf16[16,32,3072]{2,1,0:T(8,128)(2,1)}) custom-call(s32[1]{0:T(128)} %bitcast.39.refs_0_, bf16[512,1024]{1,0:T(8,128)(2,1)} %bitcast.114, bf16[3,512,1024]{2,1,0:T(8,128)(2,1)} %get-tuple-element.195.refs_2_.refs_0_), custom_call_target="tpu_custom_call" | custom-call | flops 1 | bytes 1 | tf_op jit(solution)/shard_map/pallas_call | solution.py:40
  303.1 8.3 %shard_map.156.refs_5_.refs_2_ = bf16[512,1024]{1,0:T(8,128)(2,1)} custom-call(bf16[3,512,1024]{2,1,0:T(8,128)(2,1)} %get-tuple-element.195.refs_2_.refs_0_, bf16[1024,4224]{1,0:T(8,128)(2,1)} %get-tuple-element.151.refs_1_.refs_3_, f32[512,1024]{1,0:T(8,128)} %get-tuple-element.201.refs_2_, bf16[16,32,3072]{2,1,0:T(8,128)(2,1)} %get-tuple-element.202.refs_3_.refs_2_), custom_call_target="tpu_custom_call" | custom-call | flops 1 | bytes 1 | tf_op jit(solution)/shard_map/pallas_call | solution.py:40
  311.4 11.4 %collective-permute-done.40.refs_2_ = bf16[4,2,16,5248]{3,2,1,0:T(8,128)(2,1)} collective-permute-done((bf16[4,2,16,5248]{3,2,1,0:T(8,128)(2,1)}, bf16[4,2,16,5248]{3,2,1,0:T(8,128)(2,1)}, u32[]{:S(2)}, u32[]{:S(2)}) %collective-permute-start.40) | collective-permute-done | bytes 1343520 | tf_op jit(solution)/shard_map/ppermute | solution.py:761
  331.4 13.0 %collective-permute-done.43.refs_3_ = bf16[4,16,5248]{2,1,0:T(8,128)(2,1)S(1)} collective-permute-done((bf16[4,16,5248]{2,1,0:T(8,128)(2,1)}, bf16[4,16,5248]{2,1,0:T(8,128)(2,1)S(1)}, u32[]{:S(2)}, u32[]{:S(2)}) %collective-permute-start.43) | collective-permute-done | bytes 671776 | tf_op jit(solution)/shard_map/ppermute | solution.py:761
  357.1 13.6 %collective-permute-done.47.refs_5_ = bf16[64,1024]{1,0:T(8,128)(2,1)S(1)} collective-permute-done((bf16[64,1024]{1,0:T(8,128)(2,1)S(1)}, bf16[64,1024]{1,0:T(8,128)(2,1)S(1)}, u32[]{:S(2)}, u32[]{:S(2)}) %collective-permute-start.47) | collective-permute-done | bytes 131104 | tf_op jit(solution)/shard_map/ppermute | solution.py:761
  377.2 5.5 %collective-permute-done.50 = bf16[4,16,3072]{2,1,0:T(8,128)(2,1)S(1)} collective-permute-done((bf16[4,16,3072]{2,1,0:T(8,128)(2,1)}, bf16[4,16,3072]{2,1,0:T(8,128)(2,1)S(1)}, u32[]{:S(2)}, u32[]{:S(2)}) %collective-permute-start.50) | collective-permute-done | bytes 393248 | tf_op jit(solution)/shard_map/ppermute | solution.py:761
  387.9 7.6 %collective-permute-done.52 = bf16[32,3072]{1,0:T(8,128)(2,1)S(1)} collective-permute-done((bf16[32,3072]{1,0:T(8,128)(2,1)}, bf16[32,3072]{1,0:T(8,128)(2,1)S(1)}, u32[]{:S(2)}, u32[]{:S(2)}) %collective-permute-start.52) | collective-permute-done | bytes 196640 | tf_op jit(solution)/shard_map/ppermute | solution.py:761
  397.0 4.9 %collective-permute-start.54 = (bf16[32,3072]{1,0:T(8,128)(2,1)}, bf16[32,3072]{1,0:T(8,128)(2,1)S(1)}, u32[]{:S(2)}, u32[]{:S(2)}) collective-permute-start(bf16[32,3072]{1,0:T(8,128)(2,1)} %get-tuple-element.229), channel_id=1, source_target_pairs={{0,8},{1,9},{2,10},{3,11},{4,12},{5,13},{6,14},{7,15},{8,16},{9,17... | collective-permute-start | bytes 589832 | tf_op jit(solution)/shard_map/ppermute | solution.py:761
  401.9 3.5 all-to-all-start.2
  406.3 3.4 collective-permute-done.54
  410.6 9.3 %all-to-all-done.2.refs_2_ = bf16[4,128,1024]{2,1,0:T(8,128)(2,1)S(1)} async-done(((bf16[4,128,1024]{2,1,0:T(8,128)(2,1)}), bf16[4,128,1024]{2,1,0:T(8,128)(2,1)S(1)}, u32[]{:S(2)}, u32[]{:S(2)}) %all-to-all-start.2) | async-done | bytes 1048608 | tf_op jit(solution)/shard_map/all_to_all | solution.py:866
  423.0 5.7 %collective-permute-start.56 = (bf16[32,3072]{1,0:T(8,128)(2,1)}, bf16[32,3072]{1,0:T(8,128)(2,1)S(1)}, u32[]{:S(2)}, u32[]{:S(2)}) collective-permute-start(bf16[32,3072]{1,0:T(8,128)(2,1)} %get-tuple-element.232), channel_id=1, source_target_pairs={{0,8},{1,9},{2,10},{3,11},{4,12},{5,13},{6,14},{7,15},{8,16},{9,17... | collective-permute-start | bytes 589832 | tf_op jit(solution)/shard_map/ppermute | solution.py:761
  (370 shorter events, 145.8 us)
Async XLA Ops:
  10.2 44.3 %all-to-all-start = ((bf16[4,256,1024]{2,1,0:T(8,128)(2,1)}), bf16[4,256,1024]{2,1,0:T(8,128)(2,1)S(1)}, u32[]{:S(2)}, u32[]{:S(2)}) async-start(bf16[4,256,1024]{2,1,0:T(8,128)(2,1)} %pad_maximum_fusion), calls=%async_computation | async-start | bytes 4194304 | tf_op jit(solution)/shard_map/all_to_all | solution.py:866
  14.6 107.1 %all-gather.3.cloned.1.call-start = ((), (), s32[]{:S(2)}) async-start(), calls=%async_computation.7 | async-start | bytes 2621440 | tf_op jit(solution)/shard_map/all_gather | solution.py:902
  14.7 20.4 %collective-permute-start = (bf16[32,4224]{1,0:T(8,128)(2,1)S(1)}, bf16[32,4224]{1,0:T(8,128)(2,1)S(1)}, u32[]{:S(2)}, u32[]{:S(2)}) collective-permute-start(bf16[32,4224]{1,0:T(8,128)(2,1)S(1)} %fusion.6), channel_id=1, source_target_pairs={{0,8},{1,9},{2,10},{3,11},{4,12},{5,13},{6,14},{7,15},{8,16},{9,17... | collective-permute-start | bytes 811016 | tf_op jit(solution)/shard_map/ppermute | solution.py:761
  19.1 16.1 %collective-permute-start.1 = (bf16[32,4224]{1,0:T(8,128)(2,1)S(1)}, bf16[32,4224]{1,0:T(8,128)(2,1)S(1)}, u32[]{:S(2)}, u32[]{:S(2)}) collective-permute-start(bf16[32,4224]{1,0:T(8,128)(2,1)S(1)} %fusion.6), channel_id=1, source_target_pairs={{8,0},{9,1},{10,2},{11,3},{12,4},{13,5},{14,6},{15,7},{16,8},{17,9... | collective-permute-start | bytes 811016 | tf_op jit(solution)/shard_map/ppermute | solution.py:761
  36.1 17.7 %collective-permute-start.5 = (bf16[32,4224]{1,0:T(8,128)(2,1)}, bf16[32,4224]{1,0:T(8,128)(2,1)S(1)}, u32[]{:S(2)}, u32[]{:S(2)}) collective-permute-start(bf16[32,4224]{1,0:T(8,128)(2,1)} %get-tuple-element.121), channel_id=1, source_target_pairs={{8,0},{9,1},{10,2},{11,3},{12,4},{13,5},{14,6},{15,7},{16,8},{17,9... | collective-permute-start | bytes 811016 | tf_op jit(solution)/shard_map/ppermute | solution.py:761
  37.5 17.0 %collective-permute-start.4 = (bf16[32,4224]{1,0:T(8,128)(2,1)}, bf16[32,4224]{1,0:T(8,128)(2,1)S(1)}, u32[]{:S(2)}, u32[]{:S(2)}) collective-permute-start(bf16[32,4224]{1,0:T(8,128)(2,1)} %get-tuple-element.120), channel_id=1, source_target_pairs={{8,16},{9,17},{10,18},{11,19},{12,20},{13,21},{14,22},{15,23},{16,... | collective-permute-start | bytes 811016 | tf_op jit(solution)/shard_map/ppermute | solution.py:761
  87.6 34.1 %collective-permute-start.16 = (bf16[2,4,16,4224]{3,2,1,0:T(8,128)(2,1)}, bf16[2,4,16,4224]{3,2,1,0:T(8,128)(2,1)S(1)}, u32[]{:S(2)}, u32[]{:S(2)}) collective-permute-start(bf16[2,4,16,4224]{3,2,1,0:T(8,128)(2,1)} %get-tuple-element.134.refs_2_), channel_id=1, source_target_pairs={{0,2},{1,3},{2,0},{3,1},{4,6},{5,7},{6,4},{7,5},{8,10},{9,11},{10,... | collective-permute-start | bytes 3244040 | tf_op jit(solution)/shard_map/ppermute | solution.py:761
  88.0 33.7 %collective-permute-start.17 = (bf16[2,4,16,4224]{3,2,1,0:T(8,128)(2,1)}, bf16[2,4,16,4224]{3,2,1,0:T(8,128)(2,1)S(1)}, u32[]{:S(2)}, u32[]{:S(2)}) collective-permute-start(bf16[2,4,16,4224]{3,2,1,0:T(8,128)(2,1)} %get-tuple-element.135.refs_4_), channel_id=1, source_target_pairs={{0,4},{1,5},{2,6},{3,7},{4,0},{5,1},{6,2},{7,3},{8,12},{9,13},{10,... | collective-permute-start | bytes 3244040 | tf_op jit(solution)/shard_map/ppermute | solution.py:761
  88.5 33.2 %collective-permute-start.20 = (bf16[2,4,16,4224]{3,2,1,0:T(8,128)(2,1)}, bf16[2,4,16,4224]{3,2,1,0:T(8,128)(2,1)}, u32[]{:S(2)}, u32[]{:S(2)}) collective-permute-start(bf16[2,4,16,4224]{3,2,1,0:T(8,128)(2,1)} %get-tuple-element.134.refs_2_), channel_id=1, source_target_pairs={{0,1},{1,0},{2,3},{3,2},{4,5},{5,4},{6,7},{7,6},{8,9},{9,8},{10,11... | collective-permute-start | bytes 3244040 | tf_op jit(solution)/shard_map/ppermute | solution.py:761
  88.5 33.2 %collective-permute-start.21 = (bf16[2,4,16,4224]{3,2,1,0:T(8,128)(2,1)}, bf16[2,4,16,4224]{3,2,1,0:T(8,128)(2,1)}, u32[]{:S(2)}, u32[]{:S(2)}) collective-permute-start(bf16[2,4,16,4224]{3,2,1,0:T(8,128)(2,1)} %get-tuple-element.135.refs_4_), channel_id=1, source_target_pairs={{0,1},{1,0},{2,3},{3,2},{4,5},{5,4},{6,7},{7,6},{8,9},{9,8},{10,11... | collective-permute-start | bytes 3244040 | tf_op jit(solution)/shard_map/ppermute | solution.py:761
  101.1 18.4 %collective-permute-start.18 = (bf16[4,16,4096]{2,1,0:T(8,128)(2,1)}, bf16[4,16,4096]{2,1,0:T(8,128)(2,1)}, u32[]{:S(2)}, u32[]{:S(2)}) collective-permute-start(bf16[4,16,4096]{2,1,0:T(8,128)(2,1)} %get-tuple-element.136), channel_id=1, source_target_pairs={{0,4},{1,5},{2,6},{3,7},{4,0},{5,1},{6,2},{7,3},{8,12},{9,13},{10,... | collective-permute-start | bytes 1572872 | tf_op jit(solution)/shard_map/ppermute | solution.py:761
  125.8 32.6 %collective-permute-start.22 = (bf16[2,4,16,4096]{3,2,1,0:T(8,128)(2,1)}, bf16[2,4,16,4096]{3,2,1,0:T(8,128)(2,1)S(1)}, u32[]{:S(2)}, u32[]{:S(2)}) collective-permute-start(bf16[2,4,16,4096]{3,2,1,0:T(8,128)(2,1)} %get-tuple-element.139.refs_2_), channel_id=1, source_target_pairs={{0,2},{1,3},{2,0},{3,1},{4,6},{5,7},{6,4},{7,5},{8,10},{9,11},{10,... | collective-permute-start | bytes 3145736 | tf_op jit(solution)/shard_map/ppermute | solution.py:761
  127.5 30.9 %collective-permute-start.24 = (bf16[2,4,16,4096]{3,2,1,0:T(8,128)(2,1)}, bf16[2,4,16,4096]{3,2,1,0:T(8,128)(2,1)}, u32[]{:S(2)}, u32[]{:S(2)}) collective-permute-start(bf16[2,4,16,4096]{3,2,1,0:T(8,128)(2,1)} %get-tuple-element.139.refs_2_), channel_id=1, source_target_pairs={{0,1},{1,0},{2,3},{3,2},{4,5},{5,4},{6,7},{7,6},{8,9},{9,8},{10,11... | collective-permute-start | bytes 3145736 | tf_op jit(solution)/shard_map/ppermute | solution.py:761
  127.5 30.9 %collective-permute-start.23 = (bf16[2,4,16,4096]{3,2,1,0:T(8,128)(2,1)}, bf16[2,4,16,4096]{3,2,1,0:T(8,128)(2,1)}, u32[]{:S(2)}, u32[]{:S(2)}) collective-permute-start(bf16[2,4,16,4096]{3,2,1,0:T(8,128)(2,1)} %get-tuple-element.140.refs_4_), channel_id=1, source_target_pairs={{0,4},{1,5},{2,6},{3,7},{4,0},{5,1},{6,2},{7,3},{8,12},{9,13},{10,... | collective-permute-start | bytes 3145736 | tf_op jit(solution)/shard_map/ppermute | solution.py:761
  128.1 30.4 %collective-permute-start.25 = (bf16[2,4,16,4096]{3,2,1,0:T(8,128)(2,1)}, bf16[2,4,16,4096]{3,2,1,0:T(8,128)(2,1)}, u32[]{:S(2)}, u32[]{:S(2)}) collective-permute-start(bf16[2,4,16,4096]{3,2,1,0:T(8,128)(2,1)} %get-tuple-element.140.refs_4_), channel_id=1, source_target_pairs={{0,1},{1,0},{2,3},{3,2},{4,5},{5,4},{6,7},{7,6},{8,9},{9,8},{10,11... | collective-permute-start | bytes 3145736 | tf_op jit(solution)/shard_map/ppermute | solution.py:761
  159.9 25.6 %collective-permute-start.28 = (bf16[2,4,64,1024]{3,2,1,0:T(8,128)(2,1)}, bf16[2,4,64,1024]{3,2,1,0:T(8,128)(2,1)S(1)}, u32[]{:S(2)}, u32[]{:S(2)}) collective-permute-start(bf16[2,4,64,1024]{3,2,1,0:T(8,128)(2,1)} %get-tuple-element.148.refs_5_), channel_id=1, source_target_pairs={{0,2},{1,3},{2,0},{3,1},{4,6},{5,7},{6,4},{7,5},{8,10},{9,11},{10,... | collective-permute-start | bytes 3145736 | tf_op jit(solution)/shard_map/ppermute | solution.py:761
  160.2 25.8 %collective-permute-start.30 = (bf16[2,4,64,1024]{3,2,1,0:T(8,128)(2,1)}, bf16[2,4,64,1024]{3,2,1,0:T(8,128)(2,1)S(1)}, u32[]{:S(2)}, u32[]{:S(2)}) collective-permute-start(bf16[2,4,64,1024]{3,2,1,0:T(8,128)(2,1)} %get-tuple-element.148.refs_5_), channel_id=1, source_target_pairs={{0,1},{1,0},{2,3},{3,2},{4,5},{5,4},{6,7},{7,6},{8,9},{9,8},{10,11... | collective-permute-start | bytes 3145736 | tf_op jit(solution)/shard_map/ppermute | solution.py:761
  160.2 25.8 %collective-permute-start.29 = (bf16[2,4,64,1024]{3,2,1,0:T(8,128)(2,1)}, bf16[2,4,64,1024]{3,2,1,0:T(8,128)(2,1)S(1)}, u32[]{:S(2)}, u32[]{:S(2)}) collective-permute-start(bf16[2,4,64,1024]{3,2,1,0:T(8,128)(2,1)} %get-tuple-element.149.refs_7_), channel_id=1, source_target_pairs={{0,4},{1,5},{2,6},{3,7},{4,0},{5,1},{6,2},{7,3},{8,12},{9,13},{10,... | collective-permute-start | bytes 3145736 | tf_op jit(solution)/shard_map/ppermute | solution.py:761
  162.3 23.7 %collective-permute-start.31 = (bf16[2,4,64,1024]{3,2,1,0:T(8,128)(2,1)}, bf16[2,4,64,1024]{3,2,1,0:T(8,128)(2,1)}, u32[]{:S(2)}, u32[]{:S(2)}) collective-permute-start(bf16[2,4,64,1024]{3,2,1,0:T(8,128)(2,1)} %get-tuple-element.149.refs_7_), channel_id=1, source_target_pairs={{0,1},{1,0},{2,3},{3,2},{4,5},{5,4},{6,7},{7,6},{8,9},{9,8},{10,11... | collective-permute-start | bytes 3145736 | tf_op jit(solution)/shard_map/ppermute | solution.py:761
  207.4 31.5 %all-to-all-start.1 = ((bf16[4,128,1024]{2,1,0:T(8,128)(2,1)}), bf16[4,128,1024]{2,1,0:T(8,128)(2,1)S(1)}, u32[]{:S(2)}, u32[]{:S(2)}) async-start(bf16[4,128,1024]{2,1,0:T(8,128)(2,1)} %bitcast.126), calls=%async_computation.1 | async-start | bytes 2097152 | tf_op jit(solution)/shard_map/all_to_all | solution.py:866
  210.9 140.2 %reduce-scatter.3.cloned.1.call-start = ((), (), s32[]{:S(2)}) async-start(), calls=%async_computation.5 | async-start | bytes 2621440 | tf_op jit(solution)/shard_map/reduce_scatter | solution.py:999
  256.0 29.3 %collective-permute-start.37 = (bf16[16,32,5248]{2,1,0:T(8,128)(2,1)}, bf16[16,32,5248]{2,1,0:T(8,128)(2,1)S(1)}, u32[]{:S(2)}, u32[]{:S(2)}) collective-permute-start(bf16[16,32,5248]{2,1,0:T(8,128)(2,1)} %get-tuple-element.186), channel_id=1, source_target_pairs={{0,1},{1,0},{2,3},{3,2},{4,5},{5,4},{6,7},{7,6},{8,9},{9,8},{10,11... | collective-permute-start | bytes 16121864 | tf_op jit(solution)/shard_map/ppermute | solution.py:761
  256.4 25.6 %collective-permute-start.38 = (bf16[4,2,64,1024]{3,2,1,0:T(8,128)(2,1)}, bf16[4,2,64,1024]{3,2,1,0:T(8,128)(2,1)S(1)}, u32[]{:S(2)}, u32[]{:S(2)}) collective-permute-start(bf16[4,2,64,1024]{3,2,1,0:T(8,128)(2,1)} %get-tuple-element.189), channel_id=1, source_target_pairs={{0,2},{1,3},{2,0},{3,1},{4,6},{5,7},{6,4},{7,5},{8,10},{9,11},{10,... | collective-permute-start | bytes 3145736 | tf_op jit(solution)/shard_map/ppermute | solution.py:761
  258.1 25.3 %collective-permute-start.39 = (bf16[4,2,64,1024]{3,2,1,0:T(8,128)(2,1)}, bf16[4,2,64,1024]{3,2,1,0:T(8,128)(2,1)S(1)}, u32[]{:S(2)}, u32[]{:S(2)}) collective-permute-start(bf16[4,2,64,1024]{3,2,1,0:T(8,128)(2,1)} %get-tuple-element.190), channel_id=1, source_target_pairs={{0,4},{1,5},{2,6},{3,7},{4,0},{5,1},{6,2},{7,3},{8,12},{9,13},{10,... | collective-permute-start | bytes 3145736 | tf_op jit(solution)/shard_map/ppermute | solution.py:761
  292.0 30.8 %collective-permute-start.40 = (bf16[4,2,16,5248]{3,2,1,0:T(8,128)(2,1)}, bf16[4,2,16,5248]{3,2,1,0:T(8,128)(2,1)}, u32[]{:S(2)}, u32[]{:S(2)}) collective-permute-start(bf16[4,2,16,5248]{3,2,1,0:T(8,128)(2,1)} %get-tuple-element.198), channel_id=1, source_target_pairs={{0,2},{1,3},{2,0},{3,1},{4,6},{5,7},{6,4},{7,5},{8,10},{9,11},{10,... | collective-permute-start | bytes 4030472 | tf_op jit(solution)/shard_map/ppermute | solution.py:761
  292.7 30.9 %collective-permute-start.41 = (bf16[4,2,16,5248]{3,2,1,0:T(8,128)(2,1)}, bf16[4,2,16,5248]{3,2,1,0:T(8,128)(2,1)}, u32[]{:S(2)}, u32[]{:S(2)}) collective-permute-start(bf16[4,2,16,5248]{3,2,1,0:T(8,128)(2,1)} %get-tuple-element.200), channel_id=1, source_target_pairs={{0,4},{1,5},{2,6},{3,7},{4,0},{5,1},{6,2},{7,3},{8,12},{9,13},{10,... | collective-permute-start | bytes 4030472 | tf_op jit(solution)/shard_map/ppermute | solution.py:761
  294.2 127.4 %reduce-scatter.5.cloned.1.call-start = ((), (), s32[]{:S(2)}) async-start(), calls=%async_computation.6 | async-start | bytes 1679360 | tf_op jit(solution)/shard_map/reduce_scatter | solution.py:1015
  331.4 15.5 %collective-permute-start.42 = (bf16[16,32,3072]{2,1,0:T(8,128)(2,1)}, bf16[16,32,3072]{2,1,0:T(8,128)(2,1)S(1)}, u32[]{:S(2)}, u32[]{:S(2)}) collective-permute-start(bf16[16,32,3072]{2,1,0:T(8,128)(2,1)} %get-tuple-element.205), channel_id=1, source_target_pairs={{0,1},{1,0},{2,3},{3,2},{4,5},{5,4},{6,7},{7,6},{8,9},{9,8},{10,11... | collective-permute-start | bytes 9437192 | tf_op jit(solution)/shard_map/ppermute | solution.py:761
  351.1 19.6 %collective-permute-start.45 = (bf16[4,2,16,3072]{3,2,1,0:T(8,128)(2,1)}, bf16[4,2,16,3072]{3,2,1,0:T(8,128)(2,1)S(1)}, u32[]{:S(2)}, u32[]{:S(2)}) collective-permute-start(bf16[4,2,16,3072]{3,2,1,0:T(8,128)(2,1)} %get-tuple-element.214), channel_id=1, source_target_pairs={{0,2},{1,3},{2,0},{3,1},{4,6},{5,7},{6,4},{7,5},{8,10},{9,11},{10,... | collective-permute-start | bytes 2359304 | tf_op jit(solution)/shard_map/ppermute | solution.py:761
  351.8 18.9 %collective-permute-start.46 = (bf16[4,2,16,3072]{3,2,1,0:T(8,128)(2,1)}, bf16[4,2,16,3072]{3,2,1,0:T(8,128)(2,1)S(1)}, u32[]{:S(2)}, u32[]{:S(2)}) collective-permute-start(bf16[4,2,16,3072]{3,2,1,0:T(8,128)(2,1)} %get-tuple-element.216), channel_id=1, source_target_pairs={{0,4},{1,5},{2,6},{3,7},{4,0},{5,1},{6,2},{7,3},{8,12},{9,13},{10,... | collective-permute-start | bytes 2359304 | tf_op jit(solution)/shard_map/ppermute | solution.py:761
  354.1 16.6 %collective-permute-start.47 = (bf16[64,1024]{1,0:T(8,128)(2,1)S(1)}, bf16[64,1024]{1,0:T(8,128)(2,1)S(1)}, u32[]{:S(2)}, u32[]{:S(2)}) collective-permute-start(bf16[64,1024]{1,0:T(8,128)(2,1)S(1)} %dynamic-slice_bitcast_fusion.1), channel_id=1, source_target_pairs={{0,4},{1,5},{2,6},{3,7},{4,0},{5,1},{6,2},{7,3},{8,12},{9,13},{10,... | collective-permute-start | bytes 393224 | tf_op jit(solution)/shard_map/ppermute | solution.py:761
  401.9 18.0 %all-to-all-start.2 = ((bf16[4,128,1024]{2,1,0:T(8,128)(2,1)}), bf16[4,128,1024]{2,1,0:T(8,128)(2,1)S(1)}, u32[]{:S(2)}, u32[]{:S(2)}) async-start(bf16[4,128,1024]{2,1,0:T(8,128)(2,1)} %bitcast.51), calls=%async_computation.3 | async-start | bytes 2097152 | tf_op jit(solution)/shard_map/all_to_all | solution.py:866
  (111 other events, 779.5 us)
Sparse Core Ops, SparseCore 0:
  74.6 45.1 all-gather.2
  294.3 45.1 reduce-scatter.2
  376.6 40.4 reduce-scatter.4

commit v3 on v2

--- a/solution.py
+++ b/solution.py
@@ -350,44 +350,50 @@
 def down_kernel(count, table_ref, act_ref, xhat_ref, norm_ref, up_ref, *refs):
     sources = refs[:count]
     out_ref, second_ref, ff_ref, norms_ref, kept_ref, full_ref, sem, back_sem = refs[count:]
-    for copy in start_slabs(table_ref, sources, full_ref, sem):
-        copy.wait()
+    step = pl.program_id(0)
     back = pltpu.make_async_copy(full_ref, kept_ref, back_sem)
-    back.start()
-    gain_sum = shift_sum = 0.0
-    step = 128
-    for j in range(act_ref.shape[0] // step):
-        here = slice(j * step, (j + 1) * step)
-        first_out = xhat_ref[here] * norm_ref[0:1] + norm_ref[1:2]
-        xhat, scale = normalise(first_out + dot(act_ref[here], full_ref[...]))
-        out_ref[here] = (xhat * norm_ref[2:3] + norm_ref[3:4]).astype(jnp.bfloat16)
-        upstream = up_ref[here].astype(jnp.float32)
-        grad = norm_back(upstream, xhat, scale, norm_ref[2:3])
-        second_ref[here] = grad
-        ff_ref[here] = grad.astype(jnp.bfloat16)
-        gain_sum = gain_sum + jnp.sum(upstream * xhat, axis=0, keepdims=True)
-        shift_sum = shift_sum + jnp.sum(upstream, axis=0, keepdims=True)
-    norms_ref[0:1] = gain_sum
-    norms_ref[1:2] = shift_sum
-    back.wait()
+
+    @pl.when(step == 0)
+    def _():
+        for copy in start_slabs(table_ref, sources, full_ref, sem):
+            copy.wait()
+        back.start()
+        norms_ref[...] = jnp.zeros_like(norms_ref)
+
+    first_out = xhat_ref[...] * norm_ref[0:1] + norm_ref[1:2]
+    xhat, scale = normalise(first_out + dot(act_ref[...], full_ref[...]))
+    out_ref[...] = (xhat * norm_ref[2:3] + norm_ref[3:4]).astype(jnp.bfloat16)
+    upstream = up_ref[...].astype(jnp.float32)
+    grad = norm_back(upstream, xhat, scale, norm_ref[2:3])
+    second_ref[...] = grad
+    ff_ref[...] = grad.astype(jnp.bfloat16)
+    norms_ref[0:1] += jnp.sum(upstream * xhat, axis=0, keepdims=True)
+    norms_ref[1:2] += jnp.sum(upstream, axis=0, keepdims=True)
+
+    @pl.when(step == pl.num_programs(0) - 1)
+    def _():
+        back.wait()
 
 
 def down_norm(act, table, buffers, xhat, norm_rows, upstream, after=()):
     rows, inner = act.shape
     width = xhat.shape[1]
+    step = 128
+    block = pl.BlockSpec((step, width), lambda i: (i, 0))
     return run(
         functools.partial(down_kernel, len(buffers)),
-        (table, act, xhat, norm_rows, upstream, *buffers,),
-        after,
+        (table, act, xhat, norm_rows, upstream, *buffers),
+        after,
+        grid=(rows // step,),
         in_specs=[
             SCALARS,
-            whole(act.shape),
-            whole(xhat.shape),
+            pl.BlockSpec((step, inner), lambda i: (i, 0)),
+            block,
             whole(norm_rows.shape),
-            whole(upstream.shape),
+            block,
         ]
         + [HBM] * len(buffers),
-        out_specs=[whole((rows, width))] * 3 + [whole((2, width)), HBM],
+        out_specs=[block] * 3 + [whole((2, width)), HBM],
         out_shape=[
             jax.ShapeDtypeStruct((rows, width), jnp.bfloat16),
             jax.ShapeDtypeStruct((rows, width), jnp.float32),
@@ -395,7 +401,6 @@
             jax.ShapeDtypeStruct((2, width), jnp.float32),
             jax.ShapeDtypeStruct((inner, width), jnp.bfloat16),
         ],
-        grid=(1,),
         scratch_shapes=[
             pltpu.VMEM((inner, width), jnp.bfloat16),
             pltpu.SemaphoreType.DMA,
@@ -721,7 +726,7 @@
     )
 
 
-def gate(values, after=()):
+def gate(values, after=(), room=None):
     return run(
         lambda *refs: None,
         values,
@@ -730,6 +735,7 @@
         out_specs=[pl.BlockSpec(memory_space=pl.ANY)] * len(values),
         out_shape=[jax.ShapeDtypeStruct(v.shape, v.dtype) for v in values],
         input_output_aliases={i: i for i in range(len(values))},
+        compiler_params=grant(room) if room else None,
     )
 
 
@@ -749,14 +755,6 @@
 ROUTE_C = routes(lambda z, x, y, c: (z, x, y, 1 - c))
 
 
-def route_up(low, high):
-    return routes(lambda z, x, y, c: (z + 1, x, y, c) if low <= z <= high else None)
-
-
-def route_down(low, high):
-    return routes(lambda z, x, y, c: (z - 1, x, y, c) if low <= z <= high else None)
-
-
 def send(value, route):
     return lax.ppermute(value, ALL, route)
 
@@ -766,36 +764,44 @@
     return dp // 2, dp % 2, lax.axis_index("blk"), lax.axis_index("head")
 
 
-def line_gather(own, below, above, step):
-    if step == 0:
-        return send(own, route_up(0, 2)), send(own, route_down(1, 3))
-    return send(below, route_up(step, 2)), send(above, route_down(1, 3 - step))
-
-
-def line_blocks(own, below, above, z):
-    blocks = []
-    for target in range(4):
-        value = own
-        for place in range(4):
-            if place > target:
-                value = jnp.where(z == place, below[place - target - 1], value)
-            elif place < target:
-                value = jnp.where(z == place, above[target - place - 1], value)
-        blocks.append(value)
-    return blocks
-
-
-def line_scatter(blocks, z, step, from_above=None, from_below=None):
-    down = pick(blocks, jnp.clip(z - 3 + step, 0, 3), 0)
-    up = pick(blocks, jnp.clip(z + 3 - step, 0, 3), 0)
-    if step:
-        down = sum_of([down, from_above]).astype(jnp.bfloat16)
-        up = sum_of([up, from_below]).astype(jnp.bfloat16)
-    return down, up
-
-
-def line_send(down, up, step):
-    return send(down, route_down(3 - step, 3)), send(up, route_up(0, step))
+def copy_kernel(in_ref, out_ref):
+    out_ref[...] = in_ref[...]
+
+
+def copy_after(value, after):
+    return run(
+        copy_kernel,
+        (value,),
+        after,
+        in_specs=[whole(value.shape)],
+        out_specs=whole(value.shape),
+        out_shape=jax.ShapeDtypeStruct(value.shape, value.dtype),
+        cost_estimate=NO_COST,
+    )
+
+
+def side_kernel(left_ref, right_ref, out_ref):
+    middle = left_ref.shape[1]
+    out_ref[:, :middle] = left_ref[...]
+    out_ref[:, middle:] = right_ref[...]
+
+
+def side_by_side(left, right, after):
+    blocks, first, columns = left.shape
+    both = first + right.shape[1]
+    return run(
+        side_kernel,
+        (left, right),
+        after,
+        grid=(blocks,),
+        in_specs=[
+            pl.BlockSpec((1,) + left.shape[1:], lambda i: (i, 0, 0)),
+            pl.BlockSpec((1,) + right.shape[1:], lambda i: (i, 0, 0)),
+        ],
+        out_specs=pl.BlockSpec((1, both, columns), lambda i: (i, 0, 0)),
+        out_shape=jax.ShapeDtypeStruct((blocks, both, columns), left.dtype),
+        cost_estimate=NO_COST,
+    )
 
 
 def sum_of(values):
@@ -841,7 +847,10 @@
 def split_up(grad, width):
     inner = grad.shape[1] - width - 128
     last = inner + width
-    return grad[:, :inner], grad[:, inner:last], grad[:, last : last + 4]
+    return tuple(
+        part.astype(jnp.float32)
+        for part in (grad[:, :inner], grad[:, inner:last], grad[:, last : last + 4])
+    )
 
 
 def buffers_of(a2, ay, b2, bx):
@@ -871,79 +880,53 @@
     seg_col = seg_row.reshape(full_len, 1)
     first_own, up_own = joined_shards(qkv_weight, out_weight, norm_params), up_weight
     half, ff_half = slab // 2, ff_slab // 2
-
-    fb0, fa0 = line_gather(first_own, None, None, 0)
-    ub0, ua0 = line_gather(up_own, None, None, 0)
-    both = exchange(jnp.concatenate([tokens, out_cotangent], axis=1))
-
-    fb0, fa0, ub0, ua0, down_a, down_b = gate(
-        (fb0, fa0, ub0, ua0, down_weight[:ff_half], down_weight[ff_half:])
-    )
+    line = lambda v: lax.all_gather(v, "dp", axis_index_groups=LINES)
+
+    first_line = line(first_own)
+    down_a, down_b = down_weight[:ff_half], down_weight[ff_half:]
     down_ax, down_by = send(down_a, ROUTE_X), send(down_b, ROUTE_Y)
-    fb1, fa1 = line_gather(None, fb0, fa0, 1)
-    ub1, ua1 = line_gather(None, ub0, ua0, 1)
-
-    fb1, fa1, ub1, ua1, down_ax, down_by = gate(
-        (fb1, fa1, ub1, ua1, down_ax, down_by), (both,)
-    )
-    fb2, fa2 = line_gather(None, fb1, fa1, 2)
-    ub2, ua2 = line_gather(None, ub1, ua1, 2)
-
-    blocks = line_blocks(first_own, (fb0, fb1, fb2), (fa0, fa1, fa2), z)
-    a, b, down_own = gate(
-        (
-            jnp.stack([v[:half] for v in blocks]),
-            jnp.stack([v[half:] for v in blocks]),
-            jnp.stack([down_a, down_ax, down_b, down_by]),
-        ),
-        (ub2, ua2),
-    )
+    both = exchange(side_by_side(tokens, out_cotangent, (first_own, down_ax, down_by)))
+    rows, upstream = (
+        v.reshape(full_len, width) for v in (both[:, :local_len], both[:, local_len:])
+    )
+    down_own = jnp.stack([down_a, down_ax, down_b, down_by])
+
+    a, b = gate(
+        (first_line[:, :half], first_line[:, half:]),
+        (down_own, seg_row, seg_col),
+    )
+    up_shard = copy_after(up_own, (a,))
     ax, by = send(a, ROUTE_X), send(b, ROUTE_Y)
-    down_line = lax.all_gather(down_own, "dp", axis_index_groups=LINES)
-    blocks = line_blocks(up_own, (ub0, ub1, ub2), (ua0, ua1, ua2), z)
-
-    a2, b2, up_a, up_b = gate(
-        (
-            jnp.stack([a, ax]),
-            jnp.stack([b, by]),
-            jnp.stack([v[:half] for v in blocks]),
-            jnp.stack([v[half:] for v in blocks]),
-        )
-    )
+    up_line = line(up_shard)
+
+    a2, b2 = gate((jnp.stack([a, ax]), jnp.stack([b, by])), (rows, upstream))
     ay, bx = send(a2, ROUTE_Y), send(b2, ROUTE_X)
     a2c, b2c = send(a2, ROUTE_C), send(b2, ROUTE_C)
+
+    ay, bx, up_a, up_b, down_own, a2c, b2c = gate(
+        (ay, bx, up_line[:, :half], up_line[:, half:], down_own, a2c, b2c)
+    )
+    ayc, bxc = send(ay, ROUTE_C), send(bx, ROUTE_C)
     up_ax, up_by = send(up_a, ROUTE_X), send(up_b, ROUTE_Y)
-    rows, upstream = (
-        v.reshape(full_len, width) for v in (both[:, :local_len], both[:, local_len:])
-    )
-
-    ay, bx, up_a2, up_b2, a2c, b2c, down_line = gate(
-        (ay, bx, jnp.stack([up_a, up_ax]), jnp.stack([up_b, up_by]), a2c, b2c, down_line)
-    )
-    ayc, bxc = send(ay, ROUTE_C), send(bx, ROUTE_C)
+    down_line = line(down_own)
+    table, buffers = with_partner(
+        first_own, buffers_of(a2, ay, b2, bx), (a2c, ayc, b2c, bxc)
+    )
+    projected, norm_rows, w_first = project(rows, table, buffers, 3 * width)
+
+    up_ax, up_by, projected = gate((up_ax, up_by, projected))
+    up_a2, up_b2 = jnp.stack([up_a, up_ax]), jnp.stack([up_b, up_by])
     up_ay, up_bx = send(up_a2, ROUTE_Y), send(up_b2, ROUTE_X)
     up_a2c, up_b2c = send(up_a2, ROUTE_C), send(up_b2, ROUTE_C)
-    table, buffers = with_partner(
-        first_own, buffers_of(a2, ay, b2, bx), (a2c, ayc, b2c, bxc)
-    )
-    projected, norm_rows, w_first = project(rows, table, buffers, 3 * width)
     context, log_sums = attention(projected, seg_col, seg_row)
-    down_line = jnp.swapaxes(down_line, 0, 1)
-
-    up_ay, up_bx, up_a2c, up_b2c, down_a2, down_b2, context = gate(
-        (
-            up_ay,
-            up_bx,
-            up_a2c,
-            up_b2c,
-            down_line[:2],
-            down_line[2:],
-            context,
-        )
-    )
-    up_ayc, up_bxc = send(up_ay, ROUTE_C), send(up_bx, ROUTE_C)
+
+    up_ay, up_bx, up_a2c, up_b2c, down_line, context = gate(
+        (up_ay, up_bx, up_a2c, up_b2c, down_line, context)
+    )
+    down_a2, down_b2 = jnp.swapaxes(down_line[:, :2], 0, 1), jnp.swapaxes(down_line[:, 2:], 0, 1)
     down_ay, down_bx = send(down_a2, ROUTE_Y), send(down_b2, ROUTE_X)
     down_a2c, down_b2c = send(down_a2, ROUTE_C), send(down_b2, ROUTE_C)
+    up_ayc, up_bxc = send(up_ay, ROUTE_C), send(up_bx, ROUTE_C)
     xhat, scale, first_low = branch(context, w_first, rows, norm_rows)
     table, buffers = with_partner(
         up_own, buffers_of(up_a2, up_ay, up_b2, up_bx), (up_a2c, up_ayc, up_b2c, up_bxc)
@@ -987,14 +970,14 @@
     )
 
     da_own, da_out, db_own, db_out = fold_cores(down_kept, down_came, (grad_context,))
-    da_out, db_out, up_sent, grad_context = gate((da_out, db_out, up_sent, grad_context))
+    da_out, db_out, up_sent, grad_context = gate((da_out, db_out, up_sent, grad_context), (), 1)
     da_in, db_in = send(da_out, ROUTE_Y), send(db_out, ROUTE_X)
     up_came = send(up_sent, ROUTE_C)
     grad_mixed = attention_back(projected, grad_context, seg_col, seg_row, log_sums)
 
     ua_own, ua_out, ub_own, ub_out = fold_cores(up_kept, up_came, (grad_mixed, da_in, db_in))
     down_blocks = jnp.concatenate([low(da_own, da_in), low(db_own, db_in)], axis=1)
-    ua_out, ub_out, down_blocks, grad_mixed = gate((ua_out, ub_out, down_blocks, grad_mixed))
+    ua_out, ub_out, down_blocks, grad_mixed = gate((ua_out, ub_out, down_blocks, grad_mixed), (), 1)
     ua_in, ub_in = send(ua_out, ROUTE_Y), send(ub_out, ROUTE_X)
     down_sum = lax.psum_scatter(
         down_blocks, "dp", scatter_dimension=0, axis_index_groups=LINES, tiled=False
@@ -1005,13 +988,13 @@
     ua_own, ua_out, ub_own, ub_out = fold_plane(
         place_xy, ua_own, ua_in, ub_own, ub_in, (grad_tokens,)
     )
-    ua_out, ub_out, last_sent = gate((ua_out, ub_out, last_sent))
+    ua_out, ub_out, last_sent = gate((ua_out, ub_out, last_sent), (), 1)
     ua_in2, ub_in2 = send(ua_out, ROUTE_X), send(ub_out, ROUTE_Y)
     last_came = send(last_sent, ROUTE_C)
 
     la_own, la_out, lb_own, lb_out = fold_cores(last_kept, last_came, (ua_in2, ub_in2))
     up_blocks = jnp.concatenate([low(ua_own, ua_in2), low(ub_own, ub_in2)], axis=1)
-    up_blocks, la_out, lb_out, down_sum = gate((up_blocks, la_out, lb_out, down_sum))
+    up_blocks, la_out, lb_out, down_sum = gate((up_blocks, la_out, lb_out, down_sum), (), 1)
     up_sum = lax.psum_scatter(
         up_blocks, "dp", scatter_dimension=0, axis_index_groups=LINES, tiled=False
     )
@@ -1022,7 +1005,7 @@
     la_own, la_out, lb_own, lb_out = fold_plane(
         place_xy, la_own, la_in, lb_own, lb_in, (da_in, db_in)
     )
-    la_out, lb_out, grad_tokens = gate((la_out, lb_out, grad_tokens))
+    la_out, lb_out, grad_tokens = gate((la_out, lb_out, grad_tokens), (), 1)
     la_in2, lb_in2 = send(la_out, ROUTE_X), send(lb_out, ROUTE_Y)
     grad_down = jnp.concatenate(
         [sum_of([pick(down_sum[:2], x, 0), da_in]), sum_of([pick(down_sum[2:], y, 0), db_in])],
@@ -1030,17 +1013,13 @@
     )
 
     last_blocks = jnp.concatenate([low(la_own, la_in2), low(lb_own, lb_in2)], axis=1)
-    *goes, grad_tokens = gate((*line_scatter(last_blocks, z, 0), grad_tokens))
+    last_blocks, grad_tokens, up_sum = gate((last_blocks, grad_tokens, up_sum), (), 1)
     input_grad = to_positions(grad_tokens)
-    from_above, from_below = line_send(*goes, 0)
-
-    goes = gate(line_scatter(last_blocks, z, 1, from_above, from_below))
-    from_above, from_below = line_send(*goes, 1)
-
-    goes = gate(line_scatter(last_blocks, z, 2, from_above, from_below), (input_grad, up_sum))
-    from_above, from_below = line_send(*goes, 2)
-    grad_qkv = sum_of([pick(last_blocks, z, 0), from_above, from_below])
-    grad_up, grad_out, grad_norm = split_up(up_sum.astype(jnp.float32), width)
+    last_sum = lax.psum_scatter(
+        last_blocks, "dp", scatter_dimension=0, axis_index_groups=LINES, tiled=False
+    )
+    grad_qkv = last_sum.astype(jnp.float32)
+    grad_up, grad_out, grad_norm = split_up(up_sum, width)
     return (
         layer_out,
         input_grad.astype(jnp.float32),

time: 450 us -> 402 us (0.89); the launches traced: 442 us -> 401 us
  starting transfers between devices: 75.7 us -> 45.7 us
  local copies, waits for them, and re-layouts: 46 us -> 33.9 us
  Pallas kernels: 141 us -> 150 us
  other arithmetic: 30.2 us -> 23.7 us
    ppermute x57 -> x39, waiting for transfers between devices: 125 us -> 93.8 us  [send(): return lax.ppermute(value, ALL, route)]
    ppermute x57 -> x39, starting transfers between devices: 64.2 us -> 34.7 us  [send(): return lax.ppermute(value, ALL, route)]
    all_gather x1 -> x3, waiting for transfers between devices: 0.02 us -> 18.4 us  [body_lines(): line = lambda v: lax.all_gather(v, 'dp', axis_index_groups=LINES)]
    unnamed x163 -> x117, local copies, waits for them, and re-layouts: 33.6 us -> 20.5 us
    pallas_call x31 -> x30, Pallas kernels: 141 us -> 150 us  [run(): return pl.pallas_call(body, grid_spec=spec, **rest)(*operands, *after)]
    all_to_all x3, waiting for transfers between devices: 9.32 us -> 16.9 us  [body_lines(): lax.all_to_all(v, GROUP, split_axis=0, concat_axis=0, tiled=True)]
    another operation x8 -> x5, other arithmetic: 11.3 us -> 5.36 us  [the longest x2 3.26 us: body_lines(): a2, b2 = gate((jnp.stack([a, ax]), jnp.stack([b, by])), (rows, upstream))]
  transfers between devices with their start and end apart: 63 -> 48, of which waited for: 28 -> 27; matrix products, arithmetic and copies ran while one was open for 9% -> 9% of each run, Pallas kernels for 27% -> 32%
where the time goes in v3:
time: 402 us; the launch traced here: 401 us
  Pallas kernels  150 us (37%)
  waiting for transfers between devices  132 us (33%)
  starting transfers between devices  45.7 us (11%)
  local copies, waits for them, and re-layouts  33.9 us (8%)
  other arithmetic  23.7 us (6%)
  between operations  14.7 us (4%)
    pallas_call x30, Pallas kernels, run(): return pl.pallas_call(body, grid_spec=spec, **rest)(*operands, *after)  150 us
    ppermute x39, waiting for transfers between devices, send(): return lax.ppermute(value, ALL, route)  93.8 us
    ppermute x39, starting transfers between devices, send(): return lax.ppermute(value, ALL, route)  34.7 us
    unnamed x117, local copies, waits for them, and re-layouts  20.5 us
    all_gather x3, waiting for transfers between devices, body_lines(): line = lambda v: lax.all_gather(v, 'dp', axis_index_groups=LINES)  18.4 us
    all_to_all x3, waiting for transfers between devices, body_lines(): lax.all_to_all(v, GROUP, split_axis=0, concat_axis=0, tiled=True)  16.9 us
    all_to_all x3, starting transfers between devices, body_lines(): lax.all_to_all(v, GROUP, split_axis=0, concat_axis=0, tiled=True)  10.8 us
  transfers between devices with their start and end apart: 48, of which 27 were waited for; matrix products, arithmetic and copies ran while one was open for 9% of the time, Pallas kernels for 32%

profile of v3, /device:TPU:0, one launch (start us, length us, event | category | flops | bytes accessed | tf_op | source)
XLA Modules:
  0.0 400.9 jit_solution(801249081000089154)
XLA Ops:
  10.8 3.0 collective-permute-start
  19.4 3.8 shard_map.136
  23.2 3.7 all-to-all-start
  29.1 12.3 %all-gather.7.cloned.1.call-done = bf16[128,4224]{1,0:T(8,128)(2,1)} async-done(((bf16[32,4224]{1,0:T(8,128)(2,1)}), bf16[128,4224]{1,0:T(8,128)(2,1)}) %all-gather.7.cloned.1.call-update) | async-done | bytes 1081360 | tf_op jit(solution)/shard_map/all_gather | solution.py:883
  48.4 4.7 %all-to-all-done = bf16[4,256,1024]{2,1,0:T(8,128)(2,1)S(1)} async-done(((bf16[4,256,1024]{2,1,0:T(8,128)(2,1)}), bf16[4,256,1024]{2,1,0:T(8,128)(2,1)S(1)}, u32[]{:S(2)}, u32[]{:S(2)}) %all-to-all-start) | async-done | bytes 2097184 | tf_op jit(solution)/shard_map/all_to_all | solution.py:875
  54.7 9.6 %collective-permute-done.3 = bf16[4,16,4224]{2,1,0:T(8,128)(2,1)} collective-permute-done((bf16[4,16,4224]{2,1,0:T(8,128)(2,1)}, bf16[4,16,4224]{2,1,0:T(8,128)(2,1)}, u32[]{:S(2)}, u32[]{:S(2)}) %collective-permute-start.3) | collective-permute-done | bytes 540704 | tf_op jit(solution)/shard_map/ppermute | solution.py:759
  69.4 4.7 %all-gather.9.cloned.1.call-done = bf16[128,4096]{1,0:T(8,128)(2,1)} async-done(((bf16[32,4096]{1,0:T(8,128)(2,1)}), bf16[128,4096]{1,0:T(8,128)(2,1)}) %all-gather.9.cloned.1.call-update) | async-done | bytes 1048592 | tf_op jit(solution)/shard_map/all_gather | solution.py:883
  76.3 16.8 %collective-permute-done.4.refs_0_ = bf16[2,4,16,4224]{3,2,1,0:T(8,128)(2,1)S(1)} collective-permute-done((bf16[2,4,16,4224]{3,2,1,0:T(8,128)(2,1)}, bf16[2,4,16,4224]{3,2,1,0:T(8,128)(2,1)S(1)}, u32[]{:S(2)}, u32[]{:S(2)}) %collective-permute-start.4) | collective-permute-done | bytes 1081376 | tf_op jit(solution)/shard_map/ppermute | solution.py:759
  99.6 10.4 %shard_map.140 = (bf16[512,3072]{1,0:T(8,128)(2,1)}, f32[8,1024]{1,0:T(8,128)}, bf16[1024,4224]{1,0:T(8,128)(2,1)}) custom-call(s32[64]{0:T(128)} %concatenate.24.refs_0_, bf16[512,1024]{1,0:T(8,128)(2,1)} %bitcast.63, bf16[2,4,16,4224]{3,2,1,0:T(8,128)(2,1)} %get-tuple-element.105.refs_2_, bf16[2,4,16,4224]{3,2,1,0:T(8,128)(2,1)} %get-tuple-element.109.refs_3_, ...), custom_call_target="tpu_custom_call" | custom-call | flops 1 | bytes 1 | tf_op jit(solution)/shard_map/pallas_call | solution.py:40
  116.3 13.3 %shard_map.142 = (bf16[512,1024]{1,0:T(8,128)(2,1)}, f32[8,2,512]{2,1,0:T(2,128)}) custom-call(bf16[512,3072]{1,0:T(8,128)(2,1)} %get-tuple-element.117.refs_0_.refs_1_.refs_2_, bf16[512,3072]{1,0:T(8,128)(2,1)} %get-tuple-element.117.refs_0_.refs_1_.refs_2_, bf16[512,3072]{1,0:T(8,128)(2,1)} %get-tuple-element.117.refs_0_.refs_1_.refs_2_, ...), custom_call_target="tpu_custom_call" | custom-call | flops 1 | bytes 1 | tf_op jit(solution)/shard_map/pallas_call | solution.py:40
  129.6 8.8 %collective-permute-done.13.refs_1_ = bf16[2,4,16,4096]{3,2,1,0:T(8,128)(2,1)S(1)} collective-permute-done((bf16[2,4,16,4096]{3,2,1,0:T(8,128)(2,1)S(1)}, bf16[2,4,16,4096]{3,2,1,0:T(8,128)(2,1)S(1)}, u32[]{:S(2)}, u32[]{:S(2)}) %collective-permute-start.13) | collective-permute-done | bytes 1048608 | tf_op jit(solution)/shard_map/ppermute | solution.py:759
  147.2 5.8 %shard_map.144 = (f32[512,1024]{1,0:T(8,128)}, f32[512,1]{1,0:T(8,128)}, bf16[512,1024]{1,0:T(8,128)(2,1)}) custom-call(bf16[512,1024]{1,0:T(8,128)(2,1)} %get-tuple-element.120.refs_0_.refs_1_, bf16[1024,4224]{1,0:T(8,128)(2,1)} %get-tuple-element.121.refs_1_.refs_3_, bf16[512,1024]{1,0:T(8,128)(2,1)} %bitcast.64, f32[8,1024]{1,0:T(8,128)} %get-tuple-element.122.refs_3_.refs_10_), custom_call_target="tpu_custom_call" | custom-call | flops 1 | bytes 1 | tf_op jit(solution)/shard_map/pallas_call | solution.py:40
  153.1 15.0 %shard_map.145 = (bf16[512,4096]{1,0:T(8,128)(2,1)}, bf16[512,4096]{1,0:T(8,128)(2,1)}, bf16[1024,4096]{1,0:T(8,128)(2,1)}) custom-call(s32[64]{0:T(128)} %concatenate.24.refs_0_, bf16[512,1024]{1,0:T(8,128)(2,1)} %get-tuple-element.123.refs_1_.refs_6_, bf16[2,4,16,4096]{3,2,1,0:T(8,128)(2,1)} %copy-done.35, ...), custom_call_target="tpu_custom_call" | custom-call | flops 1 | bytes 1 | tf_op jit(solution)/shard_map/pallas_call | solution.py:40
  178.8 14.2 %shard_map.147 = (bf16[512,1024]{1,0:T(8,128)(2,1)}, f32[512,1024]{1,0:T(8,128)}, bf16[512,1024]{1,0:T(8,128)(2,1)}, f32[2,1024]{1,0:T(2,128)}, bf16[4096,1024]{1,0:T(8,128)(2,1)}) custom-call(s32[64]{0:T(128)} %concatenate.22.refs_0_, bf16[512,4096]{1,0:T(8,128)(2,1)} %get-tuple-element.129.refs_1_, f32[512,1024]{1,0:T(8,128)} %get-tuple-element.130.refs_2_.refs_8_, ...), custom_call_target="tpu_custom_call" | custom-call | flops 1 | bytes 1 | tf_op jit(solution)/shard_map/pallas_call | solution.py:40
  193.0 3.5 all-to-all-start.1
  196.6 28.0 %shard_map.148 = (bf16[16,128,1024]{2,1,0:T(8,128)(2,1)}, bf16[16,128,1024]{2,1,0:T(8,128)(2,1)}, bf16[16,32,5248]{2,1,0:T(8,128)(2,1)}, bf16[16,32,5248]{2,1,0:...) custom-call(s32[1]{0:T(128)} %bitcast.26.refs_0_, ...), custom_call_target="tpu_custom_call" | custom-call | flops 1 | bytes 1 | tf_op jit(solution)/shard_map/pallas_call | solution.py:40
  226.1 7.1 %shard_map.150 = (bf16[512,1024]{1,0:T(8,128)(2,1)}, bf16[16,32,5248]{2,1,0:T(8,128)(2,1)}, bf16[16,32,5248]{2,1,0:T(8,128)(2,1)}) custom-call(s32[1]{0:T(128)} %bitcast.26.refs_0_, bf16[512,1024]{1,0:T(8,128)(2,1)} %get-tuple-element.120.refs_0_.refs_1_, ...), custom_call_target="tpu_custom_call", output_to_operand_aliasing={{1}: (6, {}), {2}: (7, {})} | custom-call | flops 1 | bytes 1 | tf_op jit(solution)/shard_map/pallas_call | solution.py:40
  234.5 4.2 %shard_map.151 = (bf16[4,2,64,1024]{3,2,1,0:T(8,128)(2,1)S(1)}, bf16[4,2,64,1024]{3,2,1,0:T(8,128)(2,1)S(1)}, bf16[4,2,64,1024]{3,2,1,0:T(8,128)(2,1)S(1)}, bf16[4,2,64,1024]{3,2,1,0:T(8,128)(2,1)S(1)}) custom-call(s32[2]{0:T(128)S(1)} %pad_add_fusion.refs_0_, bf16[4,2,2,128,1024]{4,3,2,1,0:T(8,128)(2,1)S(1)} %bitcast.57, ...), custom_call_target="tpu_custom_call" | custom-call | flops 1 | bytes 1 | tf_op jit(solution)/shard_map/pallas_call | solution.py:40
  242.4 19.3 %shard_map.153.refs_3_ = bf16[3,512,1024]{2,1,0:T(8,128)(2,1)S(1)} custom-call(bf16[512,3072]{1,0:T(8,128)(2,1)S(1)} %copy-done.2, bf16[512,3072]{1,0:T(8,128)(2,1)S(1)} %copy-done.2, bf16[512,3072]{1,0:T(8,128)(2,1)S(1)} %copy-done.2, bf16[512,1024]{1,0:T(8,128)(2,1)S(1)} %get-tuple-element.157.refs_3_, s32[512,1]{1,0:T(8,128)S(1)} %copy-done.9, ...), custom_call_target="tpu_custom_call" | custom-call | flops 1 | bytes 1 | tf_op jit(solution)/shard_map/pallas_call | solution.py:40
  261.7 2.8 collective-permute-done.26.refs_4_
  267.9 3.2 shard_map.154
  274.9 8.9 %shard_map.156 = (bf16[16,32,3072]{2,1,0:T(8,128)(2,1)}, bf16[16,32,3072]{2,1,0:T(8,128)(2,1)}) custom-call(s32[1]{0:T(128)} %bitcast.26.refs_0_, bf16[512,1024]{1,0:T(8,128)(2,1)} %bitcast.65, bf16[3,512,1024]{2,1,0:T(8,128)(2,1)} %copy-done.3), custom_call_target="tpu_custom_call" | custom-call | flops 1 | bytes 1 | tf_op jit(solution)/shard_map/pallas_call | solution.py:40
  283.8 8.3 %shard_map.157.refs_5_.refs_2_ = bf16[512,1024]{1,0:T(8,128)(2,1)} custom-call(bf16[3,512,1024]{2,1,0:T(8,128)(2,1)} %copy-done.3, bf16[1024,4224]{1,0:T(8,128)(2,1)} %get-tuple-element.121.refs_1_.refs_3_, f32[512,1024]{1,0:T(8,128)} %get-tuple-element.171.refs_2_, bf16[16,32,3072]{2,1,0:T(8,128)(2,1)} %get-tuple-element.172.refs_3_.refs_2_), custom_call_target="tpu_custom_call" | custom-call | flops 1 | bytes 1 | tf_op jit(solution)/shard_map/pallas_call | solution.py:40
  292.1 11.4 %collective-permute-done.28.refs_2_ = bf16[4,2,16,5248]{3,2,1,0:T(8,128)(2,1)} collective-permute-done((bf16[4,2,16,5248]{3,2,1,0:T(8,128)(2,1)}, bf16[4,2,16,5248]{3,2,1,0:T(8,128)(2,1)}, u32[]{:S(2)}, u32[]{:S(2)}) %collective-permute-start.28) | collective-permute-done | bytes 1343520 | tf_op jit(solution)/shard_map/ppermute | solution.py:759
  304.2 2.9 shard_map.158
  309.8 12.7 %collective-permute-done.31.refs_3_ = bf16[4,16,5248]{2,1,0:T(8,128)(2,1)S(1)} collective-permute-done((bf16[4,16,5248]{2,1,0:T(8,128)(2,1)S(1)}, bf16[4,16,5248]{2,1,0:T(8,128)(2,1)S(1)}, u32[]{:S(2)}, u32[]{:S(2)}) %collective-permute-start.31) | collective-permute-done | bytes 671776 | tf_op jit(solution)/shard_map/ppermute | solution.py:759
  326.1 2.3 shard_map.160
  336.5 14.2 %collective-permute-done.35.refs_5_ = bf16[64,1024]{1,0:T(8,128)(2,1)S(1)} collective-permute-done((bf16[64,1024]{1,0:T(8,128)(2,1)S(1)}, bf16[64,1024]{1,0:T(8,128)(2,1)S(1)}, u32[]{:S(2)}, u32[]{:S(2)}) %collective-permute-start.35) | collective-permute-done | bytes 131104 | tf_op jit(solution)/shard_map/ppermute | solution.py:759
  357.7 4.5 %collective-permute-done.37 = bf16[4,16,3072]{2,1,0:T(8,128)(2,1)S(1)} collective-permute-done((bf16[4,16,3072]{2,1,0:T(8,128)(2,1)}, bf16[4,16,3072]{2,1,0:T(8,128)(2,1)S(1)}, u32[]{:S(2)}, u32[]{:S(2)}) %collective-permute-start.37) | collective-permute-done | bytes 393248 | tf_op jit(solution)/shard_map/ppermute | solution.py:759
  368.6 3.5 all-to-all-start.2
  374.3 12.3 %all-to-all-done.2 = bf16[4,128,1024]{2,1,0:T(8,128)(2,1)S(1)} async-done(((bf16[4,128,1024]{2,1,0:T(8,128)(2,1)}), bf16[4,128,1024]{2,1,0:T(8,128)(2,1)S(1)}, u32[]{:S(2)}, u32[]{:S(2)}) %all-to-all-start.2) | async-done | bytes 1048608 | tf_op jit(solution)/shard_map/all_to_all | solution.py:875
  388.2 3.2 reduce-scatter.8.cloned.1.call-done
  (282 shorter events, 107.6 us)
Async XLA Ops:
  7.2 34.2 %all-gather.7.cloned.1.call-start = ((), (), s32[]{:S(2)}) async-start(), calls=%async_computation.9 | async-start | bytes 1351680 | tf_op jit(solution)/shard_map/all_gather | solution.py:883
  23.2 29.9 %all-to-all-start = ((bf16[4,256,1024]{2,1,0:T(8,128)(2,1)}), bf16[4,256,1024]{2,1,0:T(8,128)(2,1)S(1)}, u32[]{:S(2)}, u32[]{:S(2)}) async-start(bf16[4,256,1024]{2,1,0:T(8,128)(2,1)} %shard_map.136), calls=%async_computation | async-start | bytes 4194304 | tf_op jit(solution)/shard_map/all_to_all | solution.py:875
  26.9 47.2 %all-gather.9.cloned.1.call-start = ((), (), s32[]{:S(2)}) async-start(), calls=%async_computation.10 | async-start | bytes 1310720 | tf_op jit(solution)/shard_map/all_gather | solution.py:883
  43.7 20.6 %collective-permute-start.3 = (bf16[4,16,4224]{2,1,0:T(8,128)(2,1)}, bf16[4,16,4224]{2,1,0:T(8,128)(2,1)}, u32[]{:S(2)}, u32[]{:S(2)}) collective-permute-start(bf16[4,16,4224]{2,1,0:T(8,128)(2,1)} %get-tuple-element.104), channel_id=1, source_target_pairs={{0,2},{1,3},{2,0},{3,1},{4,6},{5,7},{6,4},{7,5},{8,10},{9,11},{10,... | collective-permute-start | bytes 1622024 | tf_op jit(solution)/shard_map/ppermute | solution.py:759
  45.1 21.3 %collective-permute-start.2 = (bf16[4,16,4224]{2,1,0:T(8,128)(2,1)}, bf16[4,16,4224]{2,1,0:T(8,128)(2,1)S(1)}, u32[]{:S(2)}, u32[]{:S(2)}) collective-permute-start(bf16[4,16,4224]{2,1,0:T(8,128)(2,1)} %get-tuple-element.103.refs_1_), channel_id=1, source_target_pairs={{0,4},{1,5},{2,6},{3,7},{4,0},{5,1},{6,2},{7,3},{8,12},{9,13},{10,... | collective-permute-start | bytes 1622024 | tf_op jit(solution)/shard_map/ppermute | solution.py:759
  48.3 93.3 %all-gather.11.cloned.1.call-start = ((), (), s32[]{:S(2)}) async-start(), calls=%async_computation.11 | async-start | bytes 2621440 | tf_op jit(solution)/shard_map/all_gather | solution.py:883
  67.6 25.6 %collective-permute-start.4 = (bf16[2,4,16,4224]{3,2,1,0:T(8,128)(2,1)}, bf16[2,4,16,4224]{3,2,1,0:T(8,128)(2,1)S(1)}, u32[]{:S(2)}, u32[]{:S(2)}) collective-permute-start(bf16[2,4,16,4224]{3,2,1,0:T(8,128)(2,1)} %get-tuple-element.105.refs_2_), channel_id=1, source_target_pairs={{0,2},{1,3},{2,0},{3,1},{4,6},{5,7},{6,4},{7,5},{8,10},{9,11},{10,... | collective-permute-start | bytes 3244040 | tf_op jit(solution)/shard_map/ppermute | solution.py:759
  67.9 25.6 %collective-permute-start.5 = (bf16[2,4,16,4224]{3,2,1,0:T(8,128)(2,1)}, bf16[2,4,16,4224]{3,2,1,0:T(8,128)(2,1)S(1)}, u32[]{:S(2)}, u32[]{:S(2)}) collective-permute-start(bf16[2,4,16,4224]{3,2,1,0:T(8,128)(2,1)} %get-tuple-element.106.refs_4_), channel_id=1, source_target_pairs={{0,4},{1,5},{2,6},{3,7},{4,0},{5,1},{6,2},{7,3},{8,12},{9,13},{10,... | collective-permute-start | bytes 3244040 | tf_op jit(solution)/shard_map/ppermute | solution.py:759
  68.8 24.7 %collective-permute-start.6 = (bf16[2,4,16,4224]{3,2,1,0:T(8,128)(2,1)}, bf16[2,4,16,4224]{3,2,1,0:T(8,128)(2,1)S(1)}, u32[]{:S(2)}, u32[]{:S(2)}) collective-permute-start(bf16[2,4,16,4224]{3,2,1,0:T(8,128)(2,1)} %get-tuple-element.105.refs_2_), channel_id=1, source_target_pairs={{0,1},{1,0},{2,3},{3,2},{4,5},{5,4},{6,7},{7,6},{8,9},{9,8},{10,11... | collective-permute-start | bytes 3244040 | tf_op jit(solution)/shard_map/ppermute | solution.py:759
  68.9 24.7 %collective-permute-start.7 = (bf16[2,4,16,4224]{3,2,1,0:T(8,128)(2,1)}, bf16[2,4,16,4224]{3,2,1,0:T(8,128)(2,1)}, u32[]{:S(2)}, u32[]{:S(2)}) collective-permute-start(bf16[2,4,16,4224]{3,2,1,0:T(8,128)(2,1)} %get-tuple-element.106.refs_4_), channel_id=1, source_target_pairs={{0,1},{1,0},{2,3},{3,2},{4,5},{5,4},{6,7},{7,6},{8,9},{9,8},{10,11... | collective-permute-start | bytes 3244040 | tf_op jit(solution)/shard_map/ppermute | solution.py:759
  113.3 25.1 %collective-permute-start.13 = (bf16[2,4,16,4096]{3,2,1,0:T(8,128)(2,1)S(1)}, bf16[2,4,16,4096]{3,2,1,0:T(8,128)(2,1)S(1)}, u32[]{:S(2)}, u32[]{:S(2)}) collective-permute-start(bf16[2,4,16,4096]{3,2,1,0:T(8,128)(2,1)S(1)} %pad_maximum_fusion.5.refs_4_), channel_id=1, source_target_pairs={{0,4},{1,5},{2,6},{3,7},{4,0},{5,1},{6,2},{7,3},{8,12},{9,13},{10,... | collective-permute-start | bytes 3145736 | tf_op jit(solution)/shard_map/ppermute | solution.py:759
  114.5 23.9 %collective-permute-start.15 = (bf16[2,4,16,4096]{3,2,1,0:T(8,128)(2,1)S(1)}, bf16[2,4,16,4096]{3,2,1,0:T(8,128)(2,1)S(1)}, u32[]{:S(2)}, u32[]{:S(2)}) collective-permute-start(bf16[2,4,16,4096]{3,2,1,0:T(8,128)(2,1)S(1)} %pad_maximum_fusion.5.refs_4_), channel_id=1, source_target_pairs={{0,1},{1,0},{2,3},{3,2},{4,5},{5,4},{6,7},{7,6},{8,9},{9,8},{10,11... | collective-permute-start | bytes 3145736 | tf_op jit(solution)/shard_map/ppermute | solution.py:759
  114.6 25.6 %collective-permute-start.12 = (bf16[2,4,16,4096]{3,2,1,0:T(8,128)(2,1)S(1)}, bf16[2,4,16,4096]{3,2,1,0:T(8,128)(2,1)S(1)}, u32[]{:S(2)}, u32[]{:S(2)}) collective-permute-start(bf16[2,4,16,4096]{3,2,1,0:T(8,128)(2,1)S(1)} %pad_maximum_fusion.4.refs_2_), channel_id=1, source_target_pairs={{0,2},{1,3},{2,0},{3,1},{4,6},{5,7},{6,4},{7,5},{8,10},{9,11},{10,... | collective-permute-start | bytes 3145736 | tf_op jit(solution)/shard_map/ppermute | solution.py:759
  116.1 24.2 %collective-permute-start.14 = (bf16[2,4,16,4096]{3,2,1,0:T(8,128)(2,1)S(1)}, bf16[2,4,16,4096]{3,2,1,0:T(8,128)(2,1)}, u32[]{:S(2)}, u32[]{:S(2)}) collective-permute-start(bf16[2,4,16,4096]{3,2,1,0:T(8,128)(2,1)S(1)} %pad_maximum_fusion.4.refs_2_), channel_id=1, source_target_pairs={{0,1},{1,0},{2,3},{3,2},{4,5},{5,4},{6,7},{7,6},{8,9},{9,8},{10,11... | collective-permute-start | bytes 3145736 | tf_op jit(solution)/shard_map/ppermute | solution.py:759
  144.0 25.2 %collective-permute-start.16 = (bf16[2,4,64,1024]{3,2,1,0:T(8,128)(2,1)S(1)}, bf16[2,4,64,1024]{3,2,1,0:T(8,128)(2,1)S(1)}, u32[]{:S(2)}, u32[]{:S(2)}) collective-permute-start(bf16[2,4,64,1024]{3,2,1,0:T(8,128)(2,1)S(1)} %get-tuple-element.228.refs_5_), channel_id=1, source_target_pairs={{0,2},{1,3},{2,0},{3,1},{4,6},{5,7},{6,4},{7,5},{8,10},{9,11},{10,... | collective-permute-start | bytes 3145736 | tf_op jit(solution)/shard_map/ppermute | solution.py:759
  145.5 25.6 %collective-permute-start.18 = (bf16[2,4,64,1024]{3,2,1,0:T(8,128)(2,1)S(1)}, bf16[2,4,64,1024]{3,2,1,0:T(8,128)(2,1)S(1)}, u32[]{:S(2)}, u32[]{:S(2)}) collective-permute-start(bf16[2,4,64,1024]{3,2,1,0:T(8,128)(2,1)S(1)} %get-tuple-element.228.refs_5_), channel_id=1, source_target_pairs={{0,1},{1,0},{2,3},{3,2},{4,5},{5,4},{6,7},{7,6},{8,9},{9,8},{10,11... | collective-permute-start | bytes 3145736 | tf_op jit(solution)/shard_map/ppermute | solution.py:759
  145.6 25.6 %collective-permute-start.17 = (bf16[2,4,64,1024]{3,2,1,0:T(8,128)(2,1)S(1)}, bf16[2,4,64,1024]{3,2,1,0:T(8,128)(2,1)S(1)}, u32[]{:S(2)}, u32[]{:S(2)}) collective-permute-start(bf16[2,4,64,1024]{3,2,1,0:T(8,128)(2,1)S(1)} %get-tuple-element.227.refs_7_), channel_id=1, source_target_pairs={{0,4},{1,5},{2,6},{3,7},{4,0},{5,1},{6,2},{7,3},{8,12},{9,13},{10,... | collective-permute-start | bytes 3145736 | tf_op jit(solution)/shard_map/ppermute | solution.py:759
  147.0 24.1 %collective-permute-start.19 = (bf16[2,4,64,1024]{3,2,1,0:T(8,128)(2,1)S(1)}, bf16[2,4,64,1024]{3,2,1,0:T(8,128)(2,1)S(1)}, u32[]{:S(2)}, u32[]{:S(2)}) collective-permute-start(bf16[2,4,64,1024]{3,2,1,0:T(8,128)(2,1)S(1)} %get-tuple-element.227.refs_7_), channel_id=1, source_target_pairs={{0,1},{1,0},{2,3},{3,2},{4,5},{5,4},{6,7},{7,6},{8,9},{9,8},{10,11... | collective-permute-start | bytes 3145736 | tf_op jit(solution)/shard_map/ppermute | solution.py:759
  193.0 31.6 %all-to-all-start.1 = ((bf16[4,128,1024]{2,1,0:T(8,128)(2,1)}), bf16[4,128,1024]{2,1,0:T(8,128)(2,1)S(1)}, u32[]{:S(2)}, u32[]{:S(2)}) async-start(bf16[4,128,1024]{2,1,0:T(8,128)(2,1)} %bitcast.77), calls=%async_computation.1 | async-start | bytes 2097152 | tf_op jit(solution)/shard_map/all_to_all | solution.py:875
  196.5 131.9 %reduce-scatter.4.cloned.1.call-start = ((), (), s32[]{:S(2)}) async-start(), calls=%async_computation.6 | async-start | bytes 2621440 | tf_op jit(solution)/shard_map/reduce_scatter | solution.py:982
  238.8 29.0 %collective-permute-start.25 = (bf16[16,32,5248]{2,1,0:T(8,128)(2,1)S(1)}, bf16[16,32,5248]{2,1,0:T(8,128)(2,1)S(1)}, u32[]{:S(2)}, u32[]{:S(2)}) collective-permute-start(bf16[16,32,5248]{2,1,0:T(8,128)(2,1)S(1)} %get-tuple-element.156), channel_id=1, source_target_pairs={{0,1},{1,0},{2,3},{3,2},{4,5},{5,4},{6,7},{7,6},{8,9},{9,8},{10,11... | collective-permute-start | bytes 16121864 | tf_op jit(solution)/shard_map/ppermute | solution.py:759
  239.1 25.3 %collective-permute-start.26 = (bf16[4,2,64,1024]{3,2,1,0:T(8,128)(2,1)S(1)}, bf16[4,2,64,1024]{3,2,1,0:T(8,128)(2,1)S(1)}, u32[]{:S(2)}, u32[]{:S(2)}) collective-permute-start(bf16[4,2,64,1024]{3,2,1,0:T(8,128)(2,1)S(1)} %get-tuple-element.159), channel_id=1, source_target_pairs={{0,2},{1,3},{2,0},{3,1},{4,6},{5,7},{6,4},{7,5},{8,10},{9,11},{10,... | collective-permute-start | bytes 3145736 | tf_op jit(solution)/shard_map/ppermute | solution.py:759
  240.9 25.0 %collective-permute-start.27 = (bf16[4,2,64,1024]{3,2,1,0:T(8,128)(2,1)S(1)}, bf16[4,2,64,1024]{3,2,1,0:T(8,128)(2,1)S(1)}, u32[]{:S(2)}, u32[]{:S(2)}) collective-permute-start(bf16[4,2,64,1024]{3,2,1,0:T(8,128)(2,1)S(1)} %get-tuple-element.160), channel_id=1, source_target_pairs={{0,4},{1,5},{2,6},{3,7},{4,0},{5,1},{6,2},{7,3},{8,12},{9,13},{10,... | collective-permute-start | bytes 3145736 | tf_op jit(solution)/shard_map/ppermute | solution.py:759
  272.7 30.8 %collective-permute-start.28 = (bf16[4,2,16,5248]{3,2,1,0:T(8,128)(2,1)}, bf16[4,2,16,5248]{3,2,1,0:T(8,128)(2,1)}, u32[]{:S(2)}, u32[]{:S(2)}) collective-permute-start(bf16[4,2,16,5248]{3,2,1,0:T(8,128)(2,1)} %get-tuple-element.168), channel_id=1, source_target_pairs={{0,2},{1,3},{2,0},{3,1},{4,6},{5,7},{6,4},{7,5},{8,10},{9,11},{10,... | collective-permute-start | bytes 4030472 | tf_op jit(solution)/shard_map/ppermute | solution.py:759
  273.4 30.9 %collective-permute-start.29 = (bf16[4,2,16,5248]{3,2,1,0:T(8,128)(2,1)}, bf16[4,2,16,5248]{3,2,1,0:T(8,128)(2,1)}, u32[]{:S(2)}, u32[]{:S(2)}) collective-permute-start(bf16[4,2,16,5248]{3,2,1,0:T(8,128)(2,1)} %get-tuple-element.170), channel_id=1, source_target_pairs={{0,4},{1,5},{2,6},{3,7},{4,0},{5,1},{6,2},{7,3},{8,12},{9,13},{10,... | collective-permute-start | bytes 4030472 | tf_op jit(solution)/shard_map/ppermute | solution.py:759
  274.9 91.2 %reduce-scatter.6.cloned.1.call-start = ((), (), s32[]{:S(2)}) async-start(), calls=%async_computation.7 | async-start | bytes 1679360 | tf_op jit(solution)/shard_map/reduce_scatter | solution.py:998
  331.1 19.6 %collective-permute-start.33 = (bf16[4,2,16,3072]{3,2,1,0:T(8,128)(2,1)}, bf16[4,2,16,3072]{3,2,1,0:T(8,128)(2,1)S(1)}, u32[]{:S(2)}, u32[]{:S(2)}) collective-permute-start(bf16[4,2,16,3072]{3,2,1,0:T(8,128)(2,1)} %get-tuple-element.184), channel_id=1, source_target_pairs={{0,2},{1,3},{2,0},{3,1},{4,6},{5,7},{6,4},{7,5},{8,10},{9,11},{10,... | collective-permute-start | bytes 2359304 | tf_op jit(solution)/shard_map/ppermute | solution.py:759
  331.8 18.9 %collective-permute-start.34 = (bf16[4,2,16,3072]{3,2,1,0:T(8,128)(2,1)}, bf16[4,2,16,3072]{3,2,1,0:T(8,128)(2,1)S(1)}, u32[]{:S(2)}, u32[]{:S(2)}) collective-permute-start(bf16[4,2,16,3072]{3,2,1,0:T(8,128)(2,1)} %copy-done.16), channel_id=1, source_target_pairs={{0,4},{1,5},{2,6},{3,7},{4,0},{5,1},{6,2},{7,3},{8,12},{9,13},{10,... | collective-permute-start | bytes 2359304 | tf_op jit(solution)/shard_map/ppermute | solution.py:759
  332.4 59.0 %reduce-scatter.8.cloned.1.call-start = ((), (), s32[]{:S(2)}) async-start(), calls=%async_computation.8 | async-start | bytes 983040 | tf_op jit(solution)/shard_map/reduce_scatter | solution.py:1018
  333.5 17.1 %collective-permute-start.35 = (bf16[64,1024]{1,0:T(8,128)(2,1)S(1)}, bf16[64,1024]{1,0:T(8,128)(2,1)S(1)}, u32[]{:S(2)}, u32[]{:S(2)}) collective-permute-start(bf16[64,1024]{1,0:T(8,128)(2,1)S(1)} %dynamic-slice_bitcast_fusion.1), channel_id=1, source_target_pairs={{0,4},{1,5},{2,6},{3,7},{4,0},{5,1},{6,2},{7,3},{8,12},{9,13},{10,... | collective-permute-start | bytes 393224 | tf_op jit(solution)/shard_map/ppermute | solution.py:759
  335.1 15.6 %collective-permute-start.36 = (bf16[64,1024]{1,0:T(8,128)(2,1)S(1)}, bf16[64,1024]{1,0:T(8,128)(2,1)S(1)}, u32[]{:S(2)}, u32[]{:S(2)}) collective-permute-start(bf16[64,1024]{1,0:T(8,128)(2,1)S(1)} %dynamic-slice_bitcast_fusion), channel_id=1, source_target_pairs={{0,2},{1,3},{2,0},{3,1},{4,6},{5,7},{6,4},{7,5},{8,10},{9,11},{10,... | collective-permute-start | bytes 393224 | tf_op jit(solution)/shard_map/ppermute | solution.py:759
  368.6 18.0 %all-to-all-start.2 = ((bf16[4,128,1024]{2,1,0:T(8,128)(2,1)}), bf16[4,128,1024]{2,1,0:T(8,128)(2,1)S(1)}, u32[]{:S(2)}, u32[]{:S(2)}) async-start(bf16[4,128,1024]{2,1,0:T(8,128)(2,1)} %bitcast.37), calls=%async_computation.4 | async-start | bytes 2097152 | tf_op jit(solution)/shard_map/all_to_all | solution.py:875
  (73 other events, 445.8 us)
Sparse Core Ops, SparseCore 0:
  10.2 31.1 all-gather.6
  48.4 25.5 all-gather.8
  95.0 46.5 all-gather.10
  275.0 43.3 reduce-scatter.3
  332.5 31.6 reduce-scatter.5
  367.9 23.4 reduce-scatter.7

commit v4 on v3

--- a/solution.py
+++ b/solution.py
@@ -214,12 +214,11 @@
 
 
 def project_kernel(count, table_ref, x_ref, *refs):
-    sources, (out_ref, norms_ref, kept_ref, full_ref, sem, back_sem) = refs[:count], refs[count:]
+    sources, (out_ref, kept_ref, full_ref, sem, back_sem) = refs[:count], refs[count:]
     for copy in start_slabs(table_ref, sources, full_ref, sem):
         copy.wait()
     back = pltpu.make_async_copy(full_ref, kept_ref, back_sem)
     back.start()
-    norms_ref[...] = full_ref[:, -128:].astype(jnp.float32).T[:8]
     x = x_ref[...]
     step = 512
     for j in range(out_ref.shape[1] // step):
@@ -235,10 +234,9 @@
         (table, x, *buffers,),
         after,
         in_specs=[SCALARS, whole(x.shape)] + [HBM] * len(buffers),
-        out_specs=[whole((x.shape[0], columns)), whole((8, total)), HBM],
+        out_specs=[whole((x.shape[0], columns)), HBM],
         out_shape=[
             jax.ShapeDtypeStruct((x.shape[0], columns), jnp.bfloat16),
-            jax.ShapeDtypeStruct((8, total), jnp.float32),
             jax.ShapeDtypeStruct((total, full_columns), jnp.bfloat16),
         ],
         grid=(1,),
@@ -269,50 +267,30 @@
     )
 
 
-def branch_kernel(context_ref, w_ref, tokens_ref, norm_ref, xhat_ref, scale_ref, low_ref):
-    step = 128
-    for j in range(context_ref.shape[0] // step):
-        here = slice(j * step, (j + 1) * step)
-        first_in = tokens_ref[here].astype(jnp.float32) + dot(context_ref[here], w_ref[...])
-        xhat, scale = normalise(first_in)
-        xhat_ref[here] = xhat
-        scale_ref[here] = scale
-        low_ref[here] = (xhat * norm_ref[0:1] + norm_ref[1:2]).astype(jnp.bfloat16)
-
-
-def branch(context, w_first, tokens, norm_rows, after=()):
-    rows, width = context.shape
-    return run(
-        branch_kernel,
-        (context, w_first, tokens, norm_rows,),
-        after,
-        grid=(1,),
-        in_specs=[
-            whole((rows, width)),
-            pl.BlockSpec((width, width), lambda i: (0, 3)),
-            whole((rows, width)),
-            whole(norm_rows.shape),
-        ],
-        out_specs=[whole((rows, width)), whole((rows, 1)), whole((rows, width))],
-        out_shape=[
-            jax.ShapeDtypeStruct((rows, width), jnp.float32),
-            jax.ShapeDtypeStruct((rows, 1), jnp.float32),
-            jax.ShapeDtypeStruct((rows, width), jnp.bfloat16),
-        ],
-        compiler_params=grant(56),
-        cost_estimate=NO_COST,
-    )
-
-
-def up_kernel(count, table_ref, x_ref, *refs):
-    sources, (act_ref, slope_ref, kept_ref, full_ref, sem, back_sem) = refs[:count], refs[count:]
+def middle_kernel(count, table_ref, context_ref, tokens_ref, *refs):
+    sources = refs[:count]
+    (xhat_ref, scale_ref, low_ref, norms_ref, act_ref, slope_ref, kept_ref) = refs[count : count + 7]
+    full_ref, sem, back_sem = refs[count + 7 :]
     for copy in start_slabs(table_ref, sources, full_ref, sem):
         copy.wait()
     back = pltpu.make_async_copy(full_ref, kept_ref, back_sem)
     back.start()
-    x = x_ref[...]
+    inner, width = act_ref.shape[1], context_ref.shape[1]
+    norms = full_ref[:, -128:].astype(jnp.float32).T[:8]
+    norms_ref[...] = norms
+    step = 128
+    for j in range(context_ref.shape[0] // step):
+        here = slice(j * step, (j + 1) * step)
+        first_in = tokens_ref[here].astype(jnp.float32) + dot(
+            context_ref[here], full_ref[:, inner : inner + width]
+        )
+        xhat, scale = normalise(first_in)
+        xhat_ref[here] = xhat
+        scale_ref[here] = scale
+        low_ref[here] = (xhat * norms[0:1] + norms[1:2]).astype(jnp.bfloat16)
+    x = low_ref[...]
     step = 256
-    for j in range(act_ref.shape[1] // step):
+    for j in range(inner // step):
         here = slice(j * step, (j + 1) * step)
         pre = dot(x, full_ref[:, here])
         below = 0.5 + 0.5 * lax.erf(pre * 0.7071067811865476)
@@ -322,23 +300,35 @@
     back.wait()
 
 
-def up_gelu(x, table, buffers, after=()):
-    total, columns = x.shape[1], buffers[0].shape[3]
-    rows = x.shape[0]
-    return run(
-        functools.partial(up_kernel, len(buffers)),
-        (table, x, *buffers,),
-        after,
-        in_specs=[SCALARS, whole(x.shape)] + [HBM] * len(buffers),
-        out_specs=[whole((rows, columns)), whole((rows, columns)), HBM],
+def middle(context, tokens, table, buffers, after=()):
+    rows, width = context.shape
+    columns = buffers[0].shape[3]
+    inner = columns - width - 128
+    return run(
+        functools.partial(middle_kernel, len(buffers)),
+        (table, context, tokens, *buffers),
+        after,
+        in_specs=[SCALARS, whole((rows, width)), whole((rows, width))] + [HBM] * len(buffers),
+        out_specs=[
+            whole((rows, width)),
+            whole((rows, 1)),
+            whole((rows, width)),
+            whole((8, width)),
+            whole((rows, inner)),
+            whole((rows, inner)),
+            HBM,
+        ],
         out_shape=[
-            jax.ShapeDtypeStruct((rows, columns), jnp.bfloat16),
-            jax.ShapeDtypeStruct((rows, columns), jnp.bfloat16),
-            jax.ShapeDtypeStruct((total, columns), jnp.bfloat16),
-        ],
-        grid=(1,),
+            jax.ShapeDtypeStruct((rows, width), jnp.float32),
+            jax.ShapeDtypeStruct((rows, 1), jnp.float32),
+            jax.ShapeDtypeStruct((rows, width), jnp.bfloat16),
+            jax.ShapeDtypeStruct((8, width), jnp.float32),
+            jax.ShapeDtypeStruct((rows, inner), jnp.bfloat16),
+            jax.ShapeDtypeStruct((rows, inner), jnp.bfloat16),
+            jax.ShapeDtypeStruct((width, columns), jnp.bfloat16),
+        ],
         scratch_shapes=[
-            pltpu.VMEM((total, columns), jnp.bfloat16),
+            pltpu.VMEM((width, columns), jnp.bfloat16),
             pltpu.SemaphoreType.DMA,
             pltpu.SemaphoreType.DMA,
         ],
@@ -601,20 +591,20 @@
         copy.wait()
 
 
-def out_grad(core, context, grad, w_first, norms_one, norms_two, kept, sent, after=()):
+def out_grad(core, context, grad, w_up, norms_one, norms_two, kept, sent, after=()):
     tokens, width = context.shape
     part = pltpu.VMEM(kept.shape[:2] + (width + 128,), jnp.bfloat16)
     out = kept.shape
     return run(
         out_grad_kernel,
-        (core, context, grad, w_first, norms_one, norms_two, kept, sent),
+        (core, context, grad, w_up, norms_one, norms_two, kept, sent),
         after,
         grid=(1,),
         in_specs=[
             SCALARS,
             whole((tokens, width)),
             whole((tokens, width)),
-            pl.BlockSpec((width, width), lambda i: (0, 3)),
+            pl.BlockSpec((width, width), lambda i: (0, w_up.shape[1] // width - 1)),
             whole((2, width)),
             whole((2, width)),
             HBM,
@@ -764,22 +754,6 @@
     return dp // 2, dp % 2, lax.axis_index("blk"), lax.axis_index("head")
 
 
-def copy_kernel(in_ref, out_ref):
-    out_ref[...] = in_ref[...]
-
-
-def copy_after(value, after):
-    return run(
-        copy_kernel,
-        (value,),
-        after,
-        in_specs=[whole(value.shape)],
-        out_specs=whole(value.shape),
-        out_shape=jax.ShapeDtypeStruct(value.shape, value.dtype),
-        cost_estimate=NO_COST,
-    )
-
-
 def side_kernel(left_ref, right_ref, out_ref):
     middle = left_ref.shape[1]
     out_ref[:, :middle] = left_ref[...]
@@ -839,9 +813,9 @@
     return jnp.stack([kept, sent], axis=1).reshape(-1, kept.shape[2])
 
 
-def joined_shards(qkv_weight, out_weight, norm_params):
+def joined_shards(up_weight, out_weight, norm_params):
     norm_wide = jnp.pad(norm_params, ((0, 0), (0, 128 - norm_params.shape[1])))
-    return jnp.concatenate([qkv_weight, out_weight, norm_wide], axis=1)
+    return jnp.concatenate([up_weight, out_weight, norm_wide], axis=1)
 
 
 def split_up(grad, width):
@@ -878,14 +852,14 @@
     own_lengths = lax.dynamic_slice_in_dim(doc_lengths, place, 1, 0)
     seg_row = segments_of(own_lengths, full_len)
     seg_col = seg_row.reshape(full_len, 1)
-    first_own, up_own = joined_shards(qkv_weight, out_weight, norm_params), up_weight
+    first_own, up_own = qkv_weight, joined_shards(up_weight, out_weight, norm_params)
     half, ff_half = slab // 2, ff_slab // 2
     line = lambda v: lax.all_gather(v, "dp", axis_index_groups=LINES)
 
     first_line = line(first_own)
     down_a, down_b = down_weight[:ff_half], down_weight[ff_half:]
     down_ax, down_by = send(down_a, ROUTE_X), send(down_b, ROUTE_Y)
-    both = exchange(side_by_side(tokens, out_cotangent, (first_own, down_ax, down_by)))
+    both = exchange(side_by_side(tokens, out_cotangent, ()))
     rows, upstream = (
         v.reshape(full_len, width) for v in (both[:, :local_len], both[:, local_len:])
     )
@@ -893,31 +867,28 @@
 
     a, b = gate(
         (first_line[:, :half], first_line[:, half:]),
-        (down_own, seg_row, seg_col),
-    )
-    up_shard = copy_after(up_own, (a,))
+        (rows, upstream, down_own, seg_row, seg_col),
+    )
     ax, by = send(a, ROUTE_X), send(b, ROUTE_Y)
-    up_line = line(up_shard)
-
-    a2, b2 = gate((jnp.stack([a, ax]), jnp.stack([b, by])), (rows, upstream))
+    up_line = line(up_own)
+
+    a2, b2 = gate((jnp.stack([a, ax]), jnp.stack([b, by])))
     ay, bx = send(a2, ROUTE_Y), send(b2, ROUTE_X)
-    a2c, b2c = send(a2, ROUTE_C), send(b2, ROUTE_C)
-
-    ay, bx, up_a, up_b, down_own, a2c, b2c = gate(
-        (ay, bx, up_line[:, :half], up_line[:, half:], down_own, a2c, b2c)
-    )
-    ayc, bxc = send(ay, ROUTE_C), send(bx, ROUTE_C)
+
+    up_a, up_b, down_own = gate((up_line[:, :half], up_line[:, half:], down_own))
     up_ax, up_by = send(up_a, ROUTE_X), send(up_b, ROUTE_Y)
     down_line = line(down_own)
-    table, buffers = with_partner(
-        first_own, buffers_of(a2, ay, b2, bx), (a2c, ayc, b2c, bxc)
-    )
-    projected, norm_rows, w_first = project(rows, table, buffers, 3 * width)
-
-    up_ax, up_by, projected = gate((up_ax, up_by, projected))
+
+    ay, bx, up_ax, up_by, a2, b2 = gate((ay, bx, up_ax, up_by, a2, b2))
+    a2c, b2c = send(a2, ROUTE_C), send(b2, ROUTE_C)
+    ayc, bxc = send(ay, ROUTE_C), send(bx, ROUTE_C)
     up_a2, up_b2 = jnp.stack([up_a, up_ax]), jnp.stack([up_b, up_by])
     up_ay, up_bx = send(up_a2, ROUTE_Y), send(up_b2, ROUTE_X)
     up_a2c, up_b2c = send(up_a2, ROUTE_C), send(up_b2, ROUTE_C)
+    table, buffers = with_partner(
+        first_own, buffers_of(a2, ay, b2, bx), (a2c, ayc, b2c, bxc)
+    )
+    projected, w_first = project(rows, table, buffers, 3 * width)
     context, log_sums = attention(projected, seg_col, seg_row)
 
     up_ay, up_bx, up_a2c, up_b2c, down_line, context = gate(
@@ -927,11 +898,10 @@
     down_ay, down_bx = send(down_a2, ROUTE_Y), send(down_b2, ROUTE_X)
     down_a2c, down_b2c = send(down_a2, ROUTE_C), send(down_b2, ROUTE_C)
     up_ayc, up_bxc = send(up_ay, ROUTE_C), send(up_bx, ROUTE_C)
-    xhat, scale, first_low = branch(context, w_first, rows, norm_rows)
     table, buffers = with_partner(
         up_own, buffers_of(up_a2, up_ay, up_b2, up_bx), (up_a2c, up_ayc, up_b2c, up_bxc)
     )
-    act, slope, w_up = up_gelu(first_low, table, buffers)
+    xhat, scale, first_low, norm_rows, act, slope, w_up = middle(context, rows, table, buffers)
 
     down_ay, down_bx, down_a2c, down_b2c, act = gate((down_ay, down_bx, down_a2c, down_b2c, act))
     down_ayc, down_bxc = send(down_ay, ROUTE_C), send(down_bx, ROUTE_C)
@@ -966,7 +936,7 @@
     down_sent, grad_branch = gate((down_sent, grad_branch), (layer_out,))
     down_came = send(down_sent, ROUTE_C)
     grad_context, up_kept, up_sent = out_grad(
-        core, context, grad_branch, w_first, norms_one, norms_two, up_kept, up_sent
+        core, context, grad_branch, w_up, norms_one, norms_two, up_kept, up_sent
     )
 
     da_own, da_out, db_own, db_out = fold_cores(down_kept, down_came, (grad_context,))
@@ -1056,11 +1026,11 @@
     own_lengths = lax.dynamic_slice_in_dim(doc_lengths, place, 1, 0)
     seg_row = segments_of(own_lengths, full_len)
     seg_col = seg_row.reshape(full_len, 1)
-    first_slots = gather(joined_shards(qkv_weight, out_weight, norm_params))
-    projected, norm_rows, w_first = project(rows, *first_slots, 3 * width)
+    first_slots = gather(qkv_weight)
+    up_slots = gather(joined_shards(up_weight, out_weight, norm_params))
+    projected, w_first = project(rows, *first_slots, 3 * width)
     context, log_sums = attention(projected, seg_col, seg_row)
-    xhat, scale, first_low = branch(context, w_first, rows, norm_rows)
-    act, slope, w_up = up_gelu(first_low, *gather(up_weight))
+    xhat, scale, first_low, norm_rows, act, slope, w_up = middle(context, rows, *up_slots)
     result, grad_second, grad_ff, norms_two, w_down = down_norm(
         act, *gather(down_weight), xhat, norm_rows, upstream
     )
@@ -1081,7 +1051,7 @@
     )
     grad_down = scatter(down_kept, down_sent)
     grad_context, up_kept, up_sent = out_grad(
-        core, context, grad_branch, w_first, norms_one, norms_two, up_kept, up_sent
+        core, context, grad_branch, w_up, norms_one, norms_two, up_kept, up_sent
     )
     grad_up, grad_out, grad_norm = split_up(scatter(up_kept, up_sent), width)
     grad_mixed = attention_back(projected, grad_context, seg_col, seg_row, log_sums)

time: 402 us -> 399 us (level)
  blocking collectives: 0 us -> 25.1 us
  waiting for transfers between devices: 132 us -> 110 us
  Pallas kernels: 150 us -> 145 us
    all_gather x0 -> x1, blocking collectives: none -> 25.1 us  [body_lines(): line = lambda v: lax.all_gather(v, 'dp', axis_index_groups=LINES)]
    all_gather x3 -> x2, waiting for transfers between devices: 18.4 us -> 0.01 us  [body_lines(): line = lambda v: lax.all_gather(v, 'dp', axis_index_groups=LINES)]
    pallas_call x30 -> x28, Pallas kernels: 150 us -> 145 us  [run(): return pl.pallas_call(body, grid_spec=spec, **rest)(*operands, *after)]
    all_to_all x3, waiting for transfers between devices: 16.9 us -> 12.3 us  [body_lines(): lax.all_to_all(v, GROUP, split_axis=0, concat_axis=0, tiled=True)]
    unnamed x117 -> x105, local copies, waits for them, and re-layouts: 20.5 us -> 19.6 us
  transfers between devices with their start and end apart: 48 -> 47, of which waited for: 27 -> 22; matrix products, arithmetic and copies ran while one was open for 9% -> 9% of each run, Pallas kernels for 32% -> 31%
where the time goes in v4:
time: 399 us; the launch traced here: 397 us
  Pallas kernels  145 us (36%)
  waiting for transfers between devices  110 us (28%)
  starting transfers between devices  45.7 us (11%)
  local copies, waits for them, and re-layouts  31.8 us (8%)
  blocking collectives  25.1 us (6%)
  other arithmetic  24.8 us (6%)
  between operations  14.4 us (4%)
    pallas_call x28, Pallas kernels, run(): return pl.pallas_call(body, grid_spec=spec, **rest)(*operands, *after)  145 us
    ppermute x39, waiting for transfers between devices, send(): return lax.ppermute(value, ALL, route)  93.5 us
    ppermute x39, starting transfers between devices, send(): return lax.ppermute(value, ALL, route)  34.7 us
    all_gather x1, blocking collectives, body_lines(): line = lambda v: lax.all_gather(v, 'dp', axis_index_groups=LINES)  25.1 us
    unnamed x105, local copies, waits for them, and re-layouts  19.6 us
    all_to_all x3, waiting for transfers between devices, body_lines(): lax.all_to_all(v, GROUP, split_axis=0, concat_axis=0, tiled=True)  12.3 us
    all_to_all x3, starting transfers between devices, body_lines(): lax.all_to_all(v, GROUP, split_axis=0, concat_axis=0, tiled=True)  10.8 us
  transfers between devices with their start and end apart: 47, of which 22 were waited for; matrix products, arithmetic and copies ran while one was open for 9% of the time, Pallas kernels for 31%

profile of v4, /device:TPU:0, one launch (start us, length us, event | category | flops | bytes accessed | tf_op | source)
XLA Modules:
  0.0 397.4 jit_solution(14193209125316947504)
XLA Ops:
  8.2 3.0 collective-permute-start
  12.7 3.8 shard_map.136
  16.5 3.8 all-to-all-start
  21.5 25.1 %all-gather.1 = bf16[128,3072]{1,0:T(8,128)(2,1)S(1)} all-gather(bf16[32,3072]{1,0:T(8,128)(2,1)S(1)} %copy-done.46), channel_id=3, replica_groups={{0,8,16,24},{4,12,20,28},{1,9,17,25},{5,13,21,29},{2,10,18,26},{6,14,22..., dimensions={0}, use_global_device_ids=true | all-gather | bytes 983040 | tf_op jit(solution)/shard_map/all_gather | solution.py:857
  55.5 7.9 %collective-permute-done.3 = bf16[4,16,3072]{2,1,0:T(8,128)(2,1)S(1)} collective-permute-done((bf16[4,16,3072]{2,1,0:T(8,128)(2,1)}, bf16[4,16,3072]{2,1,0:T(8,128)(2,1)S(1)}, u32[]{:S(2)}, u32[]{:S(2)}) %collective-permute-start.3) | collective-permute-done | bytes 393248 | tf_op jit(solution)/shard_map/ppermute | solution.py:749
  68.2 2.4 fusion.8
  73.8 25.3 %collective-permute-done.6.refs_2_ = bf16[4,16,5248]{2,1,0:T(8,128)(2,1)S(1)} collective-permute-done((bf16[4,16,5248]{2,1,0:T(8,128)(2,1)}, bf16[4,16,5248]{2,1,0:T(8,128)(2,1)S(1)}, u32[]{:S(2)}, u32[]{:S(2)}) %collective-permute-start.6) | collective-permute-done | bytes 671776 | tf_op jit(solution)/shard_map/ppermute | solution.py:749
  112.2 9.2 %shard_map.140 = (bf16[512,3072]{1,0:T(8,128)(2,1)}, bf16[1024,3072]{1,0:T(8,128)(2,1)}) custom-call(s32[64]{0:T(128)} %concatenate.24.refs_0_, bf16[512,1024]{1,0:T(8,128)(2,1)} %bitcast.63, bf16[2,4,16,3072]{3,2,1,0:T(8,128)(2,1)} %get-tuple-element.111.refs_2_, bf16[2,4,16,3072]{3,2,1,0:T(8,128)(2,1)} %get-tuple-element.112.refs_3_, ...), custom_call_target="tpu_custom_call" | custom-call | flops 1 | bytes 1 | tf_op jit(solution)/shard_map/pallas_call | solution.py:40
  121.3 13.5 %shard_map.141 = (bf16[512,1024]{1,0:T(8,128)(2,1)}, f32[8,2,512]{2,1,0:T(2,128)}) custom-call(bf16[512,3072]{1,0:T(8,128)(2,1)} %get-tuple-element.115.refs_0_.refs_1_.refs_2_, bf16[512,3072]{1,0:T(8,128)(2,1)} %get-tuple-element.115.refs_0_.refs_1_.refs_2_, bf16[512,3072]{1,0:T(8,128)(2,1)} %get-tuple-element.115.refs_0_.refs_1_.refs_2_, ...), custom_call_target="tpu_custom_call" | custom-call | flops 1 | bytes 1 | tf_op jit(solution)/shard_map/pallas_call | solution.py:40
  144.0 18.3 %shard_map.143 = (f32[512,1024]{1,0:T(8,128)}, f32[512,1]{1,0:T(8,128)}, bf16[512,1024]{1,0:T(8,128)(2,1)}, f32[8,1024]{1,0:T(8,128)}, bf16[512,4096]{1,0:T(8,12...) custom-call(s32[64]{0:T(128)} %concatenate.24.refs_0_, bf16[512,1024]{1,0:T(8,128)(2,1)} %get-tuple-element.118.refs_1_, ...), custom_call_target="tpu_custom_call" | custom-call | flops 1 | bytes 1 | tf_op jit(solution)/shard_map/pallas_call | solution.py:40
  162.3 2.2 collective-permute-done.16.refs_0_
  164.5 2.2 collective-permute-done.17.refs_1_
  174.4 14.2 %shard_map.145 = (bf16[512,1024]{1,0:T(8,128)(2,1)}, f32[512,1024]{1,0:T(8,128)}, bf16[512,1024]{1,0:T(8,128)(2,1)}, f32[2,1024]{1,0:T(2,128)}, bf16[4096,1024]{1,0:T(8,128)(2,1)}) custom-call(s32[64]{0:T(128)} %concatenate.22.refs_0_, bf16[512,4096]{1,0:T(8,128)(2,1)} %get-tuple-element.124.refs_1_, f32[512,1024]{1,0:T(8,128)} %get-tuple-element.125.refs_2_.refs_8_, ...), custom_call_target="tpu_custom_call" | custom-call | flops 1 | bytes 1 | tf_op jit(solution)/shard_map/pallas_call | solution.py:40
  188.6 3.5 all-to-all-start.1
  192.2 27.9 %shard_map.146 = (bf16[16,128,1024]{2,1,0:T(8,128)(2,1)}, bf16[16,128,1024]{2,1,0:T(8,128)(2,1)}, bf16[16,32,5248]{2,1,0:T(8,128)(2,1)}, bf16[16,32,5248]{2,1,0:...) custom-call(s32[1]{0:T(128)} %bitcast.26.refs_0_, ...), custom_call_target="tpu_custom_call" | custom-call | flops 1 | bytes 1 | tf_op jit(solution)/shard_map/pallas_call | solution.py:40
  221.5 7.3 %shard_map.148 = (bf16[512,1024]{1,0:T(8,128)(2,1)}, bf16[16,32,5248]{2,1,0:T(8,128)(2,1)}, bf16[16,32,5248]{2,1,0:T(8,128)(2,1)}) custom-call(s32[1]{0:T(128)} %bitcast.26.refs_0_, bf16[512,1024]{1,0:T(8,128)(2,1)} %get-tuple-element.118.refs_1_, bf16[512,1024]{1,0:T(8,128)(2,1)} %get-tuple-element.141.refs_2_, ...), custom_call_target="tpu_custom_call", output_to_operand_aliasing={{1}: (6, {}), {2}: (7, {})} | custom-call | flops 1 | bytes 1 | tf_op jit(solution)/shard_map/pallas_call | solution.py:40
  230.1 4.2 %shard_map.149 = (bf16[4,2,64,1024]{3,2,1,0:T(8,128)(2,1)S(1)}, bf16[4,2,64,1024]{3,2,1,0:T(8,128)(2,1)S(1)}, bf16[4,2,64,1024]{3,2,1,0:T(8,128)(2,1)S(1)}, bf16[4,2,64,1024]{3,2,1,0:T(8,128)(2,1)S(1)}) custom-call(s32[2]{0:T(128)S(1)} %pad_add_fusion.refs_0_, bf16[4,2,2,128,1024]{4,3,2,1,0:T(8,128)(2,1)S(1)} %bitcast.57, ...), custom_call_target="tpu_custom_call" | custom-call | flops 1 | bytes 1 | tf_op jit(solution)/shard_map/pallas_call | solution.py:40
  238.3 19.3 %shard_map.151.refs_3_ = bf16[3,512,1024]{2,1,0:T(8,128)(2,1)S(1)} custom-call(bf16[512,3072]{1,0:T(8,128)(2,1)S(1)} %copy-done.2, bf16[512,3072]{1,0:T(8,128)(2,1)S(1)} %copy-done.2, bf16[512,3072]{1,0:T(8,128)(2,1)S(1)} %copy-done.2, bf16[512,1024]{1,0:T(8,128)(2,1)S(1)} %get-tuple-element.154.refs_3_, s32[512,1]{1,0:T(8,128)S(1)} %copy-done.9, ...), custom_call_target="tpu_custom_call" | custom-call | flops 1 | bytes 1 | tf_op jit(solution)/shard_map/pallas_call | solution.py:40
  257.5 2.5 collective-permute-done.26.refs_4_
  263.4 3.2 shard_map.152
  270.8 9.1 %shard_map.154 = (bf16[16,32,3072]{2,1,0:T(8,128)(2,1)}, bf16[16,32,3072]{2,1,0:T(8,128)(2,1)}) custom-call(s32[1]{0:T(128)} %bitcast.26.refs_0_, bf16[512,1024]{1,0:T(8,128)(2,1)} %bitcast.65, bf16[3,512,1024]{2,1,0:T(8,128)(2,1)} %copy-done.3), custom_call_target="tpu_custom_call" | custom-call | flops 1 | bytes 1 | tf_op jit(solution)/shard_map/pallas_call | solution.py:40
  279.8 8.3 %shard_map.155.refs_5_.refs_2_ = bf16[512,1024]{1,0:T(8,128)(2,1)} custom-call(bf16[3,512,1024]{2,1,0:T(8,128)(2,1)} %copy-done.3, bf16[1024,3072]{1,0:T(8,128)(2,1)} %get-tuple-element.168.refs_1_, f32[512,1024]{1,0:T(8,128)} %get-tuple-element.169.refs_2_, bf16[16,32,3072]{2,1,0:T(8,128)(2,1)} %get-tuple-element.170.refs_3_.refs_2_), custom_call_target="tpu_custom_call" | custom-call | flops 1 | bytes 1 | tf_op jit(solution)/shard_map/pallas_call | solution.py:40
  288.1 10.9 %collective-permute-done.28.refs_2_ = bf16[4,2,16,5248]{3,2,1,0:T(8,128)(2,1)} collective-permute-done((bf16[4,2,16,5248]{3,2,1,0:T(8,128)(2,1)}, bf16[4,2,16,5248]{3,2,1,0:T(8,128)(2,1)}, u32[]{:S(2)}, u32[]{:S(2)}) %collective-permute-start.28) | collective-permute-done | bytes 1343520 | tf_op jit(solution)/shard_map/ppermute | solution.py:749
  299.7 3.0 shard_map.156
  305.5 12.4 %collective-permute-done.31.refs_3_ = bf16[4,16,5248]{2,1,0:T(8,128)(2,1)S(1)} collective-permute-done((bf16[4,16,5248]{2,1,0:T(8,128)(2,1)S(1)}, bf16[4,16,5248]{2,1,0:T(8,128)(2,1)S(1)}, u32[]{:S(2)}, u32[]{:S(2)}) %collective-permute-start.31) | collective-permute-done | bytes 671776 | tf_op jit(solution)/shard_map/ppermute | solution.py:749
  321.7 2.3 shard_map.158
  332.2 14.1 %collective-permute-done.35.refs_5_ = bf16[64,1024]{1,0:T(8,128)(2,1)S(1)} collective-permute-done((bf16[64,1024]{1,0:T(8,128)(2,1)S(1)}, bf16[64,1024]{1,0:T(8,128)(2,1)S(1)}, u32[]{:S(2)}, u32[]{:S(2)}) %collective-permute-start.35) | collective-permute-done | bytes 131104 | tf_op jit(solution)/shard_map/ppermute | solution.py:749
  346.3 2.0 shard_map.160
  353.2 4.6 %collective-permute-done.37 = bf16[4,16,3072]{2,1,0:T(8,128)(2,1)S(1)} collective-permute-done((bf16[4,16,3072]{2,1,0:T(8,128)(2,1)}, bf16[4,16,3072]{2,1,0:T(8,128)(2,1)S(1)}, u32[]{:S(2)}, u32[]{:S(2)}) %collective-permute-start.37) | collective-permute-done | bytes 393248 | tf_op jit(solution)/shard_map/ppermute | solution.py:749
  364.2 3.5 all-to-all-start.2
  369.9 12.3 %all-to-all-done.2 = bf16[4,128,1024]{2,1,0:T(8,128)(2,1)S(1)} async-done(((bf16[4,128,1024]{2,1,0:T(8,128)(2,1)}), bf16[4,128,1024]{2,1,0:T(8,128)(2,1)S(1)}, u32[]{:S(2)}, u32[]{:S(2)}) %all-to-all-start.2) | async-done | bytes 1048608 | tf_op jit(solution)/shard_map/all_to_all | solution.py:849
  383.8 4.4 %reduce-scatter.8.cloned.1.call-done = bf16[1,32,3072]{2,1,0:T(8,128)(2,1)} async-done(((bf16[4,32,3072]{2,1,0:T(8,128)(2,1)}), bf16[1,32,3072]{2,1,0:T(8,128)(2,1)}) %reduce-scatter.8.cloned.1.call-update) | async-done | bytes 196624 | tf_op jit(solution)/shard_map/reduce_scatter | solution.py:988
  (266 shorter events, 97.5 us)
Async XLA Ops:
  8.2 42.8 %collective-permute-start = (bf16[64,1024]{1,0:T(8,128)(2,1)S(1)}, bf16[64,1024]{1,0:T(8,128)(2,1)S(1)}, u32[]{:S(2)}, u32[]{:S(2)}) collective-permute-start(bf16[64,1024]{1,0:T(8,128)(2,1)S(1)} %get-tuple-element.238), channel_id=1, source_target_pairs={{0,4},{1,5},{2,6},{3,7},{4,0},{5,1},{6,2},{7,3},{8,12},{9,13},{10,... | collective-permute-start | bytes 393224 | tf_op jit(solution)/shard_map/ppermute | solution.py:749
  11.2 39.8 %collective-permute-start.1 = (bf16[64,1024]{1,0:T(8,128)(2,1)S(1)}, bf16[64,1024]{1,0:T(8,128)(2,1)S(1)}, u32[]{:S(2)}, u32[]{:S(2)}) collective-permute-start(bf16[64,1024]{1,0:T(8,128)(2,1)S(1)} %get-tuple-element.237), channel_id=1, source_target_pairs={{0,2},{1,3},{2,0},{3,1},{4,6},{5,7},{6,4},{7,5},{8,10},{9,11},{10,... | collective-permute-start | bytes 393224 | tf_op jit(solution)/shard_map/ppermute | solution.py:749
  16.5 35.3 %all-to-all-start = ((bf16[4,256,1024]{2,1,0:T(8,128)(2,1)}), bf16[4,256,1024]{2,1,0:T(8,128)(2,1)S(1)}, u32[]{:S(2)}, u32[]{:S(2)}) async-start(bf16[4,256,1024]{2,1,0:T(8,128)(2,1)} %shard_map.136), calls=%async_computation | async-start | bytes 4194304 | tf_op jit(solution)/shard_map/all_to_all | solution.py:849
  20.3 47.9 %all-gather.6.cloned.1.call-start = ((), (), s32[]{:S(2)}) async-start(), calls=%async_computation.9 | async-start | bytes 1679360 | tf_op jit(solution)/shard_map/all_gather | solution.py:857
  53.5 83.5 %all-gather.8.cloned.1.call-start = ((), (), s32[]{:S(2)}) async-start(), calls=%async_computation.10 | async-start | bytes 2621440 | tf_op jit(solution)/shard_map/all_gather | solution.py:857
  67.2 31.9 %collective-permute-start.4 = (bf16[2,4,16,3072]{3,2,1,0:T(8,128)(2,1)}, bf16[2,4,16,3072]{3,2,1,0:T(8,128)(2,1)S(1)}, u32[]{:S(2)}, u32[]{:S(2)}) collective-permute-start(bf16[2,4,16,3072]{3,2,1,0:T(8,128)(2,1)} %get-tuple-element.105.refs_4_), channel_id=1, source_target_pairs={{0,2},{1,3},{2,0},{3,1},{4,6},{5,7},{6,4},{7,5},{8,10},{9,11},{10,... | collective-permute-start | bytes 2359304 | tf_op jit(solution)/shard_map/ppermute | solution.py:749
  68.2 31.0 %collective-permute-start.5 = (bf16[2,4,16,3072]{3,2,1,0:T(8,128)(2,1)}, bf16[2,4,16,3072]{3,2,1,0:T(8,128)(2,1)S(1)}, u32[]{:S(2)}, u32[]{:S(2)}) collective-permute-start(bf16[2,4,16,3072]{3,2,1,0:T(8,128)(2,1)} %get-tuple-element.106.refs_5_), channel_id=1, source_target_pairs={{0,4},{1,5},{2,6},{3,7},{4,0},{5,1},{6,2},{7,3},{8,12},{9,13},{10,... | collective-permute-start | bytes 2359304 | tf_op jit(solution)/shard_map/ppermute | solution.py:749
  70.7 28.4 %collective-permute-start.6 = (bf16[4,16,5248]{2,1,0:T(8,128)(2,1)}, bf16[4,16,5248]{2,1,0:T(8,128)(2,1)S(1)}, u32[]{:S(2)}, u32[]{:S(2)}) collective-permute-start(bf16[4,16,5248]{2,1,0:T(8,128)(2,1)} %get-tuple-element.102), channel_id=1, source_target_pairs={{0,4},{1,5},{2,6},{3,7},{4,0},{5,1},{6,2},{7,3},{8,12},{9,13},{10,... | collective-permute-start | bytes 2015240 | tf_op jit(solution)/shard_map/ppermute | solution.py:749
  72.7 26.5 %collective-permute-start.7 = (bf16[4,16,5248]{2,1,0:T(8,128)(2,1)}, bf16[4,16,5248]{2,1,0:T(8,128)(2,1)}, u32[]{:S(2)}, u32[]{:S(2)}) collective-permute-start(bf16[4,16,5248]{2,1,0:T(8,128)(2,1)} %get-tuple-element.107), channel_id=1, source_target_pairs={{0,2},{1,3},{2,0},{3,1},{4,6},{5,7},{6,4},{7,5},{8,10},{9,11},{10,... | collective-permute-start | bytes 2015240 | tf_op jit(solution)/shard_map/ppermute | solution.py:749
  103.0 31.9 %collective-permute-start.11 = (bf16[2,4,16,5248]{3,2,1,0:T(8,128)(2,1)S(1)}, bf16[2,4,16,5248]{3,2,1,0:T(8,128)(2,1)}, u32[]{:S(2)}, u32[]{:S(2)}) collective-permute-start(bf16[2,4,16,5248]{3,2,1,0:T(8,128)(2,1)S(1)} %pad_maximum_fusion.2.refs_5_), channel_id=1, source_target_pairs={{0,1},{1,0},{2,3},{3,2},{4,5},{5,4},{6,7},{7,6},{8,9},{9,8},{10,11... | collective-permute-start | bytes 4030472 | tf_op jit(solution)/shard_map/ppermute | solution.py:749
  103.1 32.0 %collective-permute-start.9 = (bf16[2,4,16,5248]{3,2,1,0:T(8,128)(2,1)S(1)}, bf16[2,4,16,5248]{3,2,1,0:T(8,128)(2,1)}, u32[]{:S(2)}, u32[]{:S(2)}) collective-permute-start(bf16[2,4,16,5248]{3,2,1,0:T(8,128)(2,1)S(1)} %pad_maximum_fusion.2.refs_5_), channel_id=1, source_target_pairs={{0,4},{1,5},{2,6},{3,7},{4,0},{5,1},{6,2},{7,3},{8,12},{9,13},{10,... | collective-permute-start | bytes 4030472 | tf_op jit(solution)/shard_map/ppermute | solution.py:749
  104.8 30.3 %collective-permute-start.10 = (bf16[2,4,16,5248]{3,2,1,0:T(8,128)(2,1)}, bf16[2,4,16,5248]{3,2,1,0:T(8,128)(2,1)}, u32[]{:S(2)}, u32[]{:S(2)}) collective-permute-start(bf16[2,4,16,5248]{3,2,1,0:T(8,128)(2,1)} %pad_maximum_fusion.1.refs_3_), channel_id=1, source_target_pairs={{0,1},{1,0},{2,3},{3,2},{4,5},{5,4},{6,7},{7,6},{8,9},{9,8},{10,11... | collective-permute-start | bytes 4030472 | tf_op jit(solution)/shard_map/ppermute | solution.py:749
  105.1 31.9 %collective-permute-start.8 = (bf16[2,4,16,5248]{3,2,1,0:T(8,128)(2,1)}, bf16[2,4,16,5248]{3,2,1,0:T(8,128)(2,1)}, u32[]{:S(2)}, u32[]{:S(2)}) collective-permute-start(bf16[2,4,16,5248]{3,2,1,0:T(8,128)(2,1)} %pad_maximum_fusion.1.refs_3_), channel_id=1, source_target_pairs={{0,2},{1,3},{2,0},{3,1},{4,6},{5,7},{6,4},{7,5},{8,10},{9,11},{10,... | collective-permute-start | bytes 4030472 | tf_op jit(solution)/shard_map/ppermute | solution.py:749
  139.3 25.1 %collective-permute-start.16 = (bf16[2,4,64,1024]{3,2,1,0:T(8,128)(2,1)S(1)}, bf16[2,4,64,1024]{3,2,1,0:T(8,128)(2,1)S(1)}, u32[]{:S(2)}, u32[]{:S(2)}) collective-permute-start(bf16[2,4,64,1024]{3,2,1,0:T(8,128)(2,1)S(1)} %get-tuple-element.226.refs_5_), channel_id=1, source_target_pairs={{0,2},{1,3},{2,0},{3,1},{4,6},{5,7},{6,4},{7,5},{8,10},{9,11},{10,... | collective-permute-start | bytes 3145736 | tf_op jit(solution)/shard_map/ppermute | solution.py:749
  141.1 25.6 %collective-permute-start.18 = (bf16[2,4,64,1024]{3,2,1,0:T(8,128)(2,1)S(1)}, bf16[2,4,64,1024]{3,2,1,0:T(8,128)(2,1)S(1)}, u32[]{:S(2)}, u32[]{:S(2)}) collective-permute-start(bf16[2,4,64,1024]{3,2,1,0:T(8,128)(2,1)S(1)} %get-tuple-element.226.refs_5_), channel_id=1, source_target_pairs={{0,1},{1,0},{2,3},{3,2},{4,5},{5,4},{6,7},{7,6},{8,9},{9,8},{10,11... | collective-permute-start | bytes 3145736 | tf_op jit(solution)/shard_map/ppermute | solution.py:749
  141.1 25.6 %collective-permute-start.17 = (bf16[2,4,64,1024]{3,2,1,0:T(8,128)(2,1)S(1)}, bf16[2,4,64,1024]{3,2,1,0:T(8,128)(2,1)S(1)}, u32[]{:S(2)}, u32[]{:S(2)}) collective-permute-start(bf16[2,4,64,1024]{3,2,1,0:T(8,128)(2,1)S(1)} %get-tuple-element.225.refs_7_), channel_id=1, source_target_pairs={{0,4},{1,5},{2,6},{3,7},{4,0},{5,1},{6,2},{7,3},{8,12},{9,13},{10,... | collective-permute-start | bytes 3145736 | tf_op jit(solution)/shard_map/ppermute | solution.py:749
  142.9 23.8 %collective-permute-start.19 = (bf16[2,4,64,1024]{3,2,1,0:T(8,128)(2,1)S(1)}, bf16[2,4,64,1024]{3,2,1,0:T(8,128)(2,1)S(1)}, u32[]{:S(2)}, u32[]{:S(2)}) collective-permute-start(bf16[2,4,64,1024]{3,2,1,0:T(8,128)(2,1)S(1)} %get-tuple-element.225.refs_7_), channel_id=1, source_target_pairs={{0,1},{1,0},{2,3},{3,2},{4,5},{5,4},{6,7},{7,6},{8,9},{9,8},{10,11... | collective-permute-start | bytes 3145736 | tf_op jit(solution)/shard_map/ppermute | solution.py:749
  188.6 31.5 %all-to-all-start.1 = ((bf16[4,128,1024]{2,1,0:T(8,128)(2,1)}), bf16[4,128,1024]{2,1,0:T(8,128)(2,1)S(1)}, u32[]{:S(2)}, u32[]{:S(2)}) async-start(bf16[4,128,1024]{2,1,0:T(8,128)(2,1)} %bitcast.76), calls=%async_computation.1 | async-start | bytes 2097152 | tf_op jit(solution)/shard_map/all_to_all | solution.py:849
  192.1 131.9 %reduce-scatter.4.cloned.1.call-start = ((), (), s32[]{:S(2)}) async-start(), calls=%async_computation.6 | async-start | bytes 2621440 | tf_op jit(solution)/shard_map/reduce_scatter | solution.py:952
  234.4 28.9 %collective-permute-start.25 = (bf16[16,32,5248]{2,1,0:T(8,128)(2,1)S(1)}, bf16[16,32,5248]{2,1,0:T(8,128)(2,1)S(1)}, u32[]{:S(2)}, u32[]{:S(2)}) collective-permute-start(bf16[16,32,5248]{2,1,0:T(8,128)(2,1)S(1)} %get-tuple-element.153), channel_id=1, source_target_pairs={{0,1},{1,0},{2,3},{3,2},{4,5},{5,4},{6,7},{7,6},{8,9},{9,8},{10,11... | collective-permute-start | bytes 16121864 | tf_op jit(solution)/shard_map/ppermute | solution.py:749
  234.6 25.4 %collective-permute-start.26 = (bf16[4,2,64,1024]{3,2,1,0:T(8,128)(2,1)S(1)}, bf16[4,2,64,1024]{3,2,1,0:T(8,128)(2,1)S(1)}, u32[]{:S(2)}, u32[]{:S(2)}) collective-permute-start(bf16[4,2,64,1024]{3,2,1,0:T(8,128)(2,1)S(1)} %get-tuple-element.156), channel_id=1, source_target_pairs={{0,2},{1,3},{2,0},{3,1},{4,6},{5,7},{6,4},{7,5},{8,10},{9,11},{10,... | collective-permute-start | bytes 3145736 | tf_op jit(solution)/shard_map/ppermute | solution.py:749
  236.5 24.9 %collective-permute-start.27 = (bf16[4,2,64,1024]{3,2,1,0:T(8,128)(2,1)S(1)}, bf16[4,2,64,1024]{3,2,1,0:T(8,128)(2,1)S(1)}, u32[]{:S(2)}, u32[]{:S(2)}) collective-permute-start(bf16[4,2,64,1024]{3,2,1,0:T(8,128)(2,1)S(1)} %get-tuple-element.157), channel_id=1, source_target_pairs={{0,4},{1,5},{2,6},{3,7},{4,0},{5,1},{6,2},{7,3},{8,12},{9,13},{10,... | collective-permute-start | bytes 3145736 | tf_op jit(solution)/shard_map/ppermute | solution.py:749
  268.3 30.7 %collective-permute-start.28 = (bf16[4,2,16,5248]{3,2,1,0:T(8,128)(2,1)}, bf16[4,2,16,5248]{3,2,1,0:T(8,128)(2,1)}, u32[]{:S(2)}, u32[]{:S(2)}) collective-permute-start(bf16[4,2,16,5248]{3,2,1,0:T(8,128)(2,1)} %get-tuple-element.165), channel_id=1, source_target_pairs={{0,2},{1,3},{2,0},{3,1},{4,6},{5,7},{6,4},{7,5},{8,10},{9,11},{10,... | collective-permute-start | bytes 4030472 | tf_op jit(solution)/shard_map/ppermute | solution.py:749
  269.0 30.7 %collective-permute-start.29 = (bf16[4,2,16,5248]{3,2,1,0:T(8,128)(2,1)}, bf16[4,2,16,5248]{3,2,1,0:T(8,128)(2,1)}, u32[]{:S(2)}, u32[]{:S(2)}) collective-permute-start(bf16[4,2,16,5248]{3,2,1,0:T(8,128)(2,1)} %get-tuple-element.167), channel_id=1, source_target_pairs={{0,4},{1,5},{2,6},{3,7},{4,0},{5,1},{6,2},{7,3},{8,12},{9,13},{10,... | collective-permute-start | bytes 4030472 | tf_op jit(solution)/shard_map/ppermute | solution.py:749
  270.7 90.9 %reduce-scatter.6.cloned.1.call-start = ((), (), s32[]{:S(2)}) async-start(), calls=%async_computation.7 | async-start | bytes 1679360 | tf_op jit(solution)/shard_map/reduce_scatter | solution.py:968
  305.5 15.2 %collective-permute-start.30 = (bf16[16,32,3072]{2,1,0:T(8,128)(2,1)S(1)}, bf16[16,32,3072]{2,1,0:T(8,128)(2,1)S(1)}, u32[]{:S(2)}, u32[]{:S(2)}) collective-permute-start(bf16[16,32,3072]{2,1,0:T(8,128)(2,1)S(1)} %get-tuple-element.173), channel_id=1, source_target_pairs={{0,1},{1,0},{2,3},{3,2},{4,5},{5,4},{6,7},{7,6},{8,9},{9,8},{10,11... | collective-permute-start | bytes 9437192 | tf_op jit(solution)/shard_map/ppermute | solution.py:749
  326.8 19.5 %collective-permute-start.33 = (bf16[4,2,16,3072]{3,2,1,0:T(8,128)(2,1)}, bf16[4,2,16,3072]{3,2,1,0:T(8,128)(2,1)S(1)}, u32[]{:S(2)}, u32[]{:S(2)}) collective-permute-start(bf16[4,2,16,3072]{3,2,1,0:T(8,128)(2,1)} %get-tuple-element.182), channel_id=1, source_target_pairs={{0,2},{1,3},{2,0},{3,1},{4,6},{5,7},{6,4},{7,5},{8,10},{9,11},{10,... | collective-permute-start | bytes 2359304 | tf_op jit(solution)/shard_map/ppermute | solution.py:749
  327.5 18.8 %collective-permute-start.34 = (bf16[4,2,16,3072]{3,2,1,0:T(8,128)(2,1)}, bf16[4,2,16,3072]{3,2,1,0:T(8,128)(2,1)S(1)}, u32[]{:S(2)}, u32[]{:S(2)}) collective-permute-start(bf16[4,2,16,3072]{3,2,1,0:T(8,128)(2,1)} %copy-done.16), channel_id=1, source_target_pairs={{0,4},{1,5},{2,6},{3,7},{4,0},{5,1},{6,2},{7,3},{8,12},{9,13},{10,... | collective-permute-start | bytes 2359304 | tf_op jit(solution)/shard_map/ppermute | solution.py:749
  327.9 60.2 %reduce-scatter.8.cloned.1.call-start = ((), (), s32[]{:S(2)}) async-start(), calls=%async_computation.8 | async-start | bytes 983040 | tf_op jit(solution)/shard_map/reduce_scatter | solution.py:988
  329.1 17.2 %collective-permute-start.35 = (bf16[64,1024]{1,0:T(8,128)(2,1)S(1)}, bf16[64,1024]{1,0:T(8,128)(2,1)S(1)}, u32[]{:S(2)}, u32[]{:S(2)}) collective-permute-start(bf16[64,1024]{1,0:T(8,128)(2,1)S(1)} %dynamic-slice_bitcast_fusion.1), channel_id=1, source_target_pairs={{0,4},{1,5},{2,6},{3,7},{4,0},{5,1},{6,2},{7,3},{8,12},{9,13},{10,... | collective-permute-start | bytes 393224 | tf_op jit(solution)/shard_map/ppermute | solution.py:749
  330.8 15.5 %collective-permute-start.36 = (bf16[64,1024]{1,0:T(8,128)(2,1)S(1)}, bf16[64,1024]{1,0:T(8,128)(2,1)S(1)}, u32[]{:S(2)}, u32[]{:S(2)}) collective-permute-start(bf16[64,1024]{1,0:T(8,128)(2,1)S(1)} %dynamic-slice_bitcast_fusion), channel_id=1, source_target_pairs={{0,2},{1,3},{2,0},{3,1},{4,6},{5,7},{6,4},{7,5},{8,10},{9,11},{10,... | collective-permute-start | bytes 393224 | tf_op jit(solution)/shard_map/ppermute | solution.py:749
  364.2 18.0 %all-to-all-start.2 = ((bf16[4,128,1024]{2,1,0:T(8,128)(2,1)}), bf16[4,128,1024]{2,1,0:T(8,128)(2,1)S(1)}, u32[]{:S(2)}, u32[]{:S(2)}) async-start(bf16[4,128,1024]{2,1,0:T(8,128)(2,1)} %bitcast.37), calls=%async_computation.4 | async-start | bytes 2097152 | tf_op jit(solution)/shard_map/all_to_all | solution.py:849
  (66 other events, 426.6 us)
Sparse Core Ops, SparseCore 0:
  22.7 38.9 all-gather.5
  73.9 46.1 all-gather.7
  270.9 44.1 reduce-scatter.3
  328.1 33.0 reduce-scatter.5
  363.5 24.6 reduce-scatter.7

commit v5 on v4

--- a/solution.py
+++ b/solution.py
@@ -848,7 +848,6 @@
     slab, ff_slab = up_weight.shape[0], down_weight.shape[0]
     exchange = lambda v: lax.all_to_all(v, GROUP, split_axis=0, concat_axis=0, tiled=True)
     to_sequence = lambda v: exchange(v).reshape(full_len, width)
-    to_positions = lambda v: exchange(v.reshape(seqs_here, local_len, width))
     own_lengths = lax.dynamic_slice_in_dim(doc_lengths, place, 1, 0)
     seg_row = segments_of(own_lengths, full_len)
     seg_col = seg_row.reshape(full_len, 1)
@@ -916,7 +915,6 @@
 
     low = lambda *v: sum_of(v).astype(jnp.bfloat16)
     place_xy = jnp.stack([x, y])
-    layer_out = to_positions(result)
     down_kept, down_sent, up_kept, up_sent, grad_first_in, grad_branch, norms_one = ffn_back(
         core,
         act,
@@ -933,7 +931,7 @@
         ff_slab,
     )
 
-    down_sent, grad_branch = gate((down_sent, grad_branch), (layer_out,))
+    down_sent, grad_branch = gate((down_sent, grad_branch))
     down_came = send(down_sent, ROUTE_C)
     grad_context, up_kept, up_sent = out_grad(
         core, context, grad_branch, w_up, norms_one, norms_two, up_kept, up_sent
@@ -983,8 +981,11 @@
     )
 
     last_blocks = jnp.concatenate([low(la_own, la_in2), low(lb_own, lb_in2)], axis=1)
-    last_blocks, grad_tokens, up_sum = gate((last_blocks, grad_tokens, up_sum), (), 1)
-    input_grad = to_positions(grad_tokens)
+    as_blocks = lambda v: v.reshape(seqs_here, local_len, width)
+    packed = side_by_side(as_blocks(result), as_blocks(grad_tokens), ())
+    last_blocks, packed, up_sum = gate((last_blocks, packed, up_sum), (), 1)
+    returned = exchange(packed)
+    layer_out, input_grad = returned[:, :local_len], returned[:, local_len:]
     last_sum = lax.psum_scatter(
         last_blocks, "dp", scatter_dimension=0, axis_index_groups=LINES, tiled=False
     )

time: 399 us -> 403 us (1.010)
  waiting for transfers between devices: 110 us -> 116 us
  starting transfers between devices: 45.7 us -> 41 us
    all_to_all x3 -> x2, waiting for transfers between devices: 12.3 us -> 22.6 us  [body_lines(): lax.all_to_all(v, GROUP, split_axis=0, concat_axis=0, tiled=True)]
    reduce_scatter x1, waiting for transfers between devices: 4.41 us -> 0.01 us  [body_lines(): lax.psum_scatter(last_blocks, 'dp', scatter_dimension=0, axis_index_group...]
    pallas_call x28 -> x29, Pallas kernels: 145 us -> 149 us  [run(): return pl.pallas_call(body, grid_spec=spec, **rest)(*operands, *after)]
    all_to_all x3 -> x2, starting transfers between devices: 10.8 us -> 8.33 us  [body_lines(): lax.all_to_all(v, GROUP, split_axis=0, concat_axis=0, tiled=True)]
    unnamed x105 -> x110, local copies, waits for them, and re-layouts: 19.6 us -> 19.8 us
  transfers between devices with their start and end apart: 47 -> 46, of which waited for: 22 -> 21; matrix products, arithmetic and copies ran while one was open for 9% -> 9% of each run, Pallas kernels for 31% -> 25%
where the time goes in v5:
time: 403 us; the launch traced here: 402 us
  Pallas kernels  149 us (37%)
  waiting for transfers between devices  116 us (29%)
  starting transfers between devices  41 us (10%)
  local copies, waits for them, and re-layouts  32 us (8%)
  blocking collectives  25.1 us (6%)
  other arithmetic  24.8 us (6%)
  between operations  14.4 us (4%)
    pallas_call x29, Pallas kernels, run(): return pl.pallas_call(body, grid_spec=spec, **rest)(*operands, *after)  149 us
    ppermute x39, waiting for transfers between devices, send(): return lax.ppermute(value, ALL, route)  93 us
    ppermute x39, starting transfers between devices, send(): return lax.ppermute(value, ALL, route)  32.5 us
    all_gather x1, blocking collectives, body_lines(): line = lambda v: lax.all_gather(v, 'dp', axis_index_groups=LINES)  25.1 us
    all_to_all x2, waiting for transfers between devices, body_lines(): lax.all_to_all(v, GROUP, split_axis=0, concat_axis=0, tiled=True)  22.6 us
    unnamed x110, local copies, waits for them, and re-layouts  19.8 us
    all_to_all x2, starting transfers between devices, body_lines(): lax.all_to_all(v, GROUP, split_axis=0, concat_axis=0, tiled=True)  8.33 us
  transfers between devices with their start and end apart: 46, of which 21 were waited for; matrix products, arithmetic and copies ran while one was open for 9% of the time, Pallas kernels for 25%

profile of v5, /device:TPU:0, one launch (start us, length us, event | category | flops | bytes accessed | tf_op | source)
XLA Modules:
  0.0 401.9 jit_solution(18401007090298427082)
XLA Ops:
  8.2 3.0 collective-permute-start
  12.7 3.8 shard_map.135
  16.5 3.8 all-to-all-start
  21.5 25.1 %all-gather.1 = bf16[128,3072]{1,0:T(8,128)(2,1)S(1)} all-gather(bf16[32,3072]{1,0:T(8,128)(2,1)S(1)} %copy-done.49), channel_id=3, replica_groups={{0,8,16,24},{4,12,20,28},{1,9,17,25},{5,13,21,29},{2,10,18,26},{6,14,22..., dimensions={0}, use_global_device_ids=true | all-gather | bytes 983040 | tf_op jit(solution)/shard_map/all_gather | solution.py:856
  55.5 7.9 %collective-permute-done.3 = bf16[4,16,3072]{2,1,0:T(8,128)(2,1)S(1)} collective-permute-done((bf16[4,16,3072]{2,1,0:T(8,128)(2,1)}, bf16[4,16,3072]{2,1,0:T(8,128)(2,1)S(1)}, u32[]{:S(2)}, u32[]{:S(2)}) %collective-permute-start.3) | collective-permute-done | bytes 393248 | tf_op jit(solution)/shard_map/ppermute | solution.py:749
  68.2 2.5 fusion.8
  73.9 25.2 %collective-permute-done.6.refs_2_ = bf16[4,16,5248]{2,1,0:T(8,128)(2,1)S(1)} collective-permute-done((bf16[4,16,5248]{2,1,0:T(8,128)(2,1)}, bf16[4,16,5248]{2,1,0:T(8,128)(2,1)S(1)}, u32[]{:S(2)}, u32[]{:S(2)}) %collective-permute-start.6) | collective-permute-done | bytes 671776 | tf_op jit(solution)/shard_map/ppermute | solution.py:749
  112.2 9.2 %shard_map.140 = (bf16[512,3072]{1,0:T(8,128)(2,1)}, bf16[1024,3072]{1,0:T(8,128)(2,1)}) custom-call(s32[64]{0:T(128)} %concatenate.23.refs_0_, bf16[512,1024]{1,0:T(8,128)(2,1)} %bitcast.64, bf16[2,4,16,3072]{3,2,1,0:T(8,128)(2,1)} %get-tuple-element.111.refs_2_, bf16[2,4,16,3072]{3,2,1,0:T(8,128)(2,1)} %get-tuple-element.112.refs_3_, ...), custom_call_target="tpu_custom_call" | custom-call | flops 1 | bytes 1 | tf_op jit(solution)/shard_map/pallas_call | solution.py:40
  121.4 13.5 %shard_map.141 = (bf16[512,1024]{1,0:T(8,128)(2,1)}, f32[8,2,512]{2,1,0:T(2,128)}) custom-call(bf16[512,3072]{1,0:T(8,128)(2,1)} %get-tuple-element.115.refs_0_.refs_1_.refs_2_, bf16[512,3072]{1,0:T(8,128)(2,1)} %get-tuple-element.115.refs_0_.refs_1_.refs_2_, bf16[512,3072]{1,0:T(8,128)(2,1)} %get-tuple-element.115.refs_0_.refs_1_.refs_2_, ...), custom_call_target="tpu_custom_call" | custom-call | flops 1 | bytes 1 | tf_op jit(solution)/shard_map/pallas_call | solution.py:40
  144.0 18.3 %shard_map.143 = (f32[512,1024]{1,0:T(8,128)}, f32[512,1]{1,0:T(8,128)}, bf16[512,1024]{1,0:T(8,128)(2,1)}, f32[8,1024]{1,0:T(8,128)}, bf16[512,4096]{1,0:T(8,12...) custom-call(s32[64]{0:T(128)} %concatenate.23.refs_0_, bf16[512,1024]{1,0:T(8,128)(2,1)} %get-tuple-element.117.refs_1_, ...), custom_call_target="tpu_custom_call" | custom-call | flops 1 | bytes 1 | tf_op jit(solution)/shard_map/pallas_call | solution.py:40
  162.3 2.2 collective-permute-done.16.refs_0_
  164.5 2.2 collective-permute-done.17.refs_1_
  174.4 14.2 %shard_map.145 = (bf16[512,1024]{1,0:T(8,128)(2,1)}, f32[512,1024]{1,0:T(8,128)}, bf16[512,1024]{1,0:T(8,128)(2,1)}, f32[2,1024]{1,0:T(2,128)}, bf16[4096,1024]{1,0:T(8,128)(2,1)}) custom-call(s32[64]{0:T(128)} %concatenate.24.refs_0_, bf16[512,4096]{1,0:T(8,128)(2,1)} %get-tuple-element.124.refs_1_, f32[512,1024]{1,0:T(8,128)} %get-tuple-element.126.refs_2_.refs_8_, ...), custom_call_target="tpu_custom_call" | custom-call | flops 1 | bytes 1 | tf_op jit(solution)/shard_map/pallas_call | solution.py:40
  188.6 27.9 %shard_map.146 = (bf16[16,128,1024]{2,1,0:T(8,128)(2,1)}, bf16[16,128,1024]{2,1,0:T(8,128)(2,1)}, bf16[16,32,5248]{2,1,0:T(8,128)(2,1)}, bf16[16,32,5248]{2,1,0:...) custom-call(s32[1]{0:T(128)} %bitcast.2.refs_0_, ...), custom_call_target="tpu_custom_call" | custom-call | flops 1 | bytes 1 | tf_op jit(solution)/shard_map/pallas_call | solution.py:40
  216.8 7.2 %shard_map.148 = (bf16[512,1024]{1,0:T(8,128)(2,1)}, bf16[16,32,5248]{2,1,0:T(8,128)(2,1)}, bf16[16,32,5248]{2,1,0:T(8,128)(2,1)}) custom-call(s32[1]{0:T(128)} %bitcast.2.refs_0_, bf16[512,1024]{1,0:T(8,128)(2,1)} %get-tuple-element.117.refs_1_, bf16[512,1024]{1,0:T(8,128)(2,1)} %get-tuple-element.140.refs_2_, ...), custom_call_target="tpu_custom_call", output_to_operand_aliasing={{1}: (6, {}), {2}: (7, {})} | custom-call | flops 1 | bytes 1 | tf_op jit(solution)/shard_map/pallas_call | solution.py:40
  225.3 4.2 %shard_map.149 = (bf16[4,2,64,1024]{3,2,1,0:T(8,128)(2,1)S(1)}, bf16[4,2,64,1024]{3,2,1,0:T(8,128)(2,1)S(1)}, bf16[4,2,64,1024]{3,2,1,0:T(8,128)(2,1)S(1)}, bf16[4,2,64,1024]{3,2,1,0:T(8,128)(2,1)S(1)}) custom-call(s32[2]{0:T(128)S(1)} %pad_add_fusion.refs_0_, bf16[4,2,2,128,1024]{4,3,2,1,0:T(8,128)(2,1)S(1)} %bitcast.58, ...), custom_call_target="tpu_custom_call" | custom-call | flops 1 | bytes 1 | tf_op jit(solution)/shard_map/pallas_call | solution.py:40
  232.1 19.3 %shard_map.151.refs_3_ = bf16[3,512,1024]{2,1,0:T(8,128)(2,1)S(1)} custom-call(bf16[512,3072]{1,0:T(8,128)(2,1)S(1)} %copy-done.2, bf16[512,3072]{1,0:T(8,128)(2,1)S(1)} %copy-done.2, bf16[512,3072]{1,0:T(8,128)(2,1)S(1)} %copy-done.2, bf16[512,1024]{1,0:T(8,128)(2,1)S(1)} %get-tuple-element.153.refs_3_, s32[512,1]{1,0:T(8,128)S(1)} %copy-done.12, ...), custom_call_target="tpu_custom_call" | custom-call | flops 1 | bytes 1 | tf_op jit(solution)/shard_map/pallas_call | solution.py:40
  251.4 3.9 collective-permute-done.26.refs_4_
  257.7 3.1 shard_map.152
  265.6 8.9 %shard_map.154 = (bf16[16,32,3072]{2,1,0:T(8,128)(2,1)}, bf16[16,32,3072]{2,1,0:T(8,128)(2,1)}) custom-call(s32[1]{0:T(128)} %bitcast.2.refs_0_, bf16[512,1024]{1,0:T(8,128)(2,1)} %bitcast.66, bf16[3,512,1024]{2,1,0:T(8,128)(2,1)} %copy-done.3), custom_call_target="tpu_custom_call" | custom-call | flops 1 | bytes 1 | tf_op jit(solution)/shard_map/pallas_call | solution.py:40
  274.5 8.3 %shard_map.155.refs_5_.refs_2_ = bf16[512,1024]{1,0:T(8,128)(2,1)} custom-call(bf16[3,512,1024]{2,1,0:T(8,128)(2,1)} %copy-done.3, bf16[1024,3072]{1,0:T(8,128)(2,1)} %get-tuple-element.167.refs_1_, f32[512,1024]{1,0:T(8,128)} %get-tuple-element.168.refs_2_, bf16[16,32,3072]{2,1,0:T(8,128)(2,1)} %get-tuple-element.169.refs_3_.refs_2_), custom_call_target="tpu_custom_call" | custom-call | flops 1 | bytes 1 | tf_op jit(solution)/shard_map/pallas_call | solution.py:40
  282.8 10.8 %collective-permute-done.28.refs_2_ = bf16[4,2,16,5248]{3,2,1,0:T(8,128)(2,1)} collective-permute-done((bf16[4,2,16,5248]{3,2,1,0:T(8,128)(2,1)}, bf16[4,2,16,5248]{3,2,1,0:T(8,128)(2,1)}, u32[]{:S(2)}, u32[]{:S(2)}) %collective-permute-start.28) | collective-permute-done | bytes 1343520 | tf_op jit(solution)/shard_map/ppermute | solution.py:749
  295.5 2.9 shard_map.156
  301.3 12.1 %collective-permute-done.31.refs_3_ = bf16[4,16,5248]{2,1,0:T(8,128)(2,1)S(1)} collective-permute-done((bf16[4,16,5248]{2,1,0:T(8,128)(2,1)S(1)}, bf16[4,16,5248]{2,1,0:T(8,128)(2,1)S(1)}, u32[]{:S(2)}, u32[]{:S(2)}) %collective-permute-start.31) | collective-permute-done | bytes 671776 | tf_op jit(solution)/shard_map/ppermute | solution.py:749
  317.2 2.3 shard_map.158
  327.6 15.1 %collective-permute-done.35.refs_5_ = bf16[64,1024]{1,0:T(8,128)(2,1)S(1)} collective-permute-done((bf16[64,1024]{1,0:T(8,128)(2,1)S(1)}, bf16[64,1024]{1,0:T(8,128)(2,1)S(1)}, u32[]{:S(2)}, u32[]{:S(2)}) %collective-permute-start.35) | collective-permute-done | bytes 131104 | tf_op jit(solution)/shard_map/ppermute | solution.py:749
  342.8 2.0 shard_map.160
  349.4 3.8 shard_map.162.refs_1_
  353.2 2.0 collective-permute-done.37
  359.8 4.6 %all-to-all-start.1 = ((bf16[4,256,1024]{2,1,0:T(8,128)(2,1)}), bf16[4,256,1024]{2,1,0:T(8,128)(2,1)}, u32[]{:S(2)}, u32[]{:S(2)}) async-start(bf16[4,256,1024]{2,1,0:T(8,128)(2,1)} %get-tuple-element.194), calls=%async_computation.3 | async-start | bytes 4194304 | tf_op jit(solution)/shard_map/all_to_all | solution.py:849
  367.5 22.6 %all-to-all-done.1 = bf16[4,256,1024]{2,1,0:T(8,128)(2,1)} async-done(((bf16[4,256,1024]{2,1,0:T(8,128)(2,1)}), bf16[4,256,1024]{2,1,0:T(8,128)(2,1)}, u32[]{:S(2)}, u32[]{:S(2)}) %all-to-all-start.1) | async-done | bytes 2097184 | tf_op jit(solution)/shard_map/all_to_all | solution.py:849
  390.1 3.5 slice_convert_fusion
  (270 shorter events, 92.0 us)
Async XLA Ops:
  8.2 42.8 %collective-permute-start = (bf16[64,1024]{1,0:T(8,128)(2,1)S(1)}, bf16[64,1024]{1,0:T(8,128)(2,1)S(1)}, u32[]{:S(2)}, u32[]{:S(2)}) collective-permute-start(bf16[64,1024]{1,0:T(8,128)(2,1)S(1)} %get-tuple-element.240), channel_id=1, source_target_pairs={{0,4},{1,5},{2,6},{3,7},{4,0},{5,1},{6,2},{7,3},{8,12},{9,13},{10,... | collective-permute-start | bytes 393224 | tf_op jit(solution)/shard_map/ppermute | solution.py:749
  11.2 39.8 %collective-permute-start.1 = (bf16[64,1024]{1,0:T(8,128)(2,1)S(1)}, bf16[64,1024]{1,0:T(8,128)(2,1)S(1)}, u32[]{:S(2)}, u32[]{:S(2)}) collective-permute-start(bf16[64,1024]{1,0:T(8,128)(2,1)S(1)} %get-tuple-element.239), channel_id=1, source_target_pairs={{0,2},{1,3},{2,0},{3,1},{4,6},{5,7},{6,4},{7,5},{8,10},{9,11},{10,... | collective-permute-start | bytes 393224 | tf_op jit(solution)/shard_map/ppermute | solution.py:749
  16.5 35.4 %all-to-all-start = ((bf16[4,256,1024]{2,1,0:T(8,128)(2,1)}), bf16[4,256,1024]{2,1,0:T(8,128)(2,1)S(1)}, u32[]{:S(2)}, u32[]{:S(2)}) async-start(bf16[4,256,1024]{2,1,0:T(8,128)(2,1)} %shard_map.135), calls=%async_computation | async-start | bytes 4194304 | tf_op jit(solution)/shard_map/all_to_all | solution.py:849
  20.3 47.9 %all-gather.6.cloned.1.call-start = ((), (), s32[]{:S(2)}) async-start(), calls=%async_computation.8 | async-start | bytes 1679360 | tf_op jit(solution)/shard_map/all_gather | solution.py:856
  53.5 83.5 %all-gather.8.cloned.1.call-start = ((), (), s32[]{:S(2)}) async-start(), calls=%async_computation.9 | async-start | bytes 2621440 | tf_op jit(solution)/shard_map/all_gather | solution.py:856
  67.3 32.0 %collective-permute-start.4 = (bf16[2,4,16,3072]{3,2,1,0:T(8,128)(2,1)}, bf16[2,4,16,3072]{3,2,1,0:T(8,128)(2,1)S(1)}, u32[]{:S(2)}, u32[]{:S(2)}) collective-permute-start(bf16[2,4,16,3072]{3,2,1,0:T(8,128)(2,1)} %get-tuple-element.105.refs_4_), channel_id=1, source_target_pairs={{0,2},{1,3},{2,0},{3,1},{4,6},{5,7},{6,4},{7,5},{8,10},{9,11},{10,... | collective-permute-start | bytes 2359304 | tf_op jit(solution)/shard_map/ppermute | solution.py:749
  68.2 31.0 %collective-permute-start.5 = (bf16[2,4,16,3072]{3,2,1,0:T(8,128)(2,1)}, bf16[2,4,16,3072]{3,2,1,0:T(8,128)(2,1)S(1)}, u32[]{:S(2)}, u32[]{:S(2)}) collective-permute-start(bf16[2,4,16,3072]{3,2,1,0:T(8,128)(2,1)} %get-tuple-element.106.refs_5_), channel_id=1, source_target_pairs={{0,4},{1,5},{2,6},{3,7},{4,0},{5,1},{6,2},{7,3},{8,12},{9,13},{10,... | collective-permute-start | bytes 2359304 | tf_op jit(solution)/shard_map/ppermute | solution.py:749
  70.7 28.4 %collective-permute-start.6 = (bf16[4,16,5248]{2,1,0:T(8,128)(2,1)}, bf16[4,16,5248]{2,1,0:T(8,128)(2,1)S(1)}, u32[]{:S(2)}, u32[]{:S(2)}) collective-permute-start(bf16[4,16,5248]{2,1,0:T(8,128)(2,1)} %get-tuple-element.102), channel_id=1, source_target_pairs={{0,4},{1,5},{2,6},{3,7},{4,0},{5,1},{6,2},{7,3},{8,12},{9,13},{10,... | collective-permute-start | bytes 2015240 | tf_op jit(solution)/shard_map/ppermute | solution.py:749
  72.7 26.5 %collective-permute-start.7 = (bf16[4,16,5248]{2,1,0:T(8,128)(2,1)}, bf16[4,16,5248]{2,1,0:T(8,128)(2,1)}, u32[]{:S(2)}, u32[]{:S(2)}) collective-permute-start(bf16[4,16,5248]{2,1,0:T(8,128)(2,1)} %get-tuple-element.107), channel_id=1, source_target_pairs={{0,2},{1,3},{2,0},{3,1},{4,6},{5,7},{6,4},{7,5},{8,10},{9,11},{10,... | collective-permute-start | bytes 2015240 | tf_op jit(solution)/shard_map/ppermute | solution.py:749
  73.8 245.7 %reduce-scatter.4.cloned.1.call-start = ((), (), s32[]{:S(2)}) async-start(), calls=%async_computation.5 | async-start | bytes 2621440 | tf_op jit(solution)/shard_map/reduce_scatter | solution.py:950
  103.0 31.9 %collective-permute-start.11 = (bf16[2,4,16,5248]{3,2,1,0:T(8,128)(2,1)S(1)}, bf16[2,4,16,5248]{3,2,1,0:T(8,128)(2,1)}, u32[]{:S(2)}, u32[]{:S(2)}) collective-permute-start(bf16[2,4,16,5248]{3,2,1,0:T(8,128)(2,1)S(1)} %pad_maximum_fusion.2.refs_5_), channel_id=1, source_target_pairs={{0,1},{1,0},{2,3},{3,2},{4,5},{5,4},{6,7},{7,6},{8,9},{9,8},{10,11... | collective-permute-start | bytes 4030472 | tf_op jit(solution)/shard_map/ppermute | solution.py:749
  103.1 32.0 %collective-permute-start.9 = (bf16[2,4,16,5248]{3,2,1,0:T(8,128)(2,1)S(1)}, bf16[2,4,16,5248]{3,2,1,0:T(8,128)(2,1)}, u32[]{:S(2)}, u32[]{:S(2)}) collective-permute-start(bf16[2,4,16,5248]{3,2,1,0:T(8,128)(2,1)S(1)} %pad_maximum_fusion.2.refs_5_), channel_id=1, source_target_pairs={{0,4},{1,5},{2,6},{3,7},{4,0},{5,1},{6,2},{7,3},{8,12},{9,13},{10,... | collective-permute-start | bytes 4030472 | tf_op jit(solution)/shard_map/ppermute | solution.py:749
  104.8 30.3 %collective-permute-start.10 = (bf16[2,4,16,5248]{3,2,1,0:T(8,128)(2,1)}, bf16[2,4,16,5248]{3,2,1,0:T(8,128)(2,1)}, u32[]{:S(2)}, u32[]{:S(2)}) collective-permute-start(bf16[2,4,16,5248]{3,2,1,0:T(8,128)(2,1)} %pad_maximum_fusion.1.refs_3_), channel_id=1, source_target_pairs={{0,1},{1,0},{2,3},{3,2},{4,5},{5,4},{6,7},{7,6},{8,9},{9,8},{10,11... | collective-permute-start | bytes 4030472 | tf_op jit(solution)/shard_map/ppermute | solution.py:749
  105.1 31.9 %collective-permute-start.8 = (bf16[2,4,16,5248]{3,2,1,0:T(8,128)(2,1)}, bf16[2,4,16,5248]{3,2,1,0:T(8,128)(2,1)}, u32[]{:S(2)}, u32[]{:S(2)}) collective-permute-start(bf16[2,4,16,5248]{3,2,1,0:T(8,128)(2,1)} %pad_maximum_fusion.1.refs_3_), channel_id=1, source_target_pairs={{0,2},{1,3},{2,0},{3,1},{4,6},{5,7},{6,4},{7,5},{8,10},{9,11},{10,... | collective-permute-start | bytes 4030472 | tf_op jit(solution)/shard_map/ppermute | solution.py:749
  139.4 25.1 %collective-permute-start.16 = (bf16[2,4,64,1024]{3,2,1,0:T(8,128)(2,1)S(1)}, bf16[2,4,64,1024]{3,2,1,0:T(8,128)(2,1)S(1)}, u32[]{:S(2)}, u32[]{:S(2)}) collective-permute-start(bf16[2,4,64,1024]{3,2,1,0:T(8,128)(2,1)S(1)} %get-tuple-element.228.refs_5_), channel_id=1, source_target_pairs={{0,2},{1,3},{2,0},{3,1},{4,6},{5,7},{6,4},{7,5},{8,10},{9,11},{10,... | collective-permute-start | bytes 3145736 | tf_op jit(solution)/shard_map/ppermute | solution.py:749
  141.2 25.6 %collective-permute-start.18 = (bf16[2,4,64,1024]{3,2,1,0:T(8,128)(2,1)S(1)}, bf16[2,4,64,1024]{3,2,1,0:T(8,128)(2,1)S(1)}, u32[]{:S(2)}, u32[]{:S(2)}) collective-permute-start(bf16[2,4,64,1024]{3,2,1,0:T(8,128)(2,1)S(1)} %get-tuple-element.228.refs_5_), channel_id=1, source_target_pairs={{0,1},{1,0},{2,3},{3,2},{4,5},{5,4},{6,7},{7,6},{8,9},{9,8},{10,11... | collective-permute-start | bytes 3145736 | tf_op jit(solution)/shard_map/ppermute | solution.py:749
  141.2 25.6 %collective-permute-start.17 = (bf16[2,4,64,1024]{3,2,1,0:T(8,128)(2,1)S(1)}, bf16[2,4,64,1024]{3,2,1,0:T(8,128)(2,1)S(1)}, u32[]{:S(2)}, u32[]{:S(2)}) collective-permute-start(bf16[2,4,64,1024]{3,2,1,0:T(8,128)(2,1)S(1)} %get-tuple-element.227.refs_7_), channel_id=1, source_target_pairs={{0,4},{1,5},{2,6},{3,7},{4,0},{5,1},{6,2},{7,3},{8,12},{9,13},{10,... | collective-permute-start | bytes 3145736 | tf_op jit(solution)/shard_map/ppermute | solution.py:749
  142.9 23.8 %collective-permute-start.19 = (bf16[2,4,64,1024]{3,2,1,0:T(8,128)(2,1)S(1)}, bf16[2,4,64,1024]{3,2,1,0:T(8,128)(2,1)S(1)}, u32[]{:S(2)}, u32[]{:S(2)}) collective-permute-start(bf16[2,4,64,1024]{3,2,1,0:T(8,128)(2,1)S(1)} %get-tuple-element.227.refs_7_), channel_id=1, source_target_pairs={{0,1},{1,0},{2,3},{3,2},{4,5},{5,4},{6,7},{7,6},{8,9},{9,8},{10,11... | collective-permute-start | bytes 3145736 | tf_op jit(solution)/shard_map/ppermute | solution.py:749
  229.7 28.0 %collective-permute-start.25 = (bf16[16,32,5248]{2,1,0:T(8,128)(2,1)S(1)}, bf16[16,32,5248]{2,1,0:T(8,128)(2,1)S(1)}, u32[]{:S(2)}, u32[]{:S(2)}) collective-permute-start(bf16[16,32,5248]{2,1,0:T(8,128)(2,1)S(1)} %get-tuple-element.152), channel_id=1, source_target_pairs={{0,1},{1,0},{2,3},{3,2},{4,5},{5,4},{6,7},{7,6},{8,9},{9,8},{10,11... | collective-permute-start | bytes 16121864 | tf_op jit(solution)/shard_map/ppermute | solution.py:749
  230.0 25.3 %collective-permute-start.26 = (bf16[4,2,64,1024]{3,2,1,0:T(8,128)(2,1)S(1)}, bf16[4,2,64,1024]{3,2,1,0:T(8,128)(2,1)S(1)}, u32[]{:S(2)}, u32[]{:S(2)}) collective-permute-start(bf16[4,2,64,1024]{3,2,1,0:T(8,128)(2,1)S(1)} %get-tuple-element.155), channel_id=1, source_target_pairs={{0,2},{1,3},{2,0},{3,1},{4,6},{5,7},{6,4},{7,5},{8,10},{9,11},{10,... | collective-permute-start | bytes 3145736 | tf_op jit(solution)/shard_map/ppermute | solution.py:749
  230.3 25.4 %collective-permute-start.27 = (bf16[4,2,64,1024]{3,2,1,0:T(8,128)(2,1)S(1)}, bf16[4,2,64,1024]{3,2,1,0:T(8,128)(2,1)S(1)}, u32[]{:S(2)}, u32[]{:S(2)}) collective-permute-start(bf16[4,2,64,1024]{3,2,1,0:T(8,128)(2,1)S(1)} %get-tuple-element.156), channel_id=1, source_target_pairs={{0,4},{1,5},{2,6},{3,7},{4,0},{5,1},{6,2},{7,3},{8,12},{9,13},{10,... | collective-permute-start | bytes 3145736 | tf_op jit(solution)/shard_map/ppermute | solution.py:749
  262.5 31.1 %collective-permute-start.28 = (bf16[4,2,16,5248]{3,2,1,0:T(8,128)(2,1)}, bf16[4,2,16,5248]{3,2,1,0:T(8,128)(2,1)}, u32[]{:S(2)}, u32[]{:S(2)}) collective-permute-start(bf16[4,2,16,5248]{3,2,1,0:T(8,128)(2,1)} %get-tuple-element.164), channel_id=1, source_target_pairs={{0,2},{1,3},{2,0},{3,1},{4,6},{5,7},{6,4},{7,5},{8,10},{9,11},{10,... | collective-permute-start | bytes 4030472 | tf_op jit(solution)/shard_map/ppermute | solution.py:749
  263.8 30.5 %collective-permute-start.29 = (bf16[4,2,16,5248]{3,2,1,0:T(8,128)(2,1)}, bf16[4,2,16,5248]{3,2,1,0:T(8,128)(2,1)}, u32[]{:S(2)}, u32[]{:S(2)}) collective-permute-start(bf16[4,2,16,5248]{3,2,1,0:T(8,128)(2,1)} %get-tuple-element.166), channel_id=1, source_target_pairs={{0,4},{1,5},{2,6},{3,7},{4,0},{5,1},{6,2},{7,3},{8,12},{9,13},{10,... | collective-permute-start | bytes 4030472 | tf_op jit(solution)/shard_map/ppermute | solution.py:749
  265.6 92.5 %reduce-scatter.6.cloned.1.call-start = ((), (), s32[]{:S(2)}) async-start(), calls=%async_computation.6 | async-start | bytes 1679360 | tf_op jit(solution)/shard_map/reduce_scatter | solution.py:966
  298.5 14.9 %collective-permute-start.31 = (bf16[4,16,5248]{2,1,0:T(8,128)(2,1)S(1)}, bf16[4,16,5248]{2,1,0:T(8,128)(2,1)S(1)}, u32[]{:S(2)}, u32[]{:S(2)}) collective-permute-start(bf16[4,16,5248]{2,1,0:T(8,128)(2,1)S(1)} %get-tuple-element.173), channel_id=1, source_target_pairs={{0,4},{1,5},{2,6},{3,7},{4,0},{5,1},{6,2},{7,3},{8,12},{9,13},{10,... | collective-permute-start | bytes 2015240 | tf_op jit(solution)/shard_map/ppermute | solution.py:749
  301.3 14.9 %collective-permute-start.30 = (bf16[16,32,3072]{2,1,0:T(8,128)(2,1)S(1)}, bf16[16,32,3072]{2,1,0:T(8,128)(2,1)S(1)}, u32[]{:S(2)}, u32[]{:S(2)}) collective-permute-start(bf16[16,32,3072]{2,1,0:T(8,128)(2,1)S(1)} %get-tuple-element.172), channel_id=1, source_target_pairs={{0,1},{1,0},{2,3},{3,2},{4,5},{5,4},{6,7},{7,6},{8,9},{9,8},{10,11... | collective-permute-start | bytes 9437192 | tf_op jit(solution)/shard_map/ppermute | solution.py:749
  322.3 20.5 %collective-permute-start.33 = (bf16[4,2,16,3072]{3,2,1,0:T(8,128)(2,1)}, bf16[4,2,16,3072]{3,2,1,0:T(8,128)(2,1)S(1)}, u32[]{:S(2)}, u32[]{:S(2)}) collective-permute-start(bf16[4,2,16,3072]{3,2,1,0:T(8,128)(2,1)} %get-tuple-element.181), channel_id=1, source_target_pairs={{0,2},{1,3},{2,0},{3,1},{4,6},{5,7},{6,4},{7,5},{8,10},{9,11},{10,... | collective-permute-start | bytes 2359304 | tf_op jit(solution)/shard_map/ppermute | solution.py:749
  323.6 19.2 %collective-permute-start.34 = (bf16[4,2,16,3072]{3,2,1,0:T(8,128)(2,1)}, bf16[4,2,16,3072]{3,2,1,0:T(8,128)(2,1)S(1)}, u32[]{:S(2)}, u32[]{:S(2)}) collective-permute-start(bf16[4,2,16,3072]{3,2,1,0:T(8,128)(2,1)} %copy-done.19), channel_id=1, source_target_pairs={{0,4},{1,5},{2,6},{3,7},{4,0},{5,1},{6,2},{7,3},{8,12},{9,13},{10,... | collective-permute-start | bytes 2359304 | tf_op jit(solution)/shard_map/ppermute | solution.py:749
  325.2 17.5 %collective-permute-start.35 = (bf16[64,1024]{1,0:T(8,128)(2,1)S(1)}, bf16[64,1024]{1,0:T(8,128)(2,1)S(1)}, u32[]{:S(2)}, u32[]{:S(2)}) collective-permute-start(bf16[64,1024]{1,0:T(8,128)(2,1)S(1)} %dynamic-slice_bitcast_fusion.1), channel_id=1, source_target_pairs={{0,4},{1,5},{2,6},{3,7},{4,0},{5,1},{6,2},{7,3},{8,12},{9,13},{10,... | collective-permute-start | bytes 393224 | tf_op jit(solution)/shard_map/ppermute | solution.py:749
  326.9 15.9 %collective-permute-start.36 = (bf16[64,1024]{1,0:T(8,128)(2,1)S(1)}, bf16[64,1024]{1,0:T(8,128)(2,1)S(1)}, u32[]{:S(2)}, u32[]{:S(2)}) collective-permute-start(bf16[64,1024]{1,0:T(8,128)(2,1)S(1)} %dynamic-slice_bitcast_fusion), channel_id=1, source_target_pairs={{0,2},{1,3},{2,0},{3,1},{4,6},{5,7},{6,4},{7,5},{8,10},{9,11},{10,... | collective-permute-start | bytes 393224 | tf_op jit(solution)/shard_map/ppermute | solution.py:749
  359.8 30.3 %all-to-all-start.1 = ((bf16[4,256,1024]{2,1,0:T(8,128)(2,1)}), bf16[4,256,1024]{2,1,0:T(8,128)(2,1)}, u32[]{:S(2)}, u32[]{:S(2)}) async-start(bf16[4,256,1024]{2,1,0:T(8,128)(2,1)} %get-tuple-element.194), calls=%async_computation.3 | async-start | bytes 4194304 | tf_op jit(solution)/shard_map/all_to_all | solution.py:849
  364.4 29.3 %reduce-scatter.8.cloned.1.call-start = ((), (), s32[]{:S(2)}) async-start(), calls=%async_computation.7 | async-start | bytes 983040 | tf_op jit(solution)/shard_map/reduce_scatter | solution.py:989
  (68 other events, 438.7 us)
Sparse Core Ops, SparseCore 0:
  22.7 39.0 all-gather.5
  73.9 46.1 all-gather.7
  265.7 43.3 reduce-scatter.3
  324.2 32.3 reduce-scatter.5
  367.3 24.9 reduce-scatter.7
